TPU v7x, 32 devices: a whole 2x2x4 slice. The times are simulated.
32 devices in a mesh: cells: 8 (over y, x, core), energy: 4 (over z).
Axes of the slice: x: 2, y: 2, z: 4, core: 2. Of those that a mesh axis runs over, the one named last changes fastest.
Arguments:
- distribution: bfloat16 [2048, 1024], P('cells', 'energy'), may hold values from -6 to 6
- operators: bfloat16 [4, 1024, 1024], P(None, 'energy', 'cells'), may hold values from -0.1875 to 0.1875
- sections: bfloat16 [4096, 1024], P('cells', 'energy'), may hold values from -0.1875 to 0.1875
- populations: float32 [2048, 256], P(('cells', 'energy')), may hold values from 0.1 to 1
- cell_owner: int32 [2048, 1], P(('cells', 'energy')), may hold values from 0 to 7; in each aligned block of 64 rows (0 to 63, 64 to 127, ...) at most 16 rows name the same one
- partner_of: int32 [256, 1], replicated, may hold values from 0 to 3
- source: int32 [4096], replicated, may hold values from 0 to 255
- level_hop: int32 [4096], replicated, may hold values from 1 to 255
- radiative: float32 [4096], replicated, may hold values from 0.05 to 2
Outputs:
- spectrum_out: float32 [2048, 1024], P('cells', 'energy')
- levels_out: float32 [2048, 256], P(('cells', 'energy'))
Inputs may be any that keep to these rules, and one draw needn't show every extreme that they name: `cell_owner`: in each aligned block of 64 rows (the rows of one device) no zone occurs more than 16 times, and some block reaches it; every zone has some cell. `partner_of`: every partner has at least one level.
All inputs are finite; a program needn't handle non-finite values.
Results may differ from a plain program's by a relative error of at most 0.0028.
Values may be sent and summed in bfloat16 or wider, within the bound.
No kernel may reach another device: no remote copies, remote signals or barrier semaphores. Data moves between devices by JAX's collectives and lax.ppermute only.
A program may use at most 64 MiB of HBM per device.

v0:
```python
import jax
import jax.numpy as jnp
from jax import lax
from jax.sharding import PartitionSpec as P

ITERS = 2
SUB = 2


boltz_step = 0.5
level_step = 0.04
depth_scale = 2.0


def exact_product(values, table_half):
    upper = values.astype(jnp.bfloat16)
    remain = values - upper.astype(jnp.float32)
    middle = remain.astype(jnp.bfloat16)
    lowest = (remain - middle.astype(jnp.float32)).astype(jnp.bfloat16)
    total = jnp.dot(upper, table_half, preferred_element_type=jnp.float32)
    total = total + jnp.dot(middle, table_half, preferred_element_type=jnp.float32)
    return total + jnp.dot(lowest, table_half, preferred_element_type=jnp.float32)


def body(
    distribution,
    operators,
    sections,
    populations,
    cell_owner,
    partner_of,
    source,
    level_hop,
    radiative,
):
    highest = lax.Precision.HIGHEST
    cell_groups = lax.axis_size("cells")
    local_cells = populations.shape[0]
    block_cells = distribution.shape[0]
    level_total = populations.shape[1]
    partner_total = operators.shape[0]
    capacity = max(2, 2 * local_cells // cell_groups)
    slot_total = cell_groups * capacity
    target = (source + level_hop) % level_total
    level_ids = jnp.arange(level_total, dtype=jnp.int32)
    transfer = (target[:, None] == level_ids[None, :]).astype(jnp.float32) - (
        source[:, None] == level_ids[None, :]
    ).astype(jnp.float32)
    transfer_half = transfer.astype(jnp.bfloat16)
    partner_map = (
        partner_of[:, 0][:, None] == jnp.arange(partner_total, dtype=jnp.int32)[None, :]
    ).astype(jnp.float32)
    level_counts = jnp.sum(partner_map, axis=0)
    destination = cell_owner[:, 0]
    matches = (destination[:, None] == jnp.arange(cell_groups, dtype=jnp.int32)[None, :]).astype(
        jnp.int32
    )
    arrival = jnp.sum((jnp.cumsum(matches, axis=0) - matches) * matches, axis=1)
    slot_index = destination * capacity + arrival
    placing = (jnp.arange(slot_total, dtype=jnp.int32)[:, None] == slot_index[None, :]).astype(
        jnp.float32
    )

    def pack_floats(values):
        return jnp.dot(placing, values, precision=highest).reshape(
            cell_groups, capacity, values.shape[1]
        )

    def densities_of(level_rows):
        return jnp.dot(level_rows, partner_map, precision=highest) / level_counts

    section_rows = lax.all_gather(sections, "cells", axis=0, tiled=True)
    current = distribution.astype(jnp.float32)
    levels_slab = populations
    dens_local = densities_of(populations)
    for sweep in range(ITERS):
        density = lax.all_gather(dens_local, "energy", axis=0, tiled=True)
        spectra = current.astype(jnp.bfloat16)
        gathered = lax.all_gather(spectra, "energy", axis=1, tiled=True)
        product = jnp.einsum(
            "ce,poe->pco",
            gathered,
            lax.all_gather(operators, "cells", axis=2, tiled=True),
            preferred_element_type=jnp.float32,
        )
        summed = jnp.zeros_like(current)
        for partner in range(partner_total):
            summed = summed + density[:, partner : partner + 1] * product[partner]
        current = current + boltz_step * summed
        raw_sums = lax.psum_scatter(
            lax.dot_general(
                spectra, section_rows, (((1,), (1,)), ((), ())), preferred_element_type=jnp.float32
            ).astype(jnp.bfloat16),
            "energy",
            scatter_dimension=0,
            tiled=True,
        ).astype(jnp.float32)
        slab_rates = jax.nn.softplus(raw_sums)
        zone_rates = (
            lax.all_to_all(
                pack_floats(slab_rates).astype(jnp.bfloat16),
                "cells",
                split_axis=0,
                concat_axis=0,
                tiled=True,
            )
            .astype(jnp.float32)
            .reshape(slot_total, slab_rates.shape[1])
        )
        levels_zone = lax.all_to_all(
            pack_floats(levels_slab), "cells", split_axis=0, concat_axis=0, tiled=True
        ).reshape(slot_total, level_total)
        column = lax.psum(jnp.sum(levels_zone[:, 0]), "energy")
        escape = 1.0 / (1.0 + depth_scale * column / block_cells)
        reaction_rates = zone_rates + radiative[None, :] * escape
        for substep in range(SUB):
            flux = reaction_rates * levels_zone[:, source]
            levels_zone = levels_zone + level_step * exact_product(flux, transfer_half)
        returned = lax.all_to_all(
            levels_zone.reshape(cell_groups, capacity, level_total),
            "cells",
            split_axis=0,
            concat_axis=0,
            tiled=True,
        )
        levels_slab = jnp.dot(
            placing.T, returned.reshape(slot_total, returned.shape[2]), precision=highest
        )
        dens_local = densities_of(levels_slab)
    return (current, levels_slab)


def solution(mesh):
    return jax.shard_map(
        body,
        mesh=mesh,
        in_specs=(
            P("cells", "energy"),
            P(None, "energy", "cells"),
            P("cells", "energy"),
            P(("cells", "energy"), None),
            P(("cells", "energy"), None),
            P(),
            P(),
            P(),
            P(),
        ),
        out_specs=(P("cells", "energy"), P(("cells", "energy"), None)),
        check_vma=False,
    )
```

profile of v0, /device:TPU:0, one launch (start us, length us, event | category | flops | bytes accessed | tf_op | source)
XLA Modules:
  0.0 316.9 jit_solution(737151608856394431)
XLA Ops:
  7.2 0.7 all-gather.7.cloned.1.call-update
  8.0 0.7 all-gather.5.cloned.1.call-update
  8.7 31.8 %all-gather.7.cloned.1.call-done = bf16[4096,256]{1,0:T(8,128)(2,1)} async-done(((bf16[512,256]{1,0:T(8,128)(2,1)}), bf16[4096,256]{1,0:T(8,128)(2,1)}) %all-gather.7.cloned.1.call-update) | async-done | bytes 2097168 | tf_op jit(solution)/shard_map/all_gather | solution.py:72
  40.5 3.8 %convolution_convert_fusion.1 = bf16[256,4096]{1,0:T(8,128)(2,1)} fusion(bf16[256,256]{1,0:T(8,128)(2,1)} %param.9, bf16[4096,256]{1,0:T(8,128)(2,1)} %all-gather.7.cloned.1.call-done), kind=kOutput, calls=%fused_computation.5 | convolution fusion | flops 537919488 | bytes 4325376 | tf_op jit(solution)/shard_map/dot_general | solution.py:91
  44.4 0.8 copy-done.3
  45.4 0.5 copy-done.21
  46.1 11.9 %all-gather = f32[4,64,4]{1,2,0:T(4,128)S(1)} all-gather(f32[1,64,4]{1,2,0:T(4,128)S(1)} %fusion.73), channel_id=1, replica_groups=mesh['cells'=8,'energy'=4] {'energy'}, dimensions={0}, use_global_device_ids=true | all-gather | bytes 5120 | tf_op jit(solution)/shard_map/all_gather | solution.py:77
  58.1 16.0 %all_gather.21 = bf16[256,1024]{1,0:T(8,128)(2,1)S(1)} all-gather(bf16[256,256]{1,0:T(8,128)(2,1)S(1)} %copy-done.3), channel_id=1, replica_groups=mesh['cells'=8,'energy'=4] {'energy'}, dimensions={1}, use_global_device_ids=true | all-gather | bytes 655360 | tf_op jit(solution)/shard_map/all_gather | solution.py:79
  74.1 2.5 convolution_bitcast_fusion.1
  76.6 0.8 fusion.121
  77.4 2.1 convolution_convert_fusion
  79.6 0.6 copy-done.20
  80.6 0.2 fusion.107
  80.8 8.1 %all_to_all.30 = f32[8,16,256]{2,1,0:T(8,128)S(1)} all-to-all(f32[8,16,256]{2,1,0:T(8,128)S(1)} %bitcast.144), channel_id=1, replica_groups=mesh['cells'=8,'energy'=4] {'cells'}, dimensions={0} | all-to-all | bytes 262144 | tf_op jit(solution)/shard_map/all_to_all | solution.py:110
  88.8 0.6 slice_reduce_fusion.1
  89.5 11.4 %psum.14 = f32[]{:T(128)} all-reduce(f32[]{:T(128)} %slice_reduce_fusion.1), channel_id=1, replica_groups=mesh['cells'=8,'energy'=4] {'energy'}, use_global_device_ids=true, to_apply=%region_5.6 | all-reduce | flops 1 | bytes 8 | tf_op jit(solution)/shard_map/psum | solution.py:113
  101.7 14.2 %gather_fusion = f32[4096,128]{1,0:T(8,128)} fusion(f32[128,256]{0,1:T(8,128)S(1)} %copy.48, s32[4096]{0:T(1024)S(1)} %get-tuple-element.12), kind=kCustom, calls=%fused_computation | custom fusion | bytes 4210688 | tf_op jit(solution)/shard_map/gather | solution.py:117
  115.9 1.2 reduce-scatter.3.cloned.1.call-done
  117.1 3.7 %convolution_convert_fusion.3 = bf16[128,4096]{1,0:T(8,128)(2,1)} fusion(bf16[64,4096]{1,0:T(8,128)(2,1)} %reduce-scatter.3.cloned.1.call-done, s32[64]{0:T(128)S(1)} %multiply_add_fusion), kind=kOutput, calls=%fused_computation.7 | convolution fusion | flops 405020672 | bytes 1573120 | tf_op jit(solution)/shard_map/dot_general | solution.py:65
  120.8 4.2 %all-to-all-start.1 = ((bf16[8,16,4096]{2,1,0:T(8,128)(2,1)}), bf16[8,16,4096]{2,1,0:T(8,128)(2,1)}, u32[]{:S(2)}, u32[]{:S(2)}) async-start(bf16[8,16,4096]{2,1,0:T(8,128)(2,1)} %bitcast.16), calls=%async_computation.2 | async-start | bytes 2097152 | tf_op jit(solution)/shard_map/all_to_all | solution.py:100
  125.0 22.1 %all_gather.24 = bf16[256,1024]{0,1:T(8,128)(2,1)S(1)} all-gather(bf16[256,256]{0,1:T(8,128)(2,1)S(1)} %get-tuple-element.10), channel_id=1, replica_groups=mesh['cells'=8,'energy'=4] {'energy'}, dimensions={1}, use_global_device_ids=true | all-gather | bytes 655360 | tf_op jit(solution)/shard_map/all_gather | solution.py:79
  147.1 0.7 convolution_bitcast_fusion
  147.9 23.1 %reduce-scatter.5.cloned.1.call-done = bf16[64,4096]{1,0:T(8,128)(2,1)} async-done(((bf16[256,4096]{1,0:T(8,128)(2,1)}), bf16[64,4096]{1,0:T(8,128)(2,1)}) %reduce-scatter.5.cloned.1.call-update) | async-done | bytes 524304 | tf_op jit(solution)/shard_map/reduce_scatter | solution.py:90
  170.9 3.6 %convolution_convert_fusion.2 = bf16[128,4096]{1,0:T(8,128)(2,1)} fusion(bf16[64,4096]{1,0:T(8,128)(2,1)} %reduce-scatter.5.cloned.1.call-done, s32[64]{0:T(128)S(1)} %copy-done.11), kind=kOutput, calls=%fused_computation.6 | convolution fusion | flops 405020672 | bytes 1573120 | tf_op jit(solution)/shard_map/dot_general | solution.py:65
  174.6 4.4 %all-to-all-start.4 = ((bf16[8,16,4096]{2,1,0:T(8,128)(2,1)}), bf16[8,16,4096]{2,1,0:T(8,128)(2,1)}, u32[]{:S(2)}, u32[]{:S(2)}) async-start(bf16[8,16,4096]{2,1,0:T(8,128)(2,1)} %bitcast.35), calls=%async_computation.6 | async-start | bytes 2097152 | tf_op jit(solution)/shard_map/all_to_all | solution.py:100
  179.0 2.7 bitcast_convert_fusion.1
  181.8 1.9 copy.47
  183.7 1.9 bitcast_multiply_fusion.3
  185.6 1.6 fusion.10
  187.2 1.6 fusion.60
  188.9 2.3 fusion.59
  191.1 1.0 copy.49
  192.1 14.2 %gather_fusion.1 = f32[4096,128]{1,0:T(8,128)} fusion(f32[128,256]{0,1:T(8,128)S(1)} %copy.49, s32[4096]{0:T(1024)S(1)} %get-tuple-element.12), kind=kCustom, calls=%fused_computation.1 | custom fusion | bytes 4210688 | tf_op jit(solution)/shard_map/gather | solution.py:117
  206.3 1.9 bitcast_multiply_fusion.2
  208.2 1.6 fusion.7
  209.9 1.6 fusion.63
  211.5 2.3 fusion.57
  213.8 3.9 %all-to-all-start.2 = ((f32[8,16,256]{2,1,0:T(8,128)}), f32[8,16,256]{2,1,0:T(8,128)S(1)}, u32[]{:S(2)}, u32[]{:S(2)}) async-start(f32[8,16,256]{2,1,0:T(8,128)} %bitcast.20), calls=%async_computation.3 | async-start | bytes 262144 | tf_op jit(solution)/shard_map/all_to_all | solution.py:119
  217.7 2.8 bitcast_convert_fusion
  220.5 1.9 copy.53
  222.4 0.8 all-to-all-done.2
  223.3 0.2 fusion.106
  223.7 0.9 fusion.105
  224.5 11.9 %all-gather.1 = f32[4,64,4]{1,2,0:T(4,128)S(1)} all-gather(f32[1,64,4]{1,2,0:T(4,128)S(1)} %fusion.72), channel_id=1, replica_groups=mesh['cells'=8,'energy'=4] {'energy'}, dimensions={0}, use_global_device_ids=true | all-gather | bytes 5120 | tf_op jit(solution)/shard_map/all_gather | solution.py:77
  236.5 3.4 %all-to-all-start.3 = ((f32[8,16,256]{2,1,0:T(8,128)}), f32[8,16,256]{2,1,0:T(8,128)S(1)}, u32[]{:S(2)}, u32[]{:S(2)}) async-start(f32[8,16,256]{2,1,0:T(8,128)} %bitcast.142), calls=%async_computation.4 | async-start | bytes 262144 | tf_op jit(solution)/shard_map/all_to_all | solution.py:110
  239.9 0.6 fusion.123
  240.5 4.9 %all-to-all-done.3 = f32[8,16,256]{2,1,0:T(8,128)S(1)} async-done(((f32[8,16,256]{2,1,0:T(8,128)}), f32[8,16,256]{2,1,0:T(8,128)S(1)}, u32[]{:S(2)}, u32[]{:S(2)}) %all-to-all-start.3) | async-done | bytes 131104 | tf_op jit(solution)/shard_map/all_to_all | solution.py:110
  245.4 0.6 slice_reduce_fusion
  246.2 9.3 %psum.15 = f32[]{:T(128)} all-reduce(f32[]{:T(128)} %slice_reduce_fusion), channel_id=1, replica_groups=mesh['cells'=8,'energy'=4] {'energy'}, use_global_device_ids=true, to_apply=%region_8.9 | all-reduce | flops 1 | bytes 8 | tf_op jit(solution)/shard_map/psum | solution.py:113
  256.1 14.2 %gather_fusion.2 = f32[4096,128]{1,0:T(8,128)} fusion(f32[128,256]{0,1:T(8,128)S(1)} %copy.54, s32[4096]{0:T(1024)S(1)} %get-tuple-element.12), kind=kCustom, calls=%fused_computation.2 | custom fusion | bytes 4210688 | tf_op jit(solution)/shard_map/gather | solution.py:117
  270.3 1.9 bitcast_multiply_fusion.1
  272.2 1.6 fusion.4
  273.9 1.6 fusion.66
  275.5 2.3 fusion.55
  277.8 1.0 copy.55
  278.8 14.2 %gather_fusion.3 = f32[4096,128]{1,0:T(8,128)} fusion(f32[128,256]{0,1:T(8,128)S(1)} %copy.55, s32[4096]{0:T(1024)S(1)} %get-tuple-element.12), kind=kCustom, calls=%fused_computation.3 | custom fusion | bytes 4210688 | tf_op jit(solution)/shard_map/gather | solution.py:117
  292.9 1.9 bitcast_multiply_fusion
  294.9 1.6 fusion.1
  296.5 1.6 fusion.69
  298.2 2.3 fusion.53
  300.5 3.5 %all-to-all-start.5 = ((f32[8,16,256]{2,1,0:T(8,128)}), f32[8,16,256]{2,1,0:T(8,128)S(1)}, u32[]{:S(2)}, u32[]{:S(2)}) async-start(f32[8,16,256]{2,1,0:T(8,128)} %bitcast.39), calls=%async_computation.7 | async-start | bytes 262144 | tf_op jit(solution)/shard_map/all_to_all | solution.py:119
  304.1 0.8 copy.56
  305.0 4.5 %all-to-all-done.5 = f32[8,16,256]{2,1,0:T(8,128)S(1)} async-done(((f32[8,16,256]{2,1,0:T(8,128)}), f32[8,16,256]{2,1,0:T(8,128)S(1)}, u32[]{:S(2)}, u32[]{:S(2)}) %all-to-all-start.5) | async-done | bytes 131104 | tf_op jit(solution)/shard_map/all_to_all | solution.py:119
  309.5 0.9 fusion.104
  (71 shorter events, 1.6 us)
Async XLA Ops:
  7.2 38.8 %copy-start = (f32[64,256]{1,0:T(8,128)S(1)}, f32[64,256]{1,0:T(8,128)}, u32[]{:S(2)}) copy-start(f32[64,256]{1,0:T(8,128)} %param.12) | copy-start | bytes 196612
  7.2 33.4 %all-gather.7.cloned.1.call-start = ((), (), s32[]{:S(2)}) async-start(), calls=%async_computation.9 | async-start | bytes 2359296 | tf_op jit(solution)/shard_map/all_gather | solution.py:72
  7.9 66.2 %all-gather.5.cloned.1.call-start = ((), (), s32[]{:S(2)}) async-start(), calls=%async_computation.8 | async-start | bytes 2359296 | tf_op jit(solution)/shard_map/all_gather | solution.py:83
  8.7 108.4 %reduce-scatter.3.cloned.1.call-start = ((), (), s32[]{:S(2)}) async-start(), calls=%async_computation.10 | async-start | bytes 2621440 | tf_op jit(solution)/shard_map/reduce_scatter | solution.py:90
  44.3 0.9 copy-start.3
  44.3 1.0 copy-start.14
  44.3 126.6 %reduce-scatter.5.cloned.1.call-start = ((), (), s32[]{:S(2)}) async-start(), calls=%async_computation.11 | async-start | bytes 2621440 | tf_op jit(solution)/shard_map/reduce_scatter | solution.py:90
  45.4 0.5 copy-start.21
  74.1 3.3 %copy-start.2 = (bf16[4096,256]{1,0:T(8,128)(2,1)S(1)}, bf16[4096,256]{1,0:T(8,128)(2,1)}, u32[]{:S(2)}) copy-start(bf16[4096,256]{1,0:T(8,128)(2,1)} %all-gather.7.cloned.1.call-done) | copy-start | bytes 6291460
  79.5 0.7 copy-start.20
  79.5 9.9 %copy-start.8 = (s32[4096]{0:T(1024)S(1)}, s32[4096]{0:T(1024)}, u32[]{:S(2)}) copy-start(s32[4096]{0:T(1024)} %param.16) | copy-start | bytes 49156
  79.5 9.9 %copy-start.9 = (s32[4096]{0:T(1024)S(1)}, s32[4096]{0:T(1024)}, u32[]{:S(2)}) copy-start(s32[4096]{0:T(1024)} %param.15) | copy-start | bytes 49156
  80.6 36.5 %copy-start.10 = (s32[64]{0:T(128)}, s32[64]{0:T(128)S(1)}, u32[]{:S(2)}) copy-start(s32[64]{0:T(128)S(1)} %multiply_add_fusion) | copy-start | bytes 772
  115.9 9.1 %copy-start.7 = (f32[4096]{0:T(1024)S(1)}, f32[4096]{0:T(1024)}, u32[]{:S(2)}) copy-start(f32[4096]{0:T(1024)} %param.17) | copy-start | bytes 49156
  115.9 31.3 %copy-start.1 = (bf16[4,256,1024]{2,1,0:T(8,128)(2,1)S(1)}, bf16[4,256,1024]{2,1,0:T(8,128)(2,1)}, u32[]{:S(2)}) copy-start(bf16[4,256,1024]{2,1,0:T(8,128)(2,1)} %all-gather.5.cloned.1.call-done) | copy-start | bytes 6291460
  120.8 53.8 %all-to-all-start.1 = ((bf16[8,16,4096]{2,1,0:T(8,128)(2,1)}), bf16[8,16,4096]{2,1,0:T(8,128)(2,1)}, u32[]{:S(2)}, u32[]{:S(2)}) async-start(bf16[8,16,4096]{2,1,0:T(8,128)(2,1)} %bitcast.16), calls=%async_computation.2 | async-start | bytes 2097152 | tf_op jit(solution)/shard_map/all_to_all | solution.py:100
  147.1 23.8 %copy-start.11 = (s32[64]{0:T(128)S(1)}, s32[64]{0:T(128)}, u32[]{:S(2)}) copy-start(s32[64]{0:T(128)} %copy-done.10) | copy-start | bytes 772
  174.6 39.2 %all-to-all-start.4 = ((bf16[8,16,4096]{2,1,0:T(8,128)(2,1)}), bf16[8,16,4096]{2,1,0:T(8,128)(2,1)}, u32[]{:S(2)}, u32[]{:S(2)}) async-start(bf16[8,16,4096]{2,1,0:T(8,128)(2,1)} %bitcast.35), calls=%async_computation.6 | async-start | bytes 2097152 | tf_op jit(solution)/shard_map/all_to_all | solution.py:100
  209.9 1.6 copy-start.6
  213.8 9.5 %all-to-all-start.2 = ((f32[8,16,256]{2,1,0:T(8,128)}), f32[8,16,256]{2,1,0:T(8,128)S(1)}, u32[]{:S(2)}, u32[]{:S(2)}) async-start(f32[8,16,256]{2,1,0:T(8,128)} %bitcast.20), calls=%async_computation.3 | async-start | bytes 262144 | tf_op jit(solution)/shard_map/all_to_all | solution.py:119
  220.5 2.8 copy-start.12
  220.5 3.0 copy-start.15
  220.5 3.0 copy-start.22
  236.5 8.9 %all-to-all-start.3 = ((f32[8,16,256]{2,1,0:T(8,128)}), f32[8,16,256]{2,1,0:T(8,128)S(1)}, u32[]{:S(2)}, u32[]{:S(2)}) async-start(f32[8,16,256]{2,1,0:T(8,128)} %bitcast.142), calls=%async_computation.4 | async-start | bytes 262144 | tf_op jit(solution)/shard_map/all_to_all | solution.py:110
  296.5 1.6 copy-start.5
  298.2 5.8 %copy-start.4 = (f32[256,256]{0,1:T(8,128)S(1)}, f32[256,256]{0,1:T(8,128)}, u32[]{:S(2)}) copy-start(f32[256,256]{0,1:T(8,128)} %get-tuple-element.11) | copy-start | bytes 786436
  298.2 5.8 %copy-start.16 = (f32[256,1]{0,1:T(1,128)S(1)}, f32[256,1]{0,1:T(1,128)}, u32[]{:S(2)}) copy-start(f32[256,1]{0,1:T(1,128)} %get-tuple-element.14) | copy-start | bytes 3076
  298.2 5.8 %copy-start.17 = (f32[256,1]{0,1:T(1,128)S(1)}, f32[256,1]{0,1:T(1,128)}, u32[]{:S(2)}) copy-start(f32[256,1]{0,1:T(1,128)} %get-tuple-element.15) | copy-start | bytes 3076
  298.2 5.8 %copy-start.18 = (f32[256,1]{0,1:T(1,128)S(1)}, f32[256,1]{0,1:T(1,128)}, u32[]{:S(2)}) copy-start(f32[256,1]{0,1:T(1,128)} %get-tuple-element.16) | copy-start | bytes 3076
  298.2 5.8 %copy-start.19 = (f32[256,1]{0,1:T(1,128)S(1)}, f32[256,1]{0,1:T(1,128)}, u32[]{:S(2)}) copy-start(f32[256,1]{0,1:T(1,128)} %get-tuple-element.17) | copy-start | bytes 3076
  300.5 9.0 %copy-start.13 = (s32[64]{0:T(128)S(1)}, s32[64]{0:T(128)}, u32[]{:S(2)}) copy-start(s32[64]{0:T(128)} %copy-done.10) | copy-start | bytes 772
  300.5 9.0 %all-to-all-start.5 = ((f32[8,16,256]{2,1,0:T(8,128)}), f32[8,16,256]{2,1,0:T(8,128)S(1)}, u32[]{:S(2)}, u32[]{:S(2)}) async-start(f32[8,16,256]{2,1,0:T(8,128)} %bitcast.39), calls=%async_computation.7 | async-start | bytes 262144 | tf_op jit(solution)/shard_map/all_to_all | solution.py:119
Sparse Core Ops, SparseCore 0:
  9.9 30.5 all-gather.6
  42.4 28.1 all-gather.4
  72.9 44.0 reduce-scatter.2
  119.3 51.5 reduce-scatter.4
where the time goes:
time: 318 us; the launch traced here: 317 us
  blocking collectives  90.7 us (29%)
  waiting for transfers between devices  67.7 us (21%)
  local copies, waits for them, and re-layouts  66.5 us (21%)
  matrix products  40.9 us (13%)
  starting transfers between devices  19.7 us (6%)
  other arithmetic  15.9 us (5%)
  between operations  15.6 us (5%)
    gather x4, local copies, waits for them, and re-layouts, body(): flux = reaction_rates * levels_zone[:, source]  56.7 us
    all_gather x2, blocking collectives, body(): gathered = lax.all_gather(spectra, 'energy', axis=1, tiled=True)  38.1 us
    all_gather x1, waiting for transfers between devices, body(): section_rows = lax.all_gather(sections, 'cells', axis=0, tiled=True)  31.8 us
    reduce_scatter x2, waiting for transfers between devices, body(): lax.psum_scatter(lax.dot_general(spectra, section_rows, (((1,), (1,)), ((...  24.2 us
    all_gather x2, blocking collectives, body(): density = lax.all_gather(dens_local, 'energy', axis=0, tiled=True)  23.8 us
    psum x2, blocking collectives, body(): column = lax.psum(jnp.sum(levels_zone[:, 0]), 'energy')  20.7 us
    dot_general x4, matrix products, exact_product(): jnp.dot(lowest, table_half, preferred_element_type=jnp.float32)  9.12 us
    all_to_all x2, starting transfers between devices, body(): lax.all_to_all(pack_floats(slab_rates).astype(jnp.bfloat16), 'cells', spl...  8.7 us
  transfers between devices with their start and end apart: 9, of which 6 were waited for; matrix products, arithmetic and copies ran while one was open for 23% of the time, Pallas kernels for 0%

commit v1 on v0

v1 whole, which is shorter than its diff:
```python
import jax
import jax.numpy as jnp
from jax import lax
from jax.experimental import pallas as pl
from jax.experimental.pallas import tpu as pltpu
from jax.sharding import PartitionSpec as P

boltz_step = 0.5
level_step = 0.04
depth_scale = 2.0

BF = jnp.bfloat16
F32 = jnp.float32
NT = (((1,), (1,)), ((), ()))
TILE = 8
LANES = 128
COLUMN_ROW = 4
PARAMS = pltpu.CompilerParams(vmem_limit_bytes=40 << 20)


def swap(x, axis, mask, count):
    return lax.ppermute(x, axis, [(i, i ^ mask) for i in range(count)])


def others(x, ne):
    got = {mask: swap(x, "energy", mask, ne) for mask in range(ne - 1, 0, -1)}
    return [x] + [got[mask] for mask in range(1, ne)]


def cross(x, first):
    masks = (2, 4) if first else (4, 2)
    return lax.ppermute(x, "cells", [(i, i ^ masks[i & 1]) for i in range(8)])


def gather_cells(x):
    a = cross(x, True)
    b = cross(x, False)
    c = cross(b, True)
    own = [x, a, b, c]
    return own + [swap(v, "cells", 1, 8) for v in own]


def gathered_places(i):
    first = jnp.where((i & 1) == 0, 2, 4)
    own = [i, i ^ first, i ^ (6 - first), i ^ 6]
    sibling = [i ^ 1, i ^ 1 ^ (6 - first), i ^ 1 ^ first, i ^ 7]
    return own + sibling


def aligned(index, size):
    return pl.ds(pl.multiple_of(index * size, size), size)


def split(x):
    high = x.astype(BF)
    return high, (x - high.astype(F32)).astype(BF)


def halves(x):
    return jnp.concatenate(split(x), 0)


def dot(a, b):
    return jnp.dot(a, b, preferred_element_type=F32)


def dot_nt(a, b):
    return lax.dot_general(a, b, NT, preferred_element_type=F32)


def fold(x):
    n = x.shape[0] // 2
    return x[:n] + x[n:]


def call(kernel, shapes, ints, *args, scratch=()):
    return pl.pallas_call(
        kernel,
        out_shape=tuple(jax.ShapeDtypeStruct(s, t) for s, t in shapes),
        in_specs=[pl.BlockSpec(memory_space=pltpu.SMEM)]
        + [pl.BlockSpec(memory_space=pltpu.VMEM)] * len(args),
        out_specs=tuple(pl.BlockSpec(memory_space=pltpu.VMEM) for _ in shapes),
        scratch_shapes=list(scratch),
        compiler_params=PARAMS,
    )(ints, *args)


def zones_of(owner_ref):
    owner = owner_ref[...]
    lanes = lax.broadcasted_iota(jnp.int32, (owner.shape[0], LANES), 1)
    return jnp.where(owner == lanes, 1.0, 0.0)


def put_news(levels, partner_ref, owner_ref, out_ref):
    rows, total = levels.shape
    ids = lax.broadcasted_iota(jnp.int32, (TILE, total), 0)
    chosen = jnp.where(ids == partner_ref[...], 1.0, 0.0)
    number = jnp.maximum(jnp.sum(chosen, axis=1, keepdims=True), 1.0)
    chosen = chosen.astype(BF)
    high, low = split(levels)
    density = (dot_nt(chosen, high) + dot_nt(chosen, low)) / number
    tile = jnp.concatenate([density, jnp.zeros((TILE, LANES - rows), F32)], 1)
    column = jnp.sum(zones_of(owner_ref) * levels[:, 0:1], axis=0, keepdims=True)
    at = lax.broadcasted_iota(jnp.int32, (TILE, LANES), 0)
    tile = jnp.where(at == COLUMN_ROW, column, tile)
    for n in range(out_ref.shape[0] // TILE):
        out_ref[n * TILE : (n + 1) * TILE, :] = tile


def news_kernel(ints_ref, level_ref, partner_ref, owner_ref, out_ref):
    put_news(level_ref[...], partner_ref, owner_ref, out_ref)


def escape_of(news_ref, owner_ref, block):
    news = news_ref[...].reshape(news_ref.shape[0] // TILE, TILE, LANES)
    column = jnp.sum(news, axis=0)[COLUMN_ROW : COLUMN_ROW + 1]
    escape = 1.0 / (1.0 + depth_scale * column / block)
    return jnp.sum(zones_of(owner_ref) * escape, axis=1, keepdims=True)


def density_of(news_ref, i, ne, slab):
    parts = []
    for z in range(ne):
        parts.append(jnp.transpose(news_ref[aligned(i * ne + z, TILE), :])[:slab])
    return jnp.concatenate(parts, 0)


def tables_kernel(ints_ref, source_ref, target_ref, rad_ref, pick_ref, move_ref, drain_ref):
    levels, total = pick_ref.shape
    step = min(512, total)
    acc = jnp.zeros((levels, levels), F32)
    ids = lax.broadcasted_iota(jnp.int32, (levels, step), 0)
    for at in range(0, total, step):
        src = ids == source_ref[0:1, at : at + step]
        tgt = ids == target_ref[0:1, at : at + step]
        pick = jnp.where(src, 1.0, 0.0)
        move = (jnp.where(tgt, 1.0, 0.0) - pick).astype(BF)
        pick_ref[:, at : at + step] = pick.astype(BF)
        move_ref[:, at : at + step] = move
        rad = rad_ref[0:1, at : at + step]
        high = rad.astype(BF).astype(F32)
        low = rad - high
        acc += dot_nt((pick * high).astype(BF), move)
        acc += dot_nt((pick * low).astype(BF), move)
    drain_ref[...] = acc


def scatter(pairs, k, rate_refs, pick_ref, move_ref, groups):
    rows = pairs.shape[0] // (2 * groups)
    part = rate_refs[0].shape[1]
    step = min(512, part)
    acc = jnp.zeros((pairs.shape[0], pick_ref.shape[0]), F32)
    for mask, ref in enumerate(rate_refs):
        for inner in range(0, part, step):
            at = pl.ds(pl.multiple_of((k ^ mask) * part + inner, step), step)
            rate = ref[:, inner : inner + step].astype(F32)
            picked = dot(pairs, pick_ref[:, at])
            parts = []
            for g in range(groups):
                own = picked[2 * g * rows : 2 * (g + 1) * rows]
                parts.append(halves(rate * fold(own)))
            flux = parts[0] if groups == 1 else jnp.concatenate(parts, 0)
            acc += dot_nt(flux, move_ref[:, at])
    return [fold(acc[2 * g * rows : 2 * (g + 1) * rows]) for g in range(groups)]


def drained(pairs, drain_ref):
    high, low = split(drain_ref[...])
    return fold(dot(pairs, high) + dot(pairs, low))


def first_kernel(block, ne):
    def kernel(ints_ref, level_ref, news_ref, owner_ref, partner_ref, pick_ref, move_ref, drain_ref, *refs):
        rates, (out_ref, told_ref) = refs[:ne], refs[ne:]
        k = ints_ref[0]
        levels = level_ref[...]
        escape = escape_of(news_ref, owner_ref, block)
        for _ in range(2):
            pairs = halves(levels)
            (moved,) = scatter(pairs, k, rates, pick_ref, move_ref, 1)
            levels = levels + level_step * (moved + escape * drained(pairs, drain_ref))
        out_ref[...] = levels
        put_news(levels, partner_ref, owner_ref, told_ref)

    return kernel


def second_kernel(ne):
    def kernel(ints_ref, level_ref, pick_ref, move_ref, drain_ref, *refs):
        rates, (c0_ref, c1_ref, c2_ref) = refs[:ne], refs[ne:]
        k = ints_ref[0]
        levels = level_ref[...]
        pairs = halves(levels)
        (moved,) = scatter(pairs, k, rates, pick_ref, move_ref, 1)
        u = levels + level_step * moved
        v = level_step * drained(pairs, drain_ref)
        pu, pv = halves(u), halves(v)
        mu, mv = scatter(jnp.concatenate([pu, pv], 0), k, rates, pick_ref, move_ref, 2)
        c0_ref[...] = u + level_step * mu
        c1_ref[...] = v + level_step * (mv + drained(pu, drain_ref))
        c2_ref[...] = level_step * drained(pv, drain_ref)

    return kernel


def final_kernel(block, ne, slab):
    def kernel(ints_ref, news_ref, owner_ref, c0_ref, c1_ref, c2_ref, current_ref, product_ref, out_ref, level_ref):
        escape = escape_of(news_ref, owner_ref, block)
        level_ref[...] = c0_ref[...] + escape * (c1_ref[...] + escape * c2_ref[...])
        density = density_of(news_ref, ints_ref[1], ne, slab)
        summed = density[:, 0:1] * product_ref[0]
        for p in range(1, product_ref.shape[0]):
            summed = summed + density[:, p : p + 1] * product_ref[p]
        out_ref[...] = current_ref[...] + boltz_step * summed

    return kernel


def place_spectra(ints_ref, spectra, row_ref):
    k = ints_ref[0]
    for mask, ref in enumerate(spectra):
        row_ref[:, aligned(k ^ mask, ref.shape[1])] = ref[...]


def product_of(ints_ref, row_ref, parts, p):
    total = None
    for n, ref in enumerate(parts):
        width = ref.shape[2]
        lhs = row_ref[...] if len(parts) == 1 else row_ref[:, aligned(ints_ref[2 + n], width)]
        term = dot_nt(lhs, ref[p])
        total = term if total is None else total + term
    return total


def first_product_kernel(ne, slab, count):
    def kernel(ints_ref, news_ref, *refs):
        spectra, parts, (current_ref, next_ref, row_ref) = refs[:ne], refs[ne : ne + count], refs[ne + count :]
        place_spectra(ints_ref, spectra, row_ref)
        density = density_of(news_ref, ints_ref[1], ne, slab)
        summed = None
        for p in range(parts[0].shape[0]):
            term = density[:, p : p + 1] * product_of(ints_ref, row_ref, parts, p)
            summed = term if summed is None else summed + term
        current = spectra[0][...].astype(F32) + boltz_step * summed
        current_ref[...] = current
        next_ref[...] = current.astype(BF)

    return kernel


def second_product_kernel(ne, count):
    def kernel(ints_ref, *refs):
        spectra, parts, (product_ref, row_ref) = refs[:ne], refs[ne : ne + count], refs[ne + count :]
        place_spectra(ints_ref, spectra, row_ref)
        for p in range(parts[0].shape[0]):
            product_ref[p] = product_of(ints_ref, row_ref, parts, p)

    return kernel


def rates_kernel(ne, count):
    def kernel(ints_ref, *refs):
        spectra, parts = refs[:ne], refs[ne : ne + count]
        outs, (row_ref, rate_ref) = refs[ne + count : 2 * ne + count], refs[2 * ne + count :]
        place_spectra(ints_ref, spectra, row_ref)
        row = row_ref[...]
        for n, ref in enumerate(parts):
            rates = jax.nn.softplus(dot_nt(row, ref[...])).astype(BF)
            if count == 1:
                rate_ref[...] = rates
            else:
                rate_ref[:, aligned(ints_ref[2 + n], ref.shape[0])] = rates
        for mask, out in enumerate(outs):
            out[...] = rate_ref[aligned(ints_ref[0] ^ mask, out.shape[0]), :]

    return kernel


def pack_kernel(ints_ref, *refs):
    place_spectra(ints_ref, refs[:-1], refs[-1])


def body(
    distribution,
    operators,
    sections,
    populations,
    cell_owner,
    partner_of,
    source,
    level_hop,
    radiative,
):
    nc = lax.axis_size("cells")
    ne = lax.axis_size("energy")
    i = lax.axis_index("cells")
    k = lax.axis_index("energy")
    slab, level_total = populations.shape
    block, width = distribution.shape
    partner_total, outs, _ = operators.shape
    reactions = source.shape[0]
    part = sections.shape[0] // ne
    small = nc == 8
    places = gathered_places(i) if small else [i]
    ints = jnp.stack([v.astype(jnp.int32) for v in [k, i] + places])

    def collect(x, axis):
        if small:
            return gather_cells(x)
        return [lax.all_gather(x, "cells", axis=axis, tiled=True)]

    def shared(news):
        return lax.all_to_all(news, ("cells", "energy"), 0, 0, tiled=True)

    news_shape = ((nc * ne * TILE, LANES), F32)
    partner_row = partner_of.reshape(1, level_total)

    operator_parts = collect(operators, 2)
    spectra = others(distribution, ne)
    shares = [lax.dynamic_slice_in_dim(sections, (k ^ m) * part, part, 0) for m in range(ne)]
    shares = [v if m == 0 else swap(v, "energy", m, ne) for m, v in enumerate(shares)]
    (news,) = call(news_kernel, [news_shape], ints, populations, partner_row, cell_owner)
    news = shared(news)
    (packed,) = call(pack_kernel, [((part, ne * width), BF)], ints, *shares)
    section_parts = collect(packed, 0)

    target = (source + level_hop) % level_total
    pick, move, drain = call(
        tables_kernel,
        [((level_total, reactions), BF)] * 2 + [((level_total, level_total), F32)],
        ints,
        *(
            jnp.swapaxes(v.reshape(nc, ne, part), 0, 1).reshape(1, reactions)
            for v in (source, target, radiative)
        ),
    )

    row = pltpu.VMEM((block, ne * width), BF)
    count = len(places)
    current, later = call(
        first_product_kernel(ne, slab, count),
        [((block, outs), F32), ((block, outs), BF)],
        ints,
        news,
        *spectra,
        *operator_parts,
        scratch=[row],
    )
    later = others(later, ne)

    def rates_of(chunks):
        rates = call(
            rates_kernel(ne, count),
            [((slab, nc * part), BF)] * ne,
            ints,
            *chunks,
            *section_parts,
            scratch=[row, pltpu.VMEM((block, nc * part), BF)],
        )
        got = {m: swap(rates[m], "energy", m, ne) for m in range(ne - 1, 0, -1)}
        return [rates[0]] + [got[m] for m in range(1, ne)]

    rates = rates_of(spectra)
    levels, news = call(
        first_kernel(block, ne),
        [(populations.shape, F32), news_shape],
        ints,
        populations,
        news,
        cell_owner,
        partner_row,
        pick,
        move,
        drain,
        *rates,
    )
    news = shared(news)
    rates = rates_of(later)
    (products,) = call(
        second_product_kernel(ne, count),
        [((partner_total, block, outs), F32)],
        ints,
        *later,
        *operator_parts,
        scratch=[row],
    )
    terms = call(
        second_kernel(ne), [(populations.shape, F32)] * 3, ints, levels, pick, move, drain, *rates
    )
    return call(
        final_kernel(block, ne, slab),
        [((block, outs), F32), (populations.shape, F32)],
        ints,
        news,
        cell_owner,
        *terms,
        current,
        products,
    )


def solution(mesh):
    return jax.shard_map(
        body,
        mesh=mesh,
        in_specs=(
            P("cells", "energy"),
            P(None, "energy", "cells"),
            P("cells", "energy"),
            P(("cells", "energy"), None),
            P(("cells", "energy"), None),
            P(),
            P(),
            P(),
            P(),
        ),
        out_specs=(P("cells", "energy"), P(("cells", "energy"), None)),
        check_vma=False,
    )
```

time: 318 us -> 135 us (0.42)
  blocking collectives: 90.7 us -> 0 us
  matrix products: 40.9 us -> 0 us
  waiting for transfers between devices: 67.7 us -> 27.6 us
  local copies, waits for them, and re-layouts: 66.5 us -> 35.8 us
  starting transfers between devices: 19.7 us -> 45 us
  Pallas kernels: 0 us -> 24.8 us
  other arithmetic: 15.9 us -> 0.01 us
  between operations: 15.6 us -> 1.22 us
    all_gather x4 -> x0, blocking collectives: 61.9 us -> none  [the longest x2 38.1 us: body(): gathered = lax.all_gather(spectra, 'energy', axis=1, tiled=True)]
    gather x4 -> x0, local copies, waits for them, and re-layouts: 56.7 us -> none  [body(): flux = reaction_rates * levels_zone[:, source]]
    dot_general x24 -> x0, matrix products: 40.9 us -> none  [the longest x4 9.12 us: exact_product(): jnp.dot(lowest, table_half, preferred_element_type=jnp.float32)]
    ppermute x0 -> x29, starting transfers between devices: none -> 34.7 us  [the longest x23 24.1 us: swap(): return lax.ppermute(x, axis, [(i, i ^ mask) for i in range(count)])]
    all_gather x2 -> x0, waiting for transfers between devices: 31.8 us -> none  [the longest x1 31.8 us: body(): section_rows = lax.all_gather(sections, 'cells', axis=0, tiled=True)]
    unnamed x50 -> x141, local copies, waits for them, and re-layouts: 3.17 us -> 34.7 us
    ppermute x0 -> x29, waiting for transfers between devices: none -> 27.6 us  [the longest x23 24.6 us: swap(): return lax.ppermute(x, axis, [(i, i ^ mask) for i in range(count)])]
    pallas_call x0 -> x10, Pallas kernels: none -> 24.8 us  [call(): pl.pallas_call(kernel, out_shape=tuple((jax.ShapeDtypeStruct(s, t) for s,...]
  transfers between devices with their start and end apart: 9 -> 31, of which waited for: 6 -> 8; matrix products, arithmetic and copies ran while one was open for 23% -> 1% of each run, Pallas kernels for 0% -> 17%
where the time goes in v1:
time: 135 us; the launch traced here: 134 us
  starting transfers between devices  45 us (33%)
  local copies, waits for them, and re-layouts  35.8 us (27%)
  waiting for transfers between devices  27.6 us (20%)
  Pallas kernels  24.8 us (18%)
    unnamed x141, local copies, waits for them, and re-layouts  34.7 us
    pallas_call x10, Pallas kernels, call(): pl.pallas_call(kernel, out_shape=tuple((jax.ShapeDtypeStruct(s, t) for s,...  24.8 us
    ppermute x23, waiting for transfers between devices, swap(): return lax.ppermute(x, axis, [(i, i ^ mask) for i in range(count)])  24.6 us
    ppermute x23, starting transfers between devices, swap(): return lax.ppermute(x, axis, [(i, i ^ mask) for i in range(count)])  24.1 us
    ppermute x6, starting transfers between devices, cross(): return lax.ppermute(x, 'cells', [(i, i ^ masks[i & 1]) for i in range(8)])  10.6 us
    all_to_all x2, starting transfers between devices, shared(): return lax.all_to_all(news, ('cells', 'energy'), 0, 0, tiled=True)  10.4 us
    ppermute x6, waiting for transfers between devices, cross(): return lax.ppermute(x, 'cells', [(i, i ^ masks[i & 1]) for i in range(8)])  3.02 us
  transfers between devices with their start and end apart: 31, of which 8 were waited for; matrix products, arithmetic and copies ran while one was open for 1% of the time, Pallas kernels for 17%

profile of v1, /device:TPU:0, one launch (start us, length us, event | category | flops | bytes accessed | tf_op | source)
XLA Modules:
  0.0 134.4 jit_solution(2049763369909413804)
XLA Ops:
  0.7 1.0 constant_dynamic-slice_fusion
  1.7 5.1 %collective-permute-start.5 = (bf16[128,256]{1,0:T(8,128)(2,1)S(1)}, bf16[128,256]{1,0:T(8,128)(2,1)S(1)}, u32[]{:S(2)}, u32[]{:S(2)}) collective-permute-start(bf16[128,256]{1,0:T(8,128)(2,1)S(1)} %get-tuple-element.38), channel_id=1, source_target_pairs={{0,3},{1,2},{2,1},{3,0},{4,7},{5,6},{6,5},{7,4},{8,11},{9,10},{10,... | collective-permute-start | bytes 196616 | tf_op jit(solution)/shard_map/ppermute | solution.py:22
  7.4 3.7 %collective-permute-start.2 = (bf16[256,256]{1,0:T(8,128)(2,1)}, bf16[256,256]{1,0:T(8,128)(2,1)S(1)}, u32[]{:S(2)}, u32[]{:S(2)}) collective-permute-start(bf16[256,256]{1,0:T(8,128)(2,1)} %refs_0_.3), channel_id=1, source_target_pairs={{0,3},{1,2},{2,1},{3,0},{4,7},{5,6},{6,5},{7,4},{8,11},{9,10},{10,... | collective-permute-start | bytes 393224 | tf_op jit(solution)/shard_map/ppermute | solution.py:22
  11.4 5.4 %collective-permute-done.4.refs_2_ = bf16[128,256]{1,0:T(8,128)(2,1)S(1)} collective-permute-done((bf16[128,256]{1,0:T(8,128)(2,1)S(1)}, bf16[128,256]{1,0:T(8,128)(2,1)S(1)}, u32[]{:S(2)}, u32[]{:S(2)}) %collective-permute-start.4) | collective-permute-done | bytes 65568 | tf_op jit(solution)/shard_map/ppermute | solution.py:22
  17.4 1.6 %collective-permute-start.7 = (bf16[128,1024]{1,0:T(8,128)(2,1)S(1)}, bf16[128,1024]{1,0:T(8,128)(2,1)S(1)}, u32[]{:S(2)}, u32[]{:S(2)}) collective-permute-start(bf16[128,1024]{1,0:T(8,128)(2,1)S(1)} %shard_map.106.refs_4_), channel_id=1, source_target_pairs={{0,16},{4,12},{8,24},{12,4},{16,0},{20,28},{24,8},{28,20},{1,17},{... | collective-permute-start | bytes 786440 | tf_op jit(solution)/shard_map/ppermute | solution.py:32
  19.5 2.9 %collective-permute-start.16 = (bf16[4,256,128]{2,1,0:T(8,128)(2,1)}, bf16[4,256,128]{2,1,0:T(8,128)(2,1)S(1)}, u32[]{:S(2)}, u32[]{:S(2)}) collective-permute-start(bf16[4,256,128]{2,1,0:T(8,128)(2,1)} %refs_4_.3), channel_id=1, source_target_pairs={{0,8},{4,20},{8,0},{12,28},{16,24},{20,4},{24,16},{28,12},{1,9},{5... | collective-permute-start | bytes 786440 | tf_op jit(solution)/shard_map/ppermute | solution.py:32
  23.0 2.6 %collective-permute-done.1.refs_2_ = bf16[256,256]{1,0:T(8,128)(2,1)S(1)} collective-permute-done((bf16[256,256]{1,0:T(8,128)(2,1)}, bf16[256,256]{1,0:T(8,128)(2,1)S(1)}, u32[]{:S(2)}, u32[]{:S(2)}) %collective-permute-start.1) | collective-permute-done | bytes 131104 | tf_op jit(solution)/shard_map/ppermute | solution.py:22
  26.7 2.7 %collective-permute-start.8 = (bf16[128,1024]{1,0:T(8,128)(2,1)S(1)}, bf16[128,1024]{1,0:T(8,128)(2,1)S(1)}, u32[]{:S(2)}, u32[]{:S(2)}) collective-permute-start(bf16[128,1024]{1,0:T(8,128)(2,1)S(1)} %collective-permute-done.7.refs_6_), channel_id=1, source_target_pairs={{0,8},{4,20},{8,0},{12,28},{16,24},{20,4},{24,16},{28,12},{1,9},{5... | collective-permute-start | bytes 786440 | tf_op jit(solution)/shard_map/ppermute | solution.py:32
  29.3 2.1 %collective-permute-done.refs_1_ = bf16[256,256]{1,0:T(8,128)(2,1)S(1)} collective-permute-done((bf16[256,256]{1,0:T(8,128)(2,1)}, bf16[256,256]{1,0:T(8,128)(2,1)S(1)}, u32[]{:S(2)}, u32[]{:S(2)}) %collective-permute-start) | collective-permute-done | bytes 131104 | tf_op jit(solution)/shard_map/ppermute | solution.py:22
  32.1 3.0 %collective-permute-start.18 = (bf16[4,256,128]{2,1,0:T(8,128)(2,1)S(1)}, bf16[4,256,128]{2,1,0:T(8,128)(2,1)S(1)}, u32[]{:S(2)}, u32[]{:S(2)}) collective-permute-start(bf16[4,256,128]{2,1,0:T(8,128)(2,1)S(1)} %collective-permute-done.17.refs_6_), channel_id=1, source_target_pairs={{0,8},{4,20},{8,0},{12,28},{16,24},{20,4},{24,16},{28,12},{1,9},{5... | collective-permute-start | bytes 786440 | tf_op jit(solution)/shard_map/ppermute | solution.py:32
  35.7 0.7 copy-done.23
  36.8 2.6 %collective-permute-done.18.refs_7_ = bf16[4,256,128]{2,1,0:T(8,128)(2,1)S(1)} collective-permute-done((bf16[4,256,128]{2,1,0:T(8,128)(2,1)S(1)}, bf16[4,256,128]{2,1,0:T(8,128)(2,1)S(1)}, u32[]{:S(2)}, u32[]{:S(2)}) %collective-permute-start.18) | collective-permute-done | bytes 262176 | tf_op jit(solution)/shard_map/ppermute | solution.py:32
  39.4 0.7 copy-done.26
  40.7 0.7 copy-done.29
  41.4 0.7 copy.14.owner_ref
  42.1 0.8 copy-done.48
  43.0 0.7 copy-done.61
  43.7 0.7 shard_map.104
  45.0 4.1 %all-to-all-start = ((f32[32,8,128]{2,1,0:T(8,128)}), f32[32,8,128]{2,1,0:T(8,128)S(1)}, u32[]{:S(2)}, u32[]{:S(2)}) async-start(f32[32,8,128]{2,1,0:T(8,128)} %bitcast.28), calls=%async_computation | async-start | bytes 262144 | tf_op jit(solution)/shard_map/all_to_all | solution.py:313
  49.1 0.9 copy-done.24
  50.0 0.9 copy-done.27
  51.0 0.9 copy-done.30
  51.9 0.9 copy-done.34
  52.8 0.9 copy-done.37
  53.7 0.9 copy-done.40
  54.6 0.9 copy-done.43
  55.6 3.4 %shard_map.107 = (bf16[64,1024]{1,0:T(8,128)(2,1)S(1)}, bf16[64,1024]{1,0:T(8,128)(2,1)}, bf16[64,1024]{1,0:T(8,128)(2,1)S(1)}, bf16[64,1024]{1,0:T(8,128)(2,1)S(1)}) custom-call(s32[10]{0:T(128)S(1)} %stack.40.ints_ref, bf16[256,256]{1,0:T(8,128)(2,1)S(1)} %copy-done.34, bf16[256,256]{1,0:T(8,128)(2,1)S(1)} %copy-done.43, bf16[256,256]{1,0:T(8,128)(2,1)S(1)} %copy-done.40, ...), custom_call_target="tpu_custom_call" | custom-call | tf_op jit(solution)/shard_map/pallas_call | solution.py:77
  58.9 0.7 copy-done.52
  60.2 0.7 copy-done.65
  60.9 1.8 %collective-permute-start.13 = (bf16[64,1024]{1,0:T(8,128)(2,1)}, bf16[64,1024]{1,0:T(8,128)(2,1)}, u32[]{:S(2)}, u32[]{:S(2)}) collective-permute-start(bf16[64,1024]{1,0:T(8,128)(2,1)} %get-tuple-element.24), channel_id=1, source_target_pairs={{0,1},{1,0},{2,3},{3,2},{4,5},{5,4},{6,7},{7,6},{8,9},{9,8},{10,11... | collective-permute-start | bytes 393224 | tf_op jit(solution)/shard_map/ppermute | solution.py:22
  62.8 1.0 copy-done.38
  63.8 0.9 copy-done.41
  64.7 0.9 copy-done.44
  65.6 2.5 %shard_map.109 = (f32[256,256]{1,0:T(8,128)S(1)}, bf16[256,256]{1,0:T(8,128)(2,1)}) custom-call(s32[10]{0:T(128)S(1)} %stack.40.ints_ref, f32[256,128]{1,0:T(8,128)S(1)} %bitcast.26, bf16[256,256]{1,0:T(8,128)(2,1)S(1)} %copy-done.35, bf16[256,256]{1,0:T(8,128)(2,1)S(1)} %copy-done.44, bf16[256,256]{1,0:T(8,128)(2,1)S(1)} %copy-done.41, ...), custom_call_target="tpu_custom_call" | custom-call | tf_op jit(solution)/shard_map/pallas_call | solution.py:77
  68.2 0.7 copy-done.50
  68.9 2.4 %collective-permute-start.25 = (bf16[256,256]{1,0:T(8,128)(2,1)}, bf16[256,256]{1,0:T(8,128)(2,1)S(1)}, u32[]{:S(2)}, u32[]{:S(2)}) collective-permute-start(bf16[256,256]{1,0:T(8,128)(2,1)} %get-tuple-element.29.refs_0_), channel_id=1, source_target_pairs={{0,3},{1,2},{2,1},{3,0},{4,7},{5,6},{6,5},{7,4},{8,11},{9,10},{10,... | collective-permute-start | bytes 393224 | tf_op jit(solution)/shard_map/ppermute | solution.py:22
  71.3 2.0 %collective-permute-start.23 = (bf16[256,256]{1,0:T(8,128)(2,1)}, bf16[256,256]{1,0:T(8,128)(2,1)}, u32[]{:S(2)}, u32[]{:S(2)}) collective-permute-start(bf16[256,256]{1,0:T(8,128)(2,1)} %get-tuple-element.29.refs_0_), channel_id=1, source_target_pairs={{0,1},{1,0},{2,3},{3,2},{4,5},{5,4},{6,7},{7,6},{8,9},{9,8},{10,11... | collective-permute-start | bytes 393224 | tf_op jit(solution)/shard_map/ppermute | solution.py:22
  73.3 1.5 %collective-permute-start.14 = (bf16[64,1024]{1,0:T(8,128)(2,1)S(1)}, bf16[64,1024]{1,0:T(8,128)(2,1)S(1)}, u32[]{:S(2)}, u32[]{:S(2)}) collective-permute-start(bf16[64,1024]{1,0:T(8,128)(2,1)S(1)} %copy-done.66), channel_id=1, source_target_pairs={{0,2},{1,3},{2,0},{3,1},{4,6},{5,7},{6,4},{7,5},{8,10},{9,11},{10,... | collective-permute-start | bytes 393224 | tf_op jit(solution)/shard_map/ppermute | solution.py:22
  74.8 0.9 collective-permute-start.15
  75.9 2.6 %shard_map.105 = (bf16[256,4096]{1,0:T(8,128)(2,1)S(1)}, bf16[256,4096]{1,0:T(8,128)(2,1)S(1)}, f32[256,256]{1,0:T(8,128)S(1)}) custom-call(s32[10]{0:T(128)S(1)} %stack.40.ints_ref, s32[1,4096]{1,0:T(1,128)S(1)} %bitcast.32, s32[1,4096]{1,0:T(1,128)S(1)} %bitcast.30, f32[1,4096]{1,0:T(1,128)S(1)} %bitcast.31), custom_call_target="tpu_custom_call" | custom-call | tf_op jit(solution)/shard_map/pallas_call | solution.py:77
  78.5 14.2 %collective-permute-done.14.refs_2_ = bf16[64,1024]{1,0:T(8,128)(2,1)S(1)} collective-permute-done((bf16[64,1024]{1,0:T(8,128)(2,1)S(1)}, bf16[64,1024]{1,0:T(8,128)(2,1)S(1)}, u32[]{:S(2)}, u32[]{:S(2)}) %collective-permute-start.14) | collective-permute-done | bytes 131104 | tf_op jit(solution)/shard_map/ppermute | solution.py:22
  92.7 4.0 %shard_map.108 = (f32[64,256]{1,0:T(8,128)S(1)}, f32[256,128]{1,0:T(8,128)S(1)}) custom-call(s32[10]{0:T(128)S(1)} %stack.40.ints_ref, f32[64,256]{1,0:T(8,128)S(1)} %copy-done.49, f32[256,128]{1,0:T(8,128)S(1)} %bitcast.27, s32[64,1]{1,0:T(8,128)S(1)} %copy.14.owner_ref, s32[1,256]{1,0:T(1,128)S(1)} %bitcast.34, ...), custom_call_target="tpu_custom_call" | custom-call | tf_op jit(solution)/shard_map/pallas_call | solution.py:77
  97.4 0.7 copy-done.54
  98.0 6.3 %all-to-all-start.1 = ((f32[32,8,128]{2,1,0:T(8,128)}), f32[32,8,128]{2,1,0:T(8,128)}, u32[]{:S(2)}, u32[]{:S(2)}) async-start(f32[32,8,128]{2,1,0:T(8,128)} %bitcast.29), calls=%async_computation.1 | async-start | bytes 262144 | tf_op jit(solution)/shard_map/all_to_all | solution.py:313
  104.4 1.0 copy-done.22
  105.4 0.9 copy-done.25
  106.3 0.9 copy-done.28
  107.3 0.9 copy-done.31
  108.2 2.9 %shard_map.110 = (bf16[64,1024]{1,0:T(8,128)(2,1)S(1)}, bf16[64,1024]{1,0:T(8,128)(2,1)S(1)}, bf16[64,1024]{1,0:T(8,128)(2,1)S(1)}, bf16[64,1024]{1,0:T(8,128)(2,1)S(1)}) custom-call(s32[10]{0:T(128)S(1)} %stack.40.ints_ref, bf16[256,256]{1,0:T(8,128)(2,1)} %get-tuple-element.29.refs_0_, bf16[256,256]{1,0:T(8,128)(2,1)} %collective-permute-done.23.refs_1_, ...), custom_call_target="tpu_custom_call" | custom-call | tf_op jit(solution)/shard_map/pallas_call | solution.py:77
  111.2 1.6 %collective-permute-start.26 = (bf16[64,1024]{1,0:T(8,128)(2,1)S(1)}, bf16[64,1024]{1,0:T(8,128)(2,1)S(1)}, u32[]{:S(2)}, u32[]{:S(2)}) collective-permute-start(bf16[64,1024]{1,0:T(8,128)(2,1)S(1)} %get-tuple-element.31), channel_id=1, source_target_pairs={{0,1},{1,0},{2,3},{3,2},{4,5},{5,4},{6,7},{7,6},{8,9},{9,8},{10,11... | collective-permute-start | bytes 393224 | tf_op jit(solution)/shard_map/ppermute | solution.py:22
  112.8 2.4 %collective-permute-start.27 = (bf16[64,1024]{1,0:T(8,128)(2,1)S(1)}, bf16[64,1024]{1,0:T(8,128)(2,1)S(1)}, u32[]{:S(2)}, u32[]{:S(2)}) collective-permute-start(bf16[64,1024]{1,0:T(8,128)(2,1)S(1)} %get-tuple-element.32), channel_id=1, source_target_pairs={{0,2},{1,3},{2,0},{3,1},{4,6},{5,7},{6,4},{7,5},{8,10},{9,11},{10,... | collective-permute-start | bytes 393224 | tf_op jit(solution)/shard_map/ppermute | solution.py:22
  115.6 0.9 copy-done.4
  116.6 0.9 copy-done.6
  117.5 0.9 copy-done.8
  118.5 0.9 copy-done.10
  119.4 0.9 copy-done.12
  120.4 0.9 copy-done.14
  121.3 0.9 copy-done.16
  122.3 0.9 copy-done.46
  123.2 2.3 %shard_map.112.product_ref = f32[4,256,256]{2,1,0:T(8,128)S(1)} custom-call(s32[10]{0:T(128)S(1)} %stack.40.ints_ref, bf16[256,256]{1,0:T(8,128)(2,1)} %get-tuple-element.29.refs_0_, bf16[256,256]{1,0:T(8,128)(2,1)} %collective-permute-done.23.refs_1_, bf16[256,256]{1,0:T(8,128)(2,1)} %collective-permute-done.24.refs_2_, bf16[256,256]{1,0:T(8,128)(2,1)S(1)} %copy-done.46, ...), custom_call_target="tpu_custom_call" | custom-call | tf_op jit(solution)/shard_map/pallas_call | solution.py:77
  125.7 3.7 %shard_map.111 = (f32[64,256]{1,0:T(8,128)S(1)}, f32[64,256]{1,0:T(8,128)S(1)}, f32[64,256]{1,0:T(8,128)S(1)}) custom-call(s32[10]{0:T(128)S(1)} %stack.40.ints_ref, f32[64,256]{1,0:T(8,128)S(1)} %copy-done.60, bf16[256,4096]{1,0:T(8,128)(2,1)S(1)} %get-tuple-element.20.pick_ref, bf16[256,4096]{1,0:T(8,128)(2,1)S(1)} %copy-done.1, ...), custom_call_target="tpu_custom_call" | custom-call | tf_op jit(solution)/shard_map/pallas_call | solution.py:77
  130.7 0.8 copy-done.56
  131.5 0.8 copy-done.58
  132.4 2.1 %shard_map.113 = (f32[256,256]{1,0:T(8,128)}, f32[64,256]{1,0:T(8,128)}) custom-call(s32[10]{0:T(128)S(1)} %stack.40.ints_ref, f32[256,128]{1,0:T(8,128)} %bitcast.22.news_ref, s32[64,1]{1,0:T(8,128)S(1)} %copy.14.owner_ref, f32[64,256]{1,0:T(8,128)S(1)} %get-tuple-element.34.c0_ref, f32[64,256]{1,0:T(8,128)S(1)} %copy-done.56, f32[64,256]{1,0:T(8,128)S(1)} %copy-done.58, ...), custom_call_target="tpu_custom_call" | custom-call | tf_op jit(solution)/shard_map/pallas_call | solution.py:77
  (155 shorter events, 9.8 us)
Async XLA Ops:
  0.7 62.1 %copy-start.2 = (bf16[4,256,128]{2,1,0:T(8,128)(2,1)S(1)}, bf16[4,256,128]{2,1,0:T(8,128)(2,1)}, u32[]{:S(2)}) copy-start(bf16[4,256,128]{2,1,0:T(8,128)(2,1)} %refs_4_.3) | copy-start | bytes 786436
  0.7 62.1 %copy-start.35 = (bf16[256,256]{1,0:T(8,128)(2,1)S(1)}, bf16[256,256]{1,0:T(8,128)(2,1)}, u32[]{:S(2)}) copy-start(bf16[256,256]{1,0:T(8,128)(2,1)} %refs_0_.3) | copy-start | bytes 393220
  1.7 9.6 %collective-permute-start.5 = (bf16[128,256]{1,0:T(8,128)(2,1)S(1)}, bf16[128,256]{1,0:T(8,128)(2,1)S(1)}, u32[]{:S(2)}, u32[]{:S(2)}) collective-permute-start(bf16[128,256]{1,0:T(8,128)(2,1)S(1)} %get-tuple-element.38), channel_id=1, source_target_pairs={{0,3},{1,2},{2,1},{3,0},{4,7},{5,6},{6,5},{7,4},{8,11},{9,10},{10,... | collective-permute-start | bytes 196616 | tf_op jit(solution)/shard_map/ppermute | solution.py:22
  6.8 4.6 %collective-permute-start.3 = (bf16[128,256]{1,0:T(8,128)(2,1)S(1)}, bf16[128,256]{1,0:T(8,128)(2,1)S(1)}, u32[]{:S(2)}, u32[]{:S(2)}) collective-permute-start(bf16[128,256]{1,0:T(8,128)(2,1)S(1)} %get-tuple-element.39), channel_id=1, source_target_pairs={{0,1},{1,0},{2,3},{3,2},{4,5},{5,4},{6,7},{7,6},{8,9},{9,8},{10,11... | collective-permute-start | bytes 196616 | tf_op jit(solution)/shard_map/ppermute | solution.py:22
  6.8 10.0 %collective-permute-start.4 = (bf16[128,256]{1,0:T(8,128)(2,1)S(1)}, bf16[128,256]{1,0:T(8,128)(2,1)S(1)}, u32[]{:S(2)}, u32[]{:S(2)}) collective-permute-start(bf16[128,256]{1,0:T(8,128)(2,1)S(1)} %get-tuple-element.41), channel_id=1, source_target_pairs={{0,2},{1,3},{2,0},{3,1},{4,6},{5,7},{6,4},{7,5},{8,10},{9,11},{10,... | collective-permute-start | bytes 196616 | tf_op jit(solution)/shard_map/ppermute | solution.py:22
  7.4 14.9 %collective-permute-start.2 = (bf16[256,256]{1,0:T(8,128)(2,1)}, bf16[256,256]{1,0:T(8,128)(2,1)S(1)}, u32[]{:S(2)}, u32[]{:S(2)}) collective-permute-start(bf16[256,256]{1,0:T(8,128)(2,1)} %refs_0_.3), channel_id=1, source_target_pairs={{0,3},{1,2},{2,1},{3,0},{4,7},{5,6},{6,5},{7,4},{8,11},{9,10},{10,... | collective-permute-start | bytes 393224 | tf_op jit(solution)/shard_map/ppermute | solution.py:22
  17.4 9.3 %collective-permute-start.7 = (bf16[128,1024]{1,0:T(8,128)(2,1)S(1)}, bf16[128,1024]{1,0:T(8,128)(2,1)S(1)}, u32[]{:S(2)}, u32[]{:S(2)}) collective-permute-start(bf16[128,1024]{1,0:T(8,128)(2,1)S(1)} %shard_map.106.refs_4_), channel_id=1, source_target_pairs={{0,16},{4,12},{8,24},{12,4},{16,0},{20,28},{24,8},{28,20},{1,17},{... | collective-permute-start | bytes 786440 | tf_op jit(solution)/shard_map/ppermute | solution.py:32
  19.0 6.7 %collective-permute-start.1 = (bf16[256,256]{1,0:T(8,128)(2,1)}, bf16[256,256]{1,0:T(8,128)(2,1)S(1)}, u32[]{:S(2)}, u32[]{:S(2)}) collective-permute-start(bf16[256,256]{1,0:T(8,128)(2,1)} %refs_0_.3), channel_id=1, source_target_pairs={{0,2},{1,3},{2,0},{3,1},{4,6},{5,7},{6,4},{7,5},{8,10},{9,11},{10,... | collective-permute-start | bytes 393224 | tf_op jit(solution)/shard_map/ppermute | solution.py:22
  19.0 13.1 %collective-permute-start.17 = (bf16[4,256,128]{2,1,0:T(8,128)(2,1)}, bf16[4,256,128]{2,1,0:T(8,128)(2,1)S(1)}, u32[]{:S(2)}, u32[]{:S(2)}) collective-permute-start(bf16[4,256,128]{2,1,0:T(8,128)(2,1)} %refs_4_.3), channel_id=1, source_target_pairs={{0,16},{4,12},{8,24},{12,4},{16,0},{20,28},{24,8},{28,20},{1,17},{... | collective-permute-start | bytes 786440 | tf_op jit(solution)/shard_map/ppermute | solution.py:32
  19.5 15.6 %collective-permute-start.16 = (bf16[4,256,128]{2,1,0:T(8,128)(2,1)}, bf16[4,256,128]{2,1,0:T(8,128)(2,1)S(1)}, u32[]{:S(2)}, u32[]{:S(2)}) collective-permute-start(bf16[4,256,128]{2,1,0:T(8,128)(2,1)} %refs_4_.3), channel_id=1, source_target_pairs={{0,8},{4,20},{8,0},{12,28},{16,24},{20,4},{24,16},{28,12},{1,9},{5... | collective-permute-start | bytes 786440 | tf_op jit(solution)/shard_map/ppermute | solution.py:32
  23.0 12.1 %collective-permute-start.6 = (bf16[128,1024]{1,0:T(8,128)(2,1)S(1)}, bf16[128,1024]{1,0:T(8,128)(2,1)S(1)}, u32[]{:S(2)}, u32[]{:S(2)}) collective-permute-start(bf16[128,1024]{1,0:T(8,128)(2,1)S(1)} %shard_map.106.refs_4_), channel_id=1, source_target_pairs={{0,8},{4,20},{8,0},{12,28},{16,24},{20,4},{24,16},{28,12},{1,9},{5... | collective-permute-start | bytes 786440 | tf_op jit(solution)/shard_map/ppermute | solution.py:32
  26.3 5.2 %collective-permute-start = (bf16[256,256]{1,0:T(8,128)(2,1)}, bf16[256,256]{1,0:T(8,128)(2,1)S(1)}, u32[]{:S(2)}, u32[]{:S(2)}) collective-permute-start(bf16[256,256]{1,0:T(8,128)(2,1)} %refs_0_.3), channel_id=1, source_target_pairs={{0,1},{1,0},{2,3},{3,2},{4,5},{5,4},{6,7},{7,6},{8,9},{9,8},{10,11... | collective-permute-start | bytes 393224 | tf_op jit(solution)/shard_map/ppermute | solution.py:22
  26.7 41.5 %copy-start.17 = (bf16[128,1024]{1,0:T(8,128)(2,1)}, bf16[128,1024]{1,0:T(8,128)(2,1)S(1)}, u32[]{:S(2)}) copy-start(bf16[128,1024]{1,0:T(8,128)(2,1)S(1)} %collective-permute-done.7.refs_6_) | copy-start | bytes 786436
  26.7 8.9 %collective-permute-start.8 = (bf16[128,1024]{1,0:T(8,128)(2,1)S(1)}, bf16[128,1024]{1,0:T(8,128)(2,1)S(1)}, u32[]{:S(2)}, u32[]{:S(2)}) collective-permute-start(bf16[128,1024]{1,0:T(8,128)(2,1)S(1)} %collective-permute-done.7.refs_6_), channel_id=1, source_target_pairs={{0,8},{4,20},{8,0},{12,28},{16,24},{20,4},{24,16},{28,12},{1,9},{5... | collective-permute-start | bytes 786440 | tf_op jit(solution)/shard_map/ppermute | solution.py:32
  32.1 3.6 %collective-permute-start.9 = (bf16[128,1024]{1,0:T(8,128)(2,1)S(1)}, bf16[128,1024]{1,0:T(8,128)(2,1)S(1)}, u32[]{:S(2)}, u32[]{:S(2)}) collective-permute-start(bf16[128,1024]{1,0:T(8,128)(2,1)S(1)} %shard_map.106.refs_4_), channel_id=1, source_target_pairs={{0,4},{4,0},{8,12},{12,8},{16,20},{20,16},{24,28},{28,24},{1,5},{5... | collective-permute-start | bytes 786440 | tf_op jit(solution)/shard_map/ppermute | solution.py:22
  32.1 36.1 %copy-start.3 = (bf16[4,256,128]{2,1,0:T(8,128)(2,1)}, bf16[4,256,128]{2,1,0:T(8,128)(2,1)S(1)}, u32[]{:S(2)}) copy-start(bf16[4,256,128]{2,1,0:T(8,128)(2,1)S(1)} %collective-permute-done.17.refs_6_) | copy-start | bytes 786436
  32.1 7.3 %collective-permute-start.18 = (bf16[4,256,128]{2,1,0:T(8,128)(2,1)S(1)}, bf16[4,256,128]{2,1,0:T(8,128)(2,1)S(1)}, u32[]{:S(2)}, u32[]{:S(2)}) collective-permute-start(bf16[4,256,128]{2,1,0:T(8,128)(2,1)S(1)} %collective-permute-done.17.refs_6_), channel_id=1, source_target_pairs={{0,8},{4,20},{8,0},{12,28},{16,24},{20,4},{24,16},{28,12},{1,9},{5... | collective-permute-start | bytes 786440 | tf_op jit(solution)/shard_map/ppermute | solution.py:32
  35.1 33.1 %copy-start.5 = (bf16[4,256,128]{2,1,0:T(8,128)(2,1)}, bf16[4,256,128]{2,1,0:T(8,128)(2,1)S(1)}, u32[]{:S(2)}) copy-start(bf16[4,256,128]{2,1,0:T(8,128)(2,1)S(1)} %collective-permute-done.16.refs_5_) | copy-start | bytes 786436
  35.1 4.4 %collective-permute-start.11 = (bf16[128,1024]{1,0:T(8,128)(2,1)S(1)}, bf16[128,1024]{1,0:T(8,128)(2,1)S(1)}, u32[]{:S(2)}, u32[]{:S(2)}) collective-permute-start(bf16[128,1024]{1,0:T(8,128)(2,1)S(1)} %collective-permute-done.7.refs_6_), channel_id=1, source_target_pairs={{0,4},{4,0},{8,12},{12,8},{16,20},{20,16},{24,28},{28,24},{1,5},{5... | collective-permute-start | bytes 786440 | tf_op jit(solution)/shard_map/ppermute | solution.py:22
  35.1 33.1 %copy-start.19 = (bf16[128,1024]{1,0:T(8,128)(2,1)}, bf16[128,1024]{1,0:T(8,128)(2,1)S(1)}, u32[]{:S(2)}) copy-start(bf16[128,1024]{1,0:T(8,128)(2,1)S(1)} %collective-permute-done.6.refs_5_) | copy-start | bytes 786436
  35.1 5.6 %collective-permute-start.10 = (bf16[128,1024]{1,0:T(8,128)(2,1)S(1)}, bf16[128,1024]{1,0:T(8,128)(2,1)S(1)}, u32[]{:S(2)}, u32[]{:S(2)}) collective-permute-start(bf16[128,1024]{1,0:T(8,128)(2,1)S(1)} %collective-permute-done.6.refs_5_), channel_id=1, source_target_pairs={{0,4},{4,0},{8,12},{12,8},{16,20},{20,16},{24,28},{28,24},{1,5},{5... | collective-permute-start | bytes 786440 | tf_op jit(solution)/shard_map/ppermute | solution.py:22
  35.6 32.6 %copy-start.21 = (bf16[128,1024]{1,0:T(8,128)(2,1)}, bf16[128,1024]{1,0:T(8,128)(2,1)S(1)}, u32[]{:S(2)}) copy-start(bf16[128,1024]{1,0:T(8,128)(2,1)S(1)} %collective-permute-done.8.refs_7_) | copy-start | bytes 786436
  35.6 13.5 %collective-permute-start.12 = (bf16[128,1024]{1,0:T(8,128)(2,1)S(1)}, bf16[128,1024]{1,0:T(8,128)(2,1)}, u32[]{:S(2)}, u32[]{:S(2)}) collective-permute-start(bf16[128,1024]{1,0:T(8,128)(2,1)S(1)} %collective-permute-done.8.refs_7_), channel_id=1, source_target_pairs={{0,4},{4,0},{8,12},{12,8},{16,20},{20,16},{24,28},{28,24},{1,5},{5... | collective-permute-start | bytes 786440 | tf_op jit(solution)/shard_map/ppermute | solution.py:22
  36.4 26.3 %collective-permute-start.19 = (bf16[4,256,128]{2,1,0:T(8,128)(2,1)}, bf16[4,256,128]{2,1,0:T(8,128)(2,1)S(1)}, u32[]{:S(2)}, u32[]{:S(2)}) collective-permute-start(bf16[4,256,128]{2,1,0:T(8,128)(2,1)} %refs_4_.3), channel_id=1, source_target_pairs={{0,4},{4,0},{8,12},{12,8},{16,20},{20,16},{24,28},{28,24},{1,5},{5... | collective-permute-start | bytes 786440 | tf_op jit(solution)/shard_map/ppermute | solution.py:22
  39.4 28.8 %copy-start.7 = (bf16[4,256,128]{2,1,0:T(8,128)(2,1)}, bf16[4,256,128]{2,1,0:T(8,128)(2,1)S(1)}, u32[]{:S(2)}) copy-start(bf16[4,256,128]{2,1,0:T(8,128)(2,1)S(1)} %collective-permute-done.18.refs_7_) | copy-start | bytes 786436
  39.4 23.3 %collective-permute-start.21 = (bf16[4,256,128]{2,1,0:T(8,128)(2,1)S(1)}, bf16[4,256,128]{2,1,0:T(8,128)(2,1)S(1)}, u32[]{:S(2)}, u32[]{:S(2)}) collective-permute-start(bf16[4,256,128]{2,1,0:T(8,128)(2,1)S(1)} %collective-permute-done.17.refs_6_), channel_id=1, source_target_pairs={{0,4},{4,0},{8,12},{12,8},{16,20},{20,16},{24,28},{28,24},{1,5},{5... | collective-permute-start | bytes 786440 | tf_op jit(solution)/shard_map/ppermute | solution.py:22
  40.2 22.5 %collective-permute-start.20 = (bf16[4,256,128]{2,1,0:T(8,128)(2,1)S(1)}, bf16[4,256,128]{2,1,0:T(8,128)(2,1)S(1)}, u32[]{:S(2)}, u32[]{:S(2)}) collective-permute-start(bf16[4,256,128]{2,1,0:T(8,128)(2,1)S(1)} %collective-permute-done.16.refs_5_), channel_id=1, source_target_pairs={{0,4},{4,0},{8,12},{12,8},{16,20},{20,16},{24,28},{28,24},{1,5},{5... | collective-permute-start | bytes 786440 | tf_op jit(solution)/shard_map/ppermute | solution.py:22
  41.4 21.4 %collective-permute-start.22 = (bf16[4,256,128]{2,1,0:T(8,128)(2,1)S(1)}, bf16[4,256,128]{2,1,0:T(8,128)(2,1)S(1)}, u32[]{:S(2)}, u32[]{:S(2)}) collective-permute-start(bf16[4,256,128]{2,1,0:T(8,128)(2,1)S(1)} %collective-permute-done.18.refs_7_), channel_id=1, source_target_pairs={{0,4},{4,0},{8,12},{12,8},{16,20},{20,16},{24,28},{28,24},{1,5},{5... | collective-permute-start | bytes 786440 | tf_op jit(solution)/shard_map/ppermute | solution.py:22
  45.0 17.7 %all-to-all-start = ((f32[32,8,128]{2,1,0:T(8,128)}), f32[32,8,128]{2,1,0:T(8,128)S(1)}, u32[]{:S(2)}, u32[]{:S(2)}) async-start(f32[32,8,128]{2,1,0:T(8,128)} %bitcast.28), calls=%async_computation | async-start | bytes 262144 | tf_op jit(solution)/shard_map/all_to_all | solution.py:313
  49.1 1.0 copy-start.24
  50.0 0.9 copy-start.27
  55.6 20.2 %copy-start.67 = (s32[4096]{0:T(1024)S(1)}, s32[4096]{0:T(1024)}, u32[]{:S(2)}) copy-start(s32[4096]{0:T(1024)} %param.15) | copy-start | bytes 49156
  55.6 20.2 %copy-start.68 = (s32[4096]{0:T(1024)S(1)}, s32[4096]{0:T(1024)}, u32[]{:S(2)}) copy-start(s32[4096]{0:T(1024)} %param.16) | copy-start | bytes 49156
  55.6 37.1 %copy-start.49 = (f32[64,256]{1,0:T(8,128)S(1)}, f32[64,256]{1,0:T(8,128)}, u32[]{:S(2)}) copy-start(f32[64,256]{1,0:T(8,128)} %level_ref.3) | copy-start | bytes 196612
  60.9 31.8 %copy-start.62 = (s32[256,1]{0,1:T(1,128)S(1)}, s32[256,1]{0,1:T(1,128)}, u32[]{:S(2)}) copy-start(s32[256,1]{0,1:T(1,128)} %param.14) | copy-start | bytes 3076
  60.9 13.9 %collective-permute-start.13 = (bf16[64,1024]{1,0:T(8,128)(2,1)}, bf16[64,1024]{1,0:T(8,128)(2,1)}, u32[]{:S(2)}, u32[]{:S(2)}) collective-permute-start(bf16[64,1024]{1,0:T(8,128)(2,1)} %get-tuple-element.24), channel_id=1, source_target_pairs={{0,1},{1,0},{2,3},{3,2},{4,5},{5,4},{6,7},{7,6},{8,9},{9,8},{10,11... | collective-permute-start | bytes 393224 | tf_op jit(solution)/shard_map/ppermute | solution.py:22
  62.7 13.1 %copy-start.9 = (bf16[4,256,128]{2,1,0:T(8,128)(2,1)}, bf16[4,256,128]{2,1,0:T(8,128)(2,1)S(1)}, u32[]{:S(2)}) copy-start(bf16[4,256,128]{2,1,0:T(8,128)(2,1)S(1)} %collective-permute-done.19.refs_8_) | copy-start | bytes 786436
  62.7 13.1 %copy-start.11 = (bf16[4,256,128]{2,1,0:T(8,128)(2,1)}, bf16[4,256,128]{2,1,0:T(8,128)(2,1)S(1)}, u32[]{:S(2)}) copy-start(bf16[4,256,128]{2,1,0:T(8,128)(2,1)S(1)} %collective-permute-done.21.refs_10_) | copy-start | bytes 786436
  62.7 13.1 %copy-start.13 = (bf16[4,256,128]{2,1,0:T(8,128)(2,1)}, bf16[4,256,128]{2,1,0:T(8,128)(2,1)S(1)}, u32[]{:S(2)}) copy-start(bf16[4,256,128]{2,1,0:T(8,128)(2,1)S(1)} %collective-permute-done.20.refs_9_) | copy-start | bytes 786436
  62.7 13.1 %copy-start.15 = (bf16[4,256,128]{2,1,0:T(8,128)(2,1)}, bf16[4,256,128]{2,1,0:T(8,128)(2,1)S(1)}, u32[]{:S(2)}) copy-start(bf16[4,256,128]{2,1,0:T(8,128)(2,1)S(1)} %collective-permute-done.22.refs_11_) | copy-start | bytes 786436
  62.8 1.0 copy-start.38
  65.6 7.7 %copy-start.66 = (bf16[64,1024]{1,0:T(8,128)(2,1)S(1)}, bf16[64,1024]{1,0:T(8,128)(2,1)}, u32[]{:S(2)}) copy-start(bf16[64,1024]{1,0:T(8,128)(2,1)} %copy-done.65) | copy-start | bytes 393220
  65.6 9.2 %copy-start.64 = (bf16[64,1024]{1,0:T(8,128)(2,1)S(1)}, bf16[64,1024]{1,0:T(8,128)(2,1)}, u32[]{:S(2)}) copy-start(bf16[64,1024]{1,0:T(8,128)(2,1)} %copy-done.63) | copy-start | bytes 393220
  65.6 10.1 %copy-start.69 = (f32[4096]{0:T(1024)S(1)}, f32[4096]{0:T(1024)}, u32[]{:S(2)}) copy-start(f32[4096]{0:T(1024)} %param.17) | copy-start | bytes 49156
  65.6 27.1 %copy-start.53 = (bf16[64,1024]{1,0:T(8,128)(2,1)S(1)}, bf16[64,1024]{1,0:T(8,128)(2,1)}, u32[]{:S(2)}) copy-start(bf16[64,1024]{1,0:T(8,128)(2,1)} %copy-done.52) | copy-start | bytes 393220
  68.9 35.4 %collective-permute-start.25 = (bf16[256,256]{1,0:T(8,128)(2,1)}, bf16[256,256]{1,0:T(8,128)(2,1)S(1)}, u32[]{:S(2)}, u32[]{:S(2)}) collective-permute-start(bf16[256,256]{1,0:T(8,128)(2,1)} %get-tuple-element.29.refs_0_), channel_id=1, source_target_pairs={{0,3},{1,2},{2,1},{3,0},{4,7},{5,6},{6,5},{7,4},{8,11},{9,10},{10,... | collective-permute-start | bytes 393224 | tf_op jit(solution)/shard_map/ppermute | solution.py:22
  71.3 33.1 %collective-permute-start.24 = (bf16[256,256]{1,0:T(8,128)(2,1)}, bf16[256,256]{1,0:T(8,128)(2,1)}, u32[]{:S(2)}, u32[]{:S(2)}) collective-permute-start(bf16[256,256]{1,0:T(8,128)(2,1)} %get-tuple-element.29.refs_0_), channel_id=1, source_target_pairs={{0,2},{1,3},{2,0},{3,1},{4,6},{5,7},{6,4},{7,5},{8,10},{9,11},{10,... | collective-permute-start | bytes 393224 | tf_op jit(solution)/shard_map/ppermute | solution.py:22
  71.3 33.1 %collective-permute-start.23 = (bf16[256,256]{1,0:T(8,128)(2,1)}, bf16[256,256]{1,0:T(8,128)(2,1)}, u32[]{:S(2)}, u32[]{:S(2)}) collective-permute-start(bf16[256,256]{1,0:T(8,128)(2,1)} %get-tuple-element.29.refs_0_), channel_id=1, source_target_pairs={{0,1},{1,0},{2,3},{3,2},{4,5},{5,4},{6,7},{7,6},{8,9},{9,8},{10,11... | collective-permute-start | bytes 393224 | tf_op jit(solution)/shard_map/ppermute | solution.py:22
  73.3 19.4 %collective-permute-start.14 = (bf16[64,1024]{1,0:T(8,128)(2,1)S(1)}, bf16[64,1024]{1,0:T(8,128)(2,1)S(1)}, u32[]{:S(2)}, u32[]{:S(2)}) collective-permute-start(bf16[64,1024]{1,0:T(8,128)(2,1)S(1)} %copy-done.66), channel_id=1, source_target_pairs={{0,2},{1,3},{2,0},{3,1},{4,6},{5,7},{6,4},{7,5},{8,10},{9,11},{10,... | collective-permute-start | bytes 393224 | tf_op jit(solution)/shard_map/ppermute | solution.py:22
  74.8 17.9 %collective-permute-start.15 = (bf16[64,1024]{1,0:T(8,128)(2,1)S(1)}, bf16[64,1024]{1,0:T(8,128)(2,1)S(1)}, u32[]{:S(2)}, u32[]{:S(2)}) collective-permute-start(bf16[64,1024]{1,0:T(8,128)(2,1)S(1)} %copy-done.64), channel_id=1, source_target_pairs={{0,3},{1,2},{2,1},{3,0},{4,7},{5,6},{6,5},{7,4},{8,11},{9,10},{10,... | collective-permute-start | bytes 393224 | tf_op jit(solution)/shard_map/ppermute | solution.py:22
  78.4 18.3 %copy-start = (bf16[256,4096]{1,0:T(8,128)(2,1)}, bf16[256,4096]{1,0:T(8,128)(2,1)S(1)}, u32[]{:S(2)}) copy-start(bf16[256,4096]{1,0:T(8,128)(2,1)S(1)} %get-tuple-element.21.move_ref) | copy-start | bytes 6291460
  78.5 18.3 %copy-start.32 = (f32[256,256]{1,0:T(8,128)}, f32[256,256]{1,0:T(8,128)S(1)}, u32[]{:S(2)}) copy-start(f32[256,256]{1,0:T(8,128)S(1)} %get-tuple-element.22.drain_ref) | copy-start | bytes 786436
  92.7 11.7 %copy-start.18 = (bf16[128,1024]{1,0:T(8,128)(2,1)S(1)}, bf16[128,1024]{1,0:T(8,128)(2,1)}, u32[]{:S(2)}) copy-start(bf16[128,1024]{1,0:T(8,128)(2,1)} %copy-done.17) | copy-start | bytes 786436
  92.7 11.7 %copy-start.20 = (bf16[128,1024]{1,0:T(8,128)(2,1)S(1)}, bf16[128,1024]{1,0:T(8,128)(2,1)}, u32[]{:S(2)}) copy-start(bf16[128,1024]{1,0:T(8,128)(2,1)} %copy-done.19) | copy-start | bytes 786436
  98.0 32.6 %all-to-all-start.1 = ((f32[32,8,128]{2,1,0:T(8,128)}), f32[32,8,128]{2,1,0:T(8,128)}, u32[]{:S(2)}, u32[]{:S(2)}) async-start(f32[32,8,128]{2,1,0:T(8,128)} %bitcast.29), calls=%async_computation.1 | async-start | bytes 262144 | tf_op jit(solution)/shard_map/all_to_all | solution.py:313
  104.3 10.8 %copy-start.45 = (bf16[256,256]{1,0:T(8,128)(2,1)}, bf16[256,256]{1,0:T(8,128)(2,1)S(1)}, u32[]{:S(2)}) copy-start(bf16[256,256]{1,0:T(8,128)(2,1)S(1)} %collective-permute-done.25.refs_3_) | copy-start | bytes 393220
  104.4 1.0 copy-start.22
  108.2 17.4 %copy-start.33 = (f32[256,256]{1,0:T(8,128)S(1)}, f32[256,256]{1,0:T(8,128)}, u32[]{:S(2)}) copy-start(f32[256,256]{1,0:T(8,128)} %copy-done.32) | copy-start | bytes 786436
  108.2 17.4 %copy-start.60 = (f32[64,256]{1,0:T(8,128)S(1)}, f32[64,256]{1,0:T(8,128)}, u32[]{:S(2)}) copy-start(f32[64,256]{1,0:T(8,128)} %copy-done.59) | copy-start | bytes 196612
  111.2 14.5 %copy-start.1 = (bf16[256,4096]{1,0:T(8,128)(2,1)S(1)}, bf16[256,4096]{1,0:T(8,128)(2,1)}, u32[]{:S(2)}) copy-start(bf16[256,4096]{1,0:T(8,128)(2,1)} %copy-done) | copy-start | bytes 6291460
  111.2 14.4 %collective-permute-start.26 = (bf16[64,1024]{1,0:T(8,128)(2,1)S(1)}, bf16[64,1024]{1,0:T(8,128)(2,1)S(1)}, u32[]{:S(2)}, u32[]{:S(2)}) collective-permute-start(bf16[64,1024]{1,0:T(8,128)(2,1)S(1)} %get-tuple-element.31), channel_id=1, source_target_pairs={{0,1},{1,0},{2,3},{3,2},{4,5},{5,4},{6,7},{7,6},{8,9},{9,8},{10,11... | collective-permute-start | bytes 393224 | tf_op jit(solution)/shard_map/ppermute | solution.py:22
  112.8 12.9 %collective-permute-start.27 = (bf16[64,1024]{1,0:T(8,128)(2,1)S(1)}, bf16[64,1024]{1,0:T(8,128)(2,1)S(1)}, u32[]{:S(2)}, u32[]{:S(2)}) collective-permute-start(bf16[64,1024]{1,0:T(8,128)(2,1)S(1)} %get-tuple-element.32), channel_id=1, source_target_pairs={{0,2},{1,3},{2,0},{3,1},{4,6},{5,7},{6,4},{7,5},{8,10},{9,11},{10,... | collective-permute-start | bytes 393224 | tf_op jit(solution)/shard_map/ppermute | solution.py:22
  115.2 10.5 %collective-permute-start.28 = (bf16[64,1024]{1,0:T(8,128)(2,1)S(1)}, bf16[64,1024]{1,0:T(8,128)(2,1)S(1)}, u32[]{:S(2)}, u32[]{:S(2)}) collective-permute-start(bf16[64,1024]{1,0:T(8,128)(2,1)S(1)} %get-tuple-element.33), channel_id=1, source_target_pairs={{0,3},{1,2},{2,1},{3,0},{4,7},{5,6},{6,5},{7,4},{8,11},{9,10},{10,... | collective-permute-start | bytes 393224 | tf_op jit(solution)/shard_map/ppermute | solution.py:22
  125.7 5.0 %copy-start.51 = (f32[256,256]{1,0:T(8,128)S(1)}, f32[256,256]{1,0:T(8,128)}, u32[]{:S(2)}) copy-start(f32[256,256]{1,0:T(8,128)} %copy-done.50) | copy-start | bytes 786436
  (37 other events, 30.0 us)

commit v2 on v1

v2 whole, which is shorter than its diff:
```python
import jax
import jax.numpy as jnp
from jax import lax
from jax.experimental import pallas as pl
from jax.experimental.pallas import tpu as pltpu
from jax.sharding import PartitionSpec as P

boltz_step = 0.5
level_step = 0.04
depth_scale = 2.0

BF = jnp.bfloat16
F32 = jnp.float32
NT = (((1,), (1,)), ((), ()))
TILE = 8
LANES = 128
COLUMN_ROW = 4
PARAMS = pltpu.CompilerParams(vmem_limit_bytes=24 << 20)


def swap(x, axis, mask, count):
    return lax.ppermute(x, axis, [(i, i ^ mask) for i in range(count)])


def others(x, ne):
    got = {mask: swap(x, "energy", mask, ne) for mask in range(ne - 1, 0, -1)}
    return [x] + [got[mask] for mask in range(1, ne)]


def cross(x, first):
    masks = (2, 4) if first else (4, 2)
    return lax.ppermute(x, "cells", [(i, i ^ masks[i & 1]) for i in range(8)])


def gathered_places(i):
    first = jnp.where((i & 1) == 0, 2, 4)
    own = [i, i ^ first, i ^ (6 - first), i ^ 6]
    sibling = [i ^ 1, i ^ 1 ^ (6 - first), i ^ 1 ^ first, i ^ 7]
    return own + sibling


def aligned(index, size):
    return pl.ds(pl.multiple_of(index * size, size), size)


def split(x):
    high = x.astype(BF)
    return high, (x - high.astype(F32)).astype(BF)


def halves(x):
    return jnp.concatenate(split(x), 0)


def dot(a, b):
    return jnp.dot(a, b, preferred_element_type=F32)


def dot_nt(a, b):
    return lax.dot_general(a, b, NT, preferred_element_type=F32)


def fold(x):
    n = x.shape[0] // 2
    return x[:n] + x[n:]


def call(kernel, shapes, ints, args, scratch=()):
    n, o = len(args), len(shapes)

    def whole(ints_ref, *refs):
        kernel(ints_ref, refs[:n], refs[n : n + o], refs[n + o :])

    return pl.pallas_call(
        whole,
        out_shape=tuple(jax.ShapeDtypeStruct(s, t) for s, t in shapes),
        in_specs=[pl.BlockSpec(memory_space=pltpu.SMEM)] + [pl.BlockSpec()] * n,
        scratch_shapes=list(scratch),
        compiler_params=PARAMS,
    )(ints, *args)


def after(x, *others):
    return lax.optimization_barrier((x,) + others)[0]


def zones_of(owner_ref):
    rows = owner_ref.shape[1]
    owner = owner_ref[...].astype(F32)
    if rows < LANES:
        owner = jnp.concatenate([owner, jnp.zeros((1, LANES - rows), F32)], 1)
    owner = jnp.transpose(jnp.broadcast_to(owner, (TILE, LANES)))[:rows, 0:1]
    lanes = lax.broadcasted_iota(jnp.int32, (rows, LANES), 1).astype(F32)
    return jnp.where(owner == lanes, 1.0, 0.0)


def news_of(levels, zones, partner_ref):
    rows, total = levels.shape
    ids = lax.broadcasted_iota(jnp.int32, (TILE, total), 0)
    chosen = jnp.where(ids == partner_ref[...], 1.0, 0.0)
    number = jnp.maximum(jnp.sum(chosen, axis=1, keepdims=True), 1.0)
    chosen = chosen.astype(BF)
    high, low = split(levels)
    density = (dot_nt(chosen, high) + dot_nt(chosen, low)) / number
    tile = jnp.concatenate([density, jnp.zeros((TILE, LANES - rows), F32)], 1)
    column = jnp.sum(zones * levels[:, 0:1], axis=0, keepdims=True)
    at = lax.broadcasted_iota(jnp.int32, (TILE, LANES), 0)
    return jnp.where(at == COLUMN_ROW, column, tile)


def message_kernel(ints_ref, args, outs, scratch):
    section_ref, level_ref, partner_ref, owner_ref = args
    k = ints_ref[0]
    news = halves(news_of(level_ref[...], zones_of(owner_ref), partner_ref))
    part = outs[0].shape[0] - 2 * TILE
    width = outs[0].shape[1]
    if width > LANES:
        news = jnp.concatenate([news, jnp.zeros((2 * TILE, width - LANES), BF)], 1)
    for mask, out in enumerate(outs):
        out[:part, :] = section_ref[aligned(k ^ mask, part), :]
        out[part:, :] = news


def pack_kernel(ints_ref, args, outs, scratch):
    packed_ref, news_ref = outs
    k = ints_ref[0]
    part = packed_ref.shape[0] - 2 * TILE
    total = None
    for mask, ref in enumerate(args):
        packed_ref[:part, aligned(k ^ mask, ref.shape[1])] = ref[:part, :]
        news = fold(ref[part:, :LANES].astype(F32))
        news_ref[aligned(k ^ mask, TILE), :] = news
        total = news if total is None else total + news
    packed_ref[part:, :] = jnp.concatenate(
        [halves(total), jnp.zeros((2 * TILE, packed_ref.shape[1] - LANES), BF)], 1
    )


def escape_of(column, zones, block):
    escape = 1.0 / (1.0 + depth_scale * column[COLUMN_ROW : COLUMN_ROW + 1] / block)
    return jnp.sum(zones * escape, axis=1, keepdims=True)


def density_of(news_ref, first, ne, slab):
    parts = []
    for z in range(ne):
        parts.append(jnp.transpose(news_ref[aligned(first + z, TILE), :])[:slab])
    return jnp.concatenate(parts, 0)


def tables_kernel(cells, energies):
    def kernel(ints_ref, args, outs, scratch):
        source_ref, hop_ref, rad_ref = args
        pick_ref, move_ref, drain_ref = outs
        chunks, levels, step = pick_ref.shape
        part = chunks * step // (cells * energies)
        starts = [c * energies * part + z * part for z in range(energies) for c in range(cells)]
        acc = jnp.zeros((levels, levels), F32)
        ids = lax.broadcasted_iota(jnp.int32, (levels, step), 0)
        each = step // part
        for n in range(chunks):

            def row(ref):
                pieces = [ref[0:1, at : at + part] for at in starts[n * each : (n + 1) * each]]
                return pieces[0] if each == 1 else jnp.concatenate(pieces, 1)

            source = row(source_ref)
            target = source + row(hop_ref)
            target = jnp.where(target >= levels, target - levels, target)
            pick = jnp.where(ids == source, 1.0, 0.0)
            move = (jnp.where(ids == target, 1.0, 0.0) - pick).astype(BF)
            pick_ref[n] = pick.astype(BF)
            move_ref[n] = move
            rad = row(rad_ref)
            high = rad.astype(BF).astype(F32)
            acc += dot_nt((pick * high).astype(BF), move)
            acc += dot_nt((pick * (rad - high)).astype(BF), move)
        drain_ref[...] = acc

    return kernel


def scatter(pairs, k, rate_refs, pick_ref, move_ref, groups):
    rows = pairs.shape[0] // (2 * groups)
    step = pick_ref.shape[2]
    acc = jnp.zeros(pairs.shape, F32)
    for mask, ref in enumerate(rate_refs):
        each = ref.shape[1] // step
        for inner in range(each):
            n = (k ^ mask) * each + inner
            rate = ref[:, inner * step : (inner + 1) * step].astype(F32)
            picked = dot(pairs, pick_ref[n])
            parts = []
            for g in range(groups):
                parts.append(halves(rate * fold(picked[2 * g * rows : 2 * (g + 1) * rows])))
            flux = parts[0] if groups == 1 else jnp.concatenate(parts, 0)
            acc += dot_nt(flux, move_ref[n])
    return [fold(acc[2 * g * rows : 2 * (g + 1) * rows]) for g in range(groups)]


def drained(pairs, drain_ref):
    high, low = split(drain_ref[...])
    return fold(dot(pairs, high) + dot(pairs, low))


def first_kernel(block):
    def kernel(ints_ref, args, outs, scratch):
        level_ref, column_ref, owner_ref, partner_ref, pick_ref, move_ref, drain_ref, *rates = args
        levels = level_ref[...]
        zones = zones_of(owner_ref)
        escape = escape_of(column_ref[...], zones, block)
        for _ in range(2):
            pairs = halves(levels)
            (moved,) = scatter(pairs, ints_ref[0], rates, pick_ref, move_ref, 1)
            levels = levels + level_step * (moved + escape * drained(pairs, drain_ref))
        outs[0][...] = levels
        news = news_of(levels, zones, partner_ref)
        for n in range(outs[1].shape[0] // TILE):
            outs[1][n * TILE : (n + 1) * TILE, :] = news

    return kernel


def second_kernel(ints_ref, args, outs, scratch):
    level_ref, pick_ref, move_ref, drain_ref, *rates = args
    k = ints_ref[0]
    levels = level_ref[...]
    pairs = halves(levels)
    (moved,) = scatter(pairs, k, rates, pick_ref, move_ref, 1)
    u = levels + level_step * moved
    v = level_step * drained(pairs, drain_ref)
    pu, pv = halves(u), halves(v)
    mu, mv = scatter(jnp.concatenate([pu, pv], 0), k, rates, pick_ref, move_ref, 2)
    outs[0][0] = u + level_step * mu
    outs[0][1] = v + level_step * (mv + drained(pu, drain_ref))
    outs[0][2] = level_step * drained(pv, drain_ref)


def final_kernel(block, ne, slab):
    def kernel(ints_ref, args, outs, scratch):
        news_ref, owner_ref, term_ref, current_ref, product_ref = args
        news = news_ref[...].reshape(news_ref.shape[0] // TILE, TILE, LANES)
        escape = escape_of(jnp.sum(news, axis=0), zones_of(owner_ref), block)
        outs[1][...] = term_ref[0] + escape * (term_ref[1] + escape * term_ref[2])
        density = density_of(news_ref, ints_ref[1] * ne, ne, slab)
        summed = density[:, 0:1] * product_ref[0]
        for p in range(1, product_ref.shape[0]):
            summed = summed + density[:, p : p + 1] * product_ref[p]
        outs[0][...] = current_ref[...] + boltz_step * summed

    return kernel


def place(ints_ref, parts, row_ref):
    for mask, ref in enumerate(parts):
        row_ref[:, aligned(ints_ref[0] ^ mask, ref.shape[1])] = ref[...]


def product_of(ints_ref, row_ref, parts, p):
    total = None
    for n, ref in enumerate(parts):
        width = ref.shape[2]
        lhs = row_ref[...] if len(parts) == 1 else row_ref[:, aligned(ints_ref[2 + n], width)]
        term = dot_nt(lhs, ref[p])
        total = term if total is None else total + term
    return total


def first_product_kernel(ne, slab):
    def kernel(ints_ref, args, outs, scratch):
        news_ref, *args = args
        spectra, parts, (row_ref,) = args[:ne], args[ne:], scratch
        place(ints_ref, spectra, row_ref)
        density = density_of(news_ref, 0, ne, slab)
        summed = None
        for p in range(parts[0].shape[0]):
            term = density[:, p : p + 1] * product_of(ints_ref, row_ref, parts, p)
            summed = term if summed is None else summed + term
        current = spectra[0][...].astype(F32) + boltz_step * summed
        outs[0][...] = current
        outs[1][...] = current.astype(BF)

    return kernel


def second_product_kernel(ne):
    def kernel(ints_ref, args, outs, scratch):
        place(ints_ref, args[:ne], scratch[0])
        for p in range(outs[0].shape[0]):
            outs[0][p] = product_of(ints_ref, scratch[0], args[ne:], p)

    return kernel


def rates_kernel(ne, small):
    def kernel(ints_ref, args, outs, scratch):
        spectra, parts, (row_ref, rate_ref) = args[:ne], args[ne:], scratch
        outs, column_ref = outs[:ne], outs[ne]
        place(ints_ref, spectra, row_ref)
        row = row_ref[...]
        column = None
        for n, ref in enumerate(parts):
            part = ref.shape[0] - 2 * TILE
            rates = jax.nn.softplus(dot_nt(row, ref[:part, :])).astype(BF)
            if small:
                rate_ref[:, aligned(ints_ref[2 + n], part)] = rates
            else:
                rate_ref[:, n * part : (n + 1) * part] = rates
            own = fold(ref[part:, :LANES].astype(F32))
            column = own if column is None else column + own
        column_ref[...] = column
        for mask, out in enumerate(outs):
            out[...] = rate_ref[aligned(ints_ref[0] ^ mask, out.shape[0]), :]

    return kernel


def body(
    distribution,
    operators,
    sections,
    populations,
    cell_owner,
    partner_of,
    source,
    level_hop,
    radiative,
):
    nc = lax.axis_size("cells")
    ne = lax.axis_size("energy")
    i = lax.axis_index("cells")
    k = lax.axis_index("energy")
    slab, level_total = populations.shape
    block, width = distribution.shape
    partner_total, outs, _ = operators.shape
    reactions = source.shape[0]
    part = sections.shape[0] // ne
    small = nc == 8
    places = gathered_places(i) if small else []
    ints = jnp.stack([v.astype(jnp.int32) for v in [k, i] + places])
    partner_row = partner_of.reshape(1, level_total)
    owner_row = cell_owner.reshape(1, slab)

    messages = call(
        message_kernel,
        [((part + 2 * TILE, width), BF)] * ne,
        ints,
        [sections, populations, partner_row, owner_row],
    )
    shares = {m: swap(messages[m], "energy", m, ne) for m in range(ne - 1, 0, -1)}
    spectra = others(distribution, ne)
    packed_shape = [((part + 2 * TILE, ne * width), BF), ((ne * TILE, LANES), F32)]
    packed_args = [messages[0]] + [shares[m] for m in range(1, ne)]
    if small:
        a, b = cross(operators, True), cross(operators, False)
        c = cross(b, True)
        own = swap(operators, "cells", 1, 8)
        packed_args[1] = after(packed_args[1], a, b, own)
        packed, density = call(pack_kernel, packed_shape, ints, packed_args)
        operator_parts = [operators, a, b, c, own] + [swap(v, "cells", 1, 8) for v in (a, b, c)]
        a, b = cross(packed, True), cross(packed, False)
        c = cross(after(b, operator_parts[3]), True)
        section_parts = [packed, a, b, c] + [swap(v, "cells", 1, 8) for v in (packed, a, b, c)]
    else:
        packed, density = call(pack_kernel, packed_shape, ints, packed_args)
        operator_parts = [lax.all_gather(operators, "cells", axis=2, tiled=True)]
        every = lax.all_gather(packed, "cells")
        section_parts = [every[n] for n in range(nc)]

    chunks = ((max(1, reactions // 512), level_total, min(512, reactions)), BF)
    pick, move, drain = call(
        tables_kernel(nc, ne),
        [chunks, chunks, ((level_total, level_total), F32)],
        ints,
        [v.reshape(1, reactions) for v in (source, level_hop, radiative)],
    )

    row = pltpu.VMEM((block, ne * width), BF)

    def rates_of(spectra):
        *rates, column = call(
            rates_kernel(ne, small),
            [((slab, nc * part), BF)] * ne + [((TILE, LANES), F32)],
            ints,
            list(spectra) + section_parts,
            [row, pltpu.VMEM((block, nc * part), BF)],
        )
        got = {m: swap(rates[m], "energy", m, ne) for m in range(ne - 1, 0, -1)}
        return [rates[0]] + [got[m] for m in range(1, ne)], column

    current, later = call(
        first_product_kernel(ne, slab),
        [((block, outs), F32), ((block, outs), BF)],
        ints,
        [density] + spectra + operator_parts,
        [row],
    )
    later = others(later, ne)
    rates, column = rates_of(spectra)
    (products,) = call(
        second_product_kernel(ne),
        [((partner_total, block, outs), F32)],
        ints,
        later + operator_parts,
        [row],
    )
    later_rates, _ = rates_of(later)
    rates[0] = after(rates[0], later_rates[0], products)
    levels, news = call(
        first_kernel(block),
        [(populations.shape, F32), ((nc * ne * TILE, LANES), F32)],
        ints,
        [populations, column, owner_row, partner_row, pick, move, drain] + rates,
    )
    news = lax.all_to_all(news, ("cells", "energy"), 0, 0, tiled=True)
    (terms,) = call(
        second_kernel,
        [((3,) + populations.shape, F32)],
        ints,
        [levels, pick, move, drain] + later_rates,
    )
    return call(
        final_kernel(block, ne, slab),
        [((block, outs), F32), (populations.shape, F32)],
        ints,
        [after(news, terms), owner_row, terms, current, products],
    )


def solution(mesh):
    return jax.shard_map(
        body,
        mesh=mesh,
        in_specs=(
            P("cells", "energy"),
            P(None, "energy", "cells"),
            P("cells", "energy"),
            P(("cells", "energy"), None),
            P(("cells", "energy"), None),
            P(),
            P(),
            P(),
            P(),
        ),
        out_specs=(P("cells", "energy"), P(("cells", "energy"), None)),
        check_vma=False,
    )
```

time: 135 us -> 103 us (0.76)
  local copies, waits for them, and re-layouts: 35.8 us -> 12.3 us
  starting transfers between devices: 45 us -> 41 us
  Pallas kernels: 24.8 us -> 22.2 us
    unnamed x141 -> x54, local copies, waits for them, and re-layouts: 34.7 us -> 12.2 us
    all_to_all x2 -> x1, starting transfers between devices: 10.4 us -> 5.61 us  [body(): news = lax.all_to_all(news, ('cells', 'energy'), 0, 0, tiled=True)]
    ppermute x23, starting transfers between devices: 24.1 us -> 27.9 us  [swap(): return lax.ppermute(x, axis, [(i, i ^ mask) for i in range(count)])]
    ppermute x6, starting transfers between devices: 10.6 us -> 7.44 us  [cross(): return lax.ppermute(x, 'cells', [(i, i ^ masks[i & 1]) for i in range(8)])]
    pallas_call x10, Pallas kernels: 24.8 us -> 22.2 us  [call(): pl.pallas_call(whole, out_shape=tuple((jax.ShapeDtypeStruct(s, t) for s,...]
    ppermute x23, waiting for transfers between devices: 24.6 us -> 23 us  [swap(): return lax.ppermute(x, axis, [(i, i ^ mask) for i in range(count)])]
  transfers between devices with their start and end apart: 31 -> 30, of which waited for: 8 -> 12; matrix products, arithmetic and copies ran while one was open for 1% -> 0% of each run, Pallas kernels for 17% -> 15%
where the time goes in v2:
time: 103 us
  starting transfers between devices  41 us (40%)
  waiting for transfers between devices  26.4 us (26%)
  Pallas kernels  22.2 us (22%)
  local copies, waits for them, and re-layouts  12.3 us (12%)
    ppermute x23, starting transfers between devices, swap(): return lax.ppermute(x, axis, [(i, i ^ mask) for i in range(count)])  27.9 us
    ppermute x23, waiting for transfers between devices, swap(): return lax.ppermute(x, axis, [(i, i ^ mask) for i in range(count)])  23 us
    pallas_call x10, Pallas kernels, call(): pl.pallas_call(whole, out_shape=tuple((jax.ShapeDtypeStruct(s, t) for s,...  22.2 us
    unnamed x54, local copies, waits for them, and re-layouts  12.2 us
    ppermute x6, starting transfers between devices, cross(): return lax.ppermute(x, 'cells', [(i, i ^ masks[i & 1]) for i in range(8)])  7.44 us
    all_to_all x1, starting transfers between devices, body(): news = lax.all_to_all(news, ('cells', 'energy'), 0, 0, tiled=True)  5.61 us
    ppermute x6, waiting for transfers between devices, cross(): return lax.ppermute(x, 'cells', [(i, i ^ masks[i & 1]) for i in range(8)])  3.36 us
  transfers between devices with their start and end apart: 30, of which 12 were waited for; matrix products, arithmetic and copies ran while one was open for 0% of the time, Pallas kernels for 15%

profile of v2, /device:TPU:0, one launch (start us, length us, event | category | flops | bytes accessed | tf_op | source)
XLA Modules:
  0.0 102.7 jit_solution(1012782585628848763)
XLA Ops:
  0.6 0.5 collective-permute-start.6
  1.1 2.6 %collective-permute-start.5 = (bf16[4,256,128]{2,1,0:T(8,128)(2,1)}, bf16[4,256,128]{2,1,0:T(8,128)(2,1)S(1)}, u32[]{:S(2)}, u32[]{:S(2)}) collective-permute-start(bf16[4,256,128]{2,1,0:T(8,128)(2,1)} %refs_4_.1), channel_id=1, source_target_pairs={{0,16},{4,12},{8,24},{12,4},{16,0},{20,28},{24,8},{28,20},{1,17},{... | collective-permute-start | bytes 786440 | tf_op jit(solution)/shard_map/ppermute | solution.py:32
  3.7 1.5 %collective-permute-start.4 = (bf16[4,256,128]{2,1,0:T(8,128)(2,1)}, bf16[4,256,128]{2,1,0:T(8,128)(2,1)S(1)}, u32[]{:S(2)}, u32[]{:S(2)}) collective-permute-start(bf16[4,256,128]{2,1,0:T(8,128)(2,1)} %refs_4_.1), channel_id=1, source_target_pairs={{0,8},{4,20},{8,0},{12,28},{16,24},{20,4},{24,16},{28,12},{1,9},{5... | collective-permute-start | bytes 786440 | tf_op jit(solution)/shard_map/ppermute | solution.py:32
  5.2 0.1 stack.40.ints_ref
  5.3 0.8 copy-done.11
  6.2 0.9 copy-done.13
  7.1 0.7 copy-done.21
  7.8 0.7 copy-done.23
  8.4 0.7 shard_map.104
  9.2 1.6 %collective-permute-start.3 = (bf16[144,256]{1,0:T(8,128)(2,1)S(1)}, bf16[144,256]{1,0:T(8,128)(2,1)S(1)}, u32[]{:S(2)}, u32[]{:S(2)}) collective-permute-start(bf16[144,256]{1,0:T(8,128)(2,1)S(1)} %get-tuple-element.29), channel_id=1, source_target_pairs={{0,1},{1,0},{2,3},{3,2},{4,5},{5,4},{6,7},{7,6},{8,9},{9,8},{10,11... | collective-permute-start | bytes 221192 | tf_op jit(solution)/shard_map/ppermute | solution.py:22
  10.8 2.6 %collective-permute-start.7 = (bf16[144,256]{1,0:T(8,128)(2,1)S(1)}, bf16[144,256]{1,0:T(8,128)(2,1)S(1)}, u32[]{:S(2)}, u32[]{:S(2)}) collective-permute-start(bf16[144,256]{1,0:T(8,128)(2,1)S(1)} %get-tuple-element.31), channel_id=1, source_target_pairs={{0,2},{1,3},{2,0},{3,1},{4,6},{5,7},{6,4},{7,5},{8,10},{9,11},{10,... | collective-permute-start | bytes 221192 | tf_op jit(solution)/shard_map/ppermute | solution.py:22
  13.4 0.2 collective-permute-done.3.refs_1_
  13.6 4.4 %collective-permute-start.8 = (bf16[144,256]{1,0:T(8,128)(2,1)S(1)}, bf16[144,256]{1,0:T(8,128)(2,1)S(1)}, u32[]{:S(2)}, u32[]{:S(2)}) collective-permute-start(bf16[144,256]{1,0:T(8,128)(2,1)S(1)} %get-tuple-element.32), channel_id=1, source_target_pairs={{0,3},{1,2},{2,1},{3,0},{4,7},{5,6},{6,5},{7,4},{8,11},{9,10},{10,... | collective-permute-start | bytes 221192 | tf_op jit(solution)/shard_map/ppermute | solution.py:22
  18.0 0.3 collective-permute-done.7.refs_2_
  18.3 2.0 %collective-permute-done.8.refs_3_ = bf16[144,256]{1,0:T(8,128)(2,1)S(1)} collective-permute-done((bf16[144,256]{1,0:T(8,128)(2,1)S(1)}, bf16[144,256]{1,0:T(8,128)(2,1)S(1)}, u32[]{:S(2)}, u32[]{:S(2)}) %collective-permute-start.8) | collective-permute-done | bytes 73760 | tf_op jit(solution)/shard_map/ppermute | solution.py:22
  20.3 0.6 shard_map.105
  20.9 0.6 collective-permute-start.10
  21.4 0.5 collective-permute-start.11
  22.0 3.8 %collective-permute-start.2 = (bf16[256,256]{1,0:T(8,128)(2,1)}, bf16[256,256]{1,0:T(8,128)(2,1)S(1)}, u32[]{:S(2)}, u32[]{:S(2)}) collective-permute-start(bf16[256,256]{1,0:T(8,128)(2,1)} %refs_1_.3), channel_id=1, source_target_pairs={{0,3},{1,2},{2,1},{3,0},{4,7},{5,6},{6,5},{7,4},{8,11},{9,10},{10,... | collective-permute-start | bytes 393224 | tf_op jit(solution)/shard_map/ppermute | solution.py:22
  25.8 1.5 %collective-permute-start.9 = (bf16[144,1024]{1,0:T(8,128)(2,1)S(1)}, bf16[144,1024]{1,0:T(8,128)(2,1)S(1)}, u32[]{:S(2)}, u32[]{:S(2)}) collective-permute-start(bf16[144,1024]{1,0:T(8,128)(2,1)S(1)} %get-tuple-element.33.refs_4_), channel_id=1, source_target_pairs={{0,8},{4,20},{8,0},{12,28},{16,24},{20,4},{24,16},{28,12},{1,9},{5... | collective-permute-start | bytes 884744 | tf_op jit(solution)/shard_map/ppermute | solution.py:32
  27.3 0.5 collective-permute-done.11.refs_8_.refs_7_
  27.8 2.8 %collective-permute-done.10.refs_6_ = bf16[144,1024]{1,0:T(8,128)(2,1)S(1)} collective-permute-done((bf16[144,1024]{1,0:T(8,128)(2,1)S(1)}, bf16[144,1024]{1,0:T(8,128)(2,1)S(1)}, u32[]{:S(2)}, u32[]{:S(2)}) %collective-permute-start.10) | collective-permute-done | bytes 294944 | tf_op jit(solution)/shard_map/ppermute | solution.py:32
  30.6 0.8 collective-permute-start.12
  31.4 0.5 collective-permute-start.17
  31.9 2.5 %collective-permute-done.1.refs_2_.refs_3_ = bf16[256,256]{1,0:T(8,128)(2,1)S(1)} collective-permute-done((bf16[256,256]{1,0:T(8,128)(2,1)}, bf16[256,256]{1,0:T(8,128)(2,1)S(1)}, u32[]{:S(2)}, u32[]{:S(2)}) %collective-permute-start.1) | collective-permute-done | bytes 131104 | tf_op jit(solution)/shard_map/ppermute | solution.py:22
  34.4 5.4 %collective-permute-done.refs_1_.refs_2_ = bf16[256,256]{1,0:T(8,128)(2,1)S(1)} collective-permute-done((bf16[256,256]{1,0:T(8,128)(2,1)}, bf16[256,256]{1,0:T(8,128)(2,1)S(1)}, u32[]{:S(2)}, u32[]{:S(2)}) %collective-permute-start) | collective-permute-done | bytes 131104 | tf_op jit(solution)/shard_map/ppermute | solution.py:22
  39.8 0.5 collective-permute-start.13
  40.4 0.1 collective-permute-start.15
  40.4 0.4 collective-permute-start.14
  40.9 0.1 collective-permute-start.16
  40.9 0.4 collective-permute-done.19.refs_12_.refs_11_
  41.4 0.9 copy-done.2
  42.3 0.9 copy-done.10
  43.2 1.8 %shard_map.108 = (f32[256,256]{1,0:T(8,128)S(1)}, bf16[256,256]{1,0:T(8,128)(2,1)S(1)}) custom-call(s32[10]{0:T(128)S(1)} %stack.40.ints_ref, f32[32,128]{1,0:T(8,128)S(1)} %get-tuple-element.40.refs_0_, bf16[256,256]{1,0:T(8,128)(2,1)S(1)} %copy-done.10, bf16[256,256]{1,0:T(8,128)(2,1)S(1)} %collective-permute-done.refs_1_.refs_2_, ...), custom_call_target="tpu_custom_call" | custom-call | tf_op jit(solution)/shard_map/pallas_call | solution.py:74
  45.1 0.0 copy-start.19
  45.1 0.0 copy-start.20
  45.1 1.9 %collective-permute-start.22 = (bf16[256,256]{1,0:T(8,128)(2,1)S(1)}, bf16[256,256]{1,0:T(8,128)(2,1)S(1)}, u32[]{:S(2)}, u32[]{:S(2)}) collective-permute-start(bf16[256,256]{1,0:T(8,128)(2,1)S(1)} %get-tuple-element.41.refs_0_), channel_id=1, source_target_pairs={{0,3},{1,2},{2,1},{3,0},{4,7},{5,6},{6,5},{7,4},{8,11},{9,10},{10,... | collective-permute-start | bytes 393224 | tf_op jit(solution)/shard_map/ppermute | solution.py:22
  47.1 2.5 %collective-permute-start.20 = (bf16[256,256]{1,0:T(8,128)(2,1)S(1)}, bf16[256,256]{1,0:T(8,128)(2,1)S(1)}, u32[]{:S(2)}, u32[]{:S(2)}) collective-permute-start(bf16[256,256]{1,0:T(8,128)(2,1)S(1)} %get-tuple-element.41.refs_0_), channel_id=1, source_target_pairs={{0,1},{1,0},{2,3},{3,2},{4,5},{5,4},{6,7},{7,6},{8,9},{9,8},{10,11... | collective-permute-start | bytes 393224 | tf_op jit(solution)/shard_map/ppermute | solution.py:22
  49.6 2.3 %shard_map.106 = (bf16[64,1024]{1,0:T(8,128)(2,1)S(1)}, bf16[64,1024]{1,0:T(8,128)(2,1)S(1)}, bf16[64,1024]{1,0:T(8,128)(2,1)S(1)}, bf16[64,1024]{1,0:T(8,128)(2,1)S(1)}, f32[8,128]{1,0:T(8,128)S(1)}) custom-call(s32[10]{0:T(128)S(1)} %stack.40.ints_ref, bf16[256,256]{1,0:T(8,128)(2,1)S(1)} %copy-done.10, ...), custom_call_target="tpu_custom_call" | custom-call | tf_op jit(solution)/shard_map/pallas_call | solution.py:74
  51.9 0.1 collective-permute-start.23
  52.0 2.4 %collective-permute-start.24 = (bf16[64,1024]{1,0:T(8,128)(2,1)S(1)}, bf16[64,1024]{1,0:T(8,128)(2,1)S(1)}, u32[]{:S(2)}, u32[]{:S(2)}) collective-permute-start(bf16[64,1024]{1,0:T(8,128)(2,1)S(1)} %get-tuple-element.45), channel_id=1, source_target_pairs={{0,2},{1,3},{2,0},{3,1},{4,6},{5,7},{6,4},{7,5},{8,10},{9,11},{10,... | collective-permute-start | bytes 393224 | tf_op jit(solution)/shard_map/ppermute | solution.py:22
  54.4 2.0 %collective-permute-start.25 = (bf16[64,1024]{1,0:T(8,128)(2,1)S(1)}, bf16[64,1024]{1,0:T(8,128)(2,1)S(1)}, u32[]{:S(2)}, u32[]{:S(2)}) collective-permute-start(bf16[64,1024]{1,0:T(8,128)(2,1)S(1)} %get-tuple-element.46), channel_id=1, source_target_pairs={{0,3},{1,2},{2,1},{3,0},{4,7},{5,6},{6,5},{7,4},{8,11},{9,10},{10,... | collective-permute-start | bytes 393224 | tf_op jit(solution)/shard_map/ppermute | solution.py:22
  56.4 2.6 %shard_map.107 = (bf16[8,256,512]{2,1,0:T(8,128)(2,1)S(1)}, bf16[8,256,512]{2,1,0:T(8,128)(2,1)S(1)}, f32[256,256]{1,0:T(8,128)S(1)}) custom-call(s32[10]{0:T(128)S(1)} %stack.40.ints_ref, s32[1,4096]{1,0:T(1,128)S(1)} %bitcast.17, s32[1,4096]{1,0:T(1,128)S(1)} %bitcast.18, f32[1,4096]{1,0:T(1,128)S(1)} %bitcast.19), custom_call_target="tpu_custom_call" | custom-call | tf_op jit(solution)/shard_map/pallas_call | solution.py:74
  59.0 0.5 collective-permute-done.21.refs_2_
  59.6 1.1 %copy-done.5 = bf16[4,256,128]{2,1,0:T(8,128)(2,1)S(1)} copy-done((bf16[4,256,128]{2,1,0:T(8,128)(2,1)S(1)}, bf16[4,256,128]{2,1,0:T(8,128)(2,1)}, u32[]{:S(2)}) %copy-start.5) | copy-done | bytes 262168
  60.7 0.9 copy-done.7
  61.7 1.8 %shard_map.110.refs_4_ = f32[4,256,256]{2,1,0:T(8,128)S(1)} custom-call(s32[10]{0:T(128)S(1)} %stack.40.ints_ref, bf16[256,256]{1,0:T(8,128)(2,1)S(1)} %get-tuple-element.41.refs_0_, bf16[256,256]{1,0:T(8,128)(2,1)S(1)} %collective-permute-done.20.refs_1_, bf16[256,256]{1,0:T(8,128)(2,1)S(1)} %collective-permute-done.21.refs_2_, ...), custom_call_target="tpu_custom_call" | custom-call | tf_op jit(solution)/shard_map/pallas_call | solution.py:74
  63.5 0.0 copy-start.12
  63.6 2.8 %shard_map.109 = (bf16[64,1024]{1,0:T(8,128)(2,1)S(1)}, bf16[64,1024]{1,0:T(8,128)(2,1)S(1)}, bf16[64,1024]{1,0:T(8,128)(2,1)S(1)}, bf16[64,1024]{1,0:T(8,128)(2,1)S(1)}, f32[8,128]{1,0:T(8,128)}) custom-call(s32[10]{0:T(128)S(1)} %stack.40.ints_ref, bf16[256,256]{1,0:T(8,128)(2,1)S(1)} %get-tuple-element.41.refs_0_, ...), custom_call_target="tpu_custom_call" | custom-call | tf_op jit(solution)/shard_map/pallas_call | solution.py:74
  66.4 0.7 copy-done.16
  67.1 0.9 collective-permute-done.24.refs_9_
  68.0 4.2 %shard_map.111 = (f32[64,256]{1,0:T(8,128)S(1)}, f32[256,128]{1,0:T(8,128)}) custom-call(s32[10]{0:T(128)S(1)} %stack.40.ints_ref, f32[64,256]{1,0:T(8,128)S(1)} %copy-done.12, f32[8,128]{1,0:T(8,128)S(1)} %get-tuple-element.35.refs_1_, s32[1,64]{1,0:T(1,128)S(1)} %bitcast.21, s32[1,256]{1,0:T(1,128)S(1)} %bitcast.24, ...), custom_call_target="tpu_custom_call" | custom-call | tf_op jit(solution)/shard_map/pallas_call | solution.py:74
  72.1 5.6 %all-to-all-start = ((f32[32,8,128]{2,1,0:T(8,128)}), f32[32,8,128]{2,1,0:T(8,128)S(1)}, u32[]{:S(2)}, u32[]{:S(2)}) async-start(f32[32,8,128]{2,1,0:T(8,128)} %bitcast.14), calls=%async_computation | async-start | bytes 262144 | tf_op jit(solution)/shard_map/all_to_all | solution.py:415
  77.7 1.7 %collective-permute-start.26 = (bf16[64,1024]{1,0:T(8,128)(2,1)}, bf16[64,1024]{1,0:T(8,128)(2,1)S(1)}, u32[]{:S(2)}, u32[]{:S(2)}) collective-permute-start(bf16[64,1024]{1,0:T(8,128)(2,1)} %copy-done.26), channel_id=1, source_target_pairs={{0,1},{1,0},{2,3},{3,2},{4,5},{5,4},{6,7},{7,6},{8,9},{9,8},{10,11... | collective-permute-start | bytes 393224 | tf_op jit(solution)/shard_map/ppermute | solution.py:22
  79.4 2.4 %collective-permute-start.27 = (bf16[64,1024]{1,0:T(8,128)(2,1)}, bf16[64,1024]{1,0:T(8,128)(2,1)S(1)}, u32[]{:S(2)}, u32[]{:S(2)}) collective-permute-start(bf16[64,1024]{1,0:T(8,128)(2,1)} %copy-done.25), channel_id=1, source_target_pairs={{0,2},{1,3},{2,0},{3,1},{4,6},{5,7},{6,4},{7,5},{8,10},{9,11},{10,... | collective-permute-start | bytes 393224 | tf_op jit(solution)/shard_map/ppermute | solution.py:22
  81.8 0.4 collective-permute-start.28
  82.2 6.0 %collective-permute-done.26.refs_5_ = bf16[64,1024]{1,0:T(8,128)(2,1)S(1)} collective-permute-done((bf16[64,1024]{1,0:T(8,128)(2,1)}, bf16[64,1024]{1,0:T(8,128)(2,1)S(1)}, u32[]{:S(2)}, u32[]{:S(2)}) %collective-permute-start.26) | collective-permute-done | bytes 131104 | tf_op jit(solution)/shard_map/ppermute | solution.py:22
  88.2 4.8 %collective-permute-done.28.refs_7_ = bf16[64,1024]{1,0:T(8,128)(2,1)S(1)} collective-permute-done((bf16[64,1024]{1,0:T(8,128)(2,1)S(1)}, bf16[64,1024]{1,0:T(8,128)(2,1)S(1)}, u32[]{:S(2)}, u32[]{:S(2)}) %collective-permute-start.28) | collective-permute-done | bytes 131104 | tf_op jit(solution)/shard_map/ppermute | solution.py:22
  92.9 1.6 %copy-done.1 = bf16[8,256,512]{2,1,0:T(8,128)(2,1)S(1)} copy-done((bf16[8,256,512]{2,1,0:T(8,128)(2,1)S(1)}, bf16[8,256,512]{2,1,0:T(8,128)(2,1)}, u32[]{:S(2)}) %copy-start.1) | copy-done | bytes 2097176
  94.5 0.9 copy-done.9
  95.5 0.9 copy-done.17
  96.4 3.7 %shard_map.112.refs_2_ = f32[3,64,256]{2,1,0:T(8,128)S(1)} custom-call(s32[10]{0:T(128)S(1)} %stack.40.ints_ref, f32[64,256]{1,0:T(8,128)S(1)} %get-tuple-element.48.refs_0_, bf16[8,256,512]{2,1,0:T(8,128)(2,1)S(1)} %get-tuple-element.36.refs_4_.refs_1_, bf16[8,256,512]{2,1,0:T(8,128)(2,1)S(1)} %copy-done.1, f32[256,256]{1,0:T(8,128)S(1)} %copy-done.9, ...), custom_call_target="tpu_custom_call" | custom-call | tf_op jit(solution)/shard_map/pallas_call | solution.py:74
  100.1 0.9 copy-done.15
  101.1 1.7 %shard_map.113 = (f32[256,256]{1,0:T(8,128)}, f32[64,256]{1,0:T(8,128)}) custom-call(s32[10]{0:T(128)S(1)} %stack.40.ints_ref, f32[256,128]{1,0:T(8,128)S(1)} %bitcast.16, s32[1,64]{1,0:T(1,128)S(1)} %bitcast.22, f32[3,64,256]{2,1,0:T(8,128)S(1)} %shard_map.112.refs_2_, f32[256,256]{1,0:T(8,128)S(1)} %copy-done.15, f32[4,256,256]{2,1,0:T(8,128)S(1)} %shard_map.110.refs_4_), custom_call_target="tpu_custom_call" | custom-call | tf_op jit(solution)/shard_map/pallas_call | solution.py:74
  (61 shorter events, 0.1 us)
Async XLA Ops:
  0.6 17.3 %collective-permute-start.6 = (bf16[4,256,128]{2,1,0:T(8,128)(2,1)}, bf16[4,256,128]{2,1,0:T(8,128)(2,1)S(1)}, u32[]{:S(2)}, u32[]{:S(2)}) collective-permute-start(bf16[4,256,128]{2,1,0:T(8,128)(2,1)} %refs_4_.1), channel_id=1, source_target_pairs={{0,4},{4,0},{8,12},{12,8},{16,20},{20,16},{24,28},{28,24},{1,5},{5... | collective-permute-start | bytes 786440 | tf_op jit(solution)/shard_map/ppermute | solution.py:22
  1.1 16.8 %collective-permute-start.5 = (bf16[4,256,128]{2,1,0:T(8,128)(2,1)}, bf16[4,256,128]{2,1,0:T(8,128)(2,1)S(1)}, u32[]{:S(2)}, u32[]{:S(2)}) collective-permute-start(bf16[4,256,128]{2,1,0:T(8,128)(2,1)} %refs_4_.1), channel_id=1, source_target_pairs={{0,16},{4,12},{8,24},{12,4},{16,0},{20,28},{24,8},{28,20},{1,17},{... | collective-permute-start | bytes 786440 | tf_op jit(solution)/shard_map/ppermute | solution.py:32
  3.7 14.2 %collective-permute-start.4 = (bf16[4,256,128]{2,1,0:T(8,128)(2,1)}, bf16[4,256,128]{2,1,0:T(8,128)(2,1)S(1)}, u32[]{:S(2)}, u32[]{:S(2)}) collective-permute-start(bf16[4,256,128]{2,1,0:T(8,128)(2,1)} %refs_4_.1), channel_id=1, source_target_pairs={{0,8},{4,20},{8,0},{12,28},{16,24},{20,4},{24,16},{28,12},{1,9},{5... | collective-permute-start | bytes 786440 | tf_op jit(solution)/shard_map/ppermute | solution.py:32
  5.3 0.8 copy-start.11
  6.2 0.9 copy-start.13
  7.1 0.7 copy-start.21
  7.8 0.7 copy-start.23
  9.2 4.4 %collective-permute-start.3 = (bf16[144,256]{1,0:T(8,128)(2,1)S(1)}, bf16[144,256]{1,0:T(8,128)(2,1)S(1)}, u32[]{:S(2)}, u32[]{:S(2)}) collective-permute-start(bf16[144,256]{1,0:T(8,128)(2,1)S(1)} %get-tuple-element.29), channel_id=1, source_target_pairs={{0,1},{1,0},{2,3},{3,2},{4,5},{5,4},{6,7},{7,6},{8,9},{9,8},{10,11... | collective-permute-start | bytes 221192 | tf_op jit(solution)/shard_map/ppermute | solution.py:22
  10.8 7.5 %collective-permute-start.7 = (bf16[144,256]{1,0:T(8,128)(2,1)S(1)}, bf16[144,256]{1,0:T(8,128)(2,1)S(1)}, u32[]{:S(2)}, u32[]{:S(2)}) collective-permute-start(bf16[144,256]{1,0:T(8,128)(2,1)S(1)} %get-tuple-element.31), channel_id=1, source_target_pairs={{0,2},{1,3},{2,0},{3,1},{4,6},{5,7},{6,4},{7,5},{8,10},{9,11},{10,... | collective-permute-start | bytes 221192 | tf_op jit(solution)/shard_map/ppermute | solution.py:22
  13.6 6.7 %collective-permute-start.8 = (bf16[144,256]{1,0:T(8,128)(2,1)S(1)}, bf16[144,256]{1,0:T(8,128)(2,1)S(1)}, u32[]{:S(2)}, u32[]{:S(2)}) collective-permute-start(bf16[144,256]{1,0:T(8,128)(2,1)S(1)} %get-tuple-element.32), channel_id=1, source_target_pairs={{0,3},{1,2},{2,1},{3,0},{4,7},{5,6},{6,5},{7,4},{8,11},{9,10},{10,... | collective-permute-start | bytes 221192 | tf_op jit(solution)/shard_map/ppermute | solution.py:22
  18.0 33.9 %copy-start.4 = (bf16[4,256,128]{2,1,0:T(8,128)(2,1)}, bf16[4,256,128]{2,1,0:T(8,128)(2,1)S(1)}, u32[]{:S(2)}) copy-start(bf16[4,256,128]{2,1,0:T(8,128)(2,1)S(1)} %collective-permute-done.5.refs_7_.refs_6_) | copy-start | bytes 786436
  18.0 33.9 %copy-start.6 = (bf16[4,256,128]{2,1,0:T(8,128)(2,1)}, bf16[4,256,128]{2,1,0:T(8,128)(2,1)S(1)}, u32[]{:S(2)}) copy-start(bf16[4,256,128]{2,1,0:T(8,128)(2,1)S(1)} %collective-permute-done.4.refs_6_.refs_5_) | copy-start | bytes 786436
  20.9 9.8 %collective-permute-start.10 = (bf16[144,1024]{1,0:T(8,128)(2,1)S(1)}, bf16[144,1024]{1,0:T(8,128)(2,1)S(1)}, u32[]{:S(2)}, u32[]{:S(2)}) collective-permute-start(bf16[144,1024]{1,0:T(8,128)(2,1)S(1)} %get-tuple-element.33.refs_4_), channel_id=1, source_target_pairs={{0,16},{4,12},{8,24},{12,4},{16,0},{20,28},{24,8},{28,20},{1,17},{... | collective-permute-start | bytes 884744 | tf_op jit(solution)/shard_map/ppermute | solution.py:32
  21.4 6.4 %collective-permute-start.11 = (bf16[4,256,128]{2,1,0:T(8,128)(2,1)S(1)}, bf16[4,256,128]{2,1,0:T(8,128)(2,1)S(1)}, u32[]{:S(2)}, u32[]{:S(2)}) collective-permute-start(bf16[4,256,128]{2,1,0:T(8,128)(2,1)S(1)} %collective-permute-done.5.refs_7_.refs_6_), channel_id=1, source_target_pairs={{0,8},{4,20},{8,0},{12,28},{16,24},{20,4},{24,16},{28,12},{1,9},{5... | collective-permute-start | bytes 786440 | tf_op jit(solution)/shard_map/ppermute | solution.py:32
  22.0 9.4 %collective-permute-start.2 = (bf16[256,256]{1,0:T(8,128)(2,1)}, bf16[256,256]{1,0:T(8,128)(2,1)S(1)}, u32[]{:S(2)}, u32[]{:S(2)}) collective-permute-start(bf16[256,256]{1,0:T(8,128)(2,1)} %refs_1_.3), channel_id=1, source_target_pairs={{0,3},{1,2},{2,1},{3,0},{4,7},{5,6},{6,5},{7,4},{8,11},{9,10},{10,... | collective-permute-start | bytes 393224 | tf_op jit(solution)/shard_map/ppermute | solution.py:22
  25.8 8.6 %collective-permute-start.1 = (bf16[256,256]{1,0:T(8,128)(2,1)}, bf16[256,256]{1,0:T(8,128)(2,1)S(1)}, u32[]{:S(2)}, u32[]{:S(2)}) collective-permute-start(bf16[256,256]{1,0:T(8,128)(2,1)} %refs_1_.3), channel_id=1, source_target_pairs={{0,2},{1,3},{2,0},{3,1},{4,6},{5,7},{6,4},{7,5},{8,10},{9,11},{10,... | collective-permute-start | bytes 393224 | tf_op jit(solution)/shard_map/ppermute | solution.py:22
  25.8 14.6 %collective-permute-start.9 = (bf16[144,1024]{1,0:T(8,128)(2,1)S(1)}, bf16[144,1024]{1,0:T(8,128)(2,1)S(1)}, u32[]{:S(2)}, u32[]{:S(2)}) collective-permute-start(bf16[144,1024]{1,0:T(8,128)(2,1)S(1)} %get-tuple-element.33.refs_4_), channel_id=1, source_target_pairs={{0,8},{4,20},{8,0},{12,28},{16,24},{20,4},{24,16},{28,12},{1,9},{5... | collective-permute-start | bytes 884744 | tf_op jit(solution)/shard_map/ppermute | solution.py:32
  30.6 10.2 %collective-permute-start.12 = (bf16[144,1024]{1,0:T(8,128)(2,1)S(1)}, bf16[144,1024]{1,0:T(8,128)(2,1)S(1)}, u32[]{:S(2)}, u32[]{:S(2)}) collective-permute-start(bf16[144,1024]{1,0:T(8,128)(2,1)S(1)} %collective-permute-done.10.refs_6_), channel_id=1, source_target_pairs={{0,8},{4,20},{8,0},{12,28},{16,24},{20,4},{24,16},{28,12},{1,9},{5... | collective-permute-start | bytes 884744 | tf_op jit(solution)/shard_map/ppermute | solution.py:32
  31.4 8.4 %collective-permute-start.18 = (bf16[4,256,128]{2,1,0:T(8,128)(2,1)S(1)}, bf16[4,256,128]{2,1,0:T(8,128)(2,1)S(1)}, u32[]{:S(2)}, u32[]{:S(2)}) collective-permute-start(bf16[4,256,128]{2,1,0:T(8,128)(2,1)S(1)} %collective-permute-done.5.refs_7_.refs_6_), channel_id=1, source_target_pairs={{0,4},{4,0},{8,12},{12,8},{16,20},{20,16},{24,28},{28,24},{1,5},{5... | collective-permute-start | bytes 786440 | tf_op jit(solution)/shard_map/ppermute | solution.py:22
  31.4 8.9 %collective-permute-start.17 = (bf16[4,256,128]{2,1,0:T(8,128)(2,1)S(1)}, bf16[4,256,128]{2,1,0:T(8,128)(2,1)S(1)}, u32[]{:S(2)}, u32[]{:S(2)}) collective-permute-start(bf16[4,256,128]{2,1,0:T(8,128)(2,1)S(1)} %collective-permute-done.4.refs_6_.refs_5_), channel_id=1, source_target_pairs={{0,4},{4,0},{8,12},{12,8},{16,20},{20,16},{24,28},{28,24},{1,5},{5... | collective-permute-start | bytes 786440 | tf_op jit(solution)/shard_map/ppermute | solution.py:22
  34.4 5.4 %collective-permute-start = (bf16[256,256]{1,0:T(8,128)(2,1)}, bf16[256,256]{1,0:T(8,128)(2,1)S(1)}, u32[]{:S(2)}, u32[]{:S(2)}) collective-permute-start(bf16[256,256]{1,0:T(8,128)(2,1)} %refs_1_.3), channel_id=1, source_target_pairs={{0,1},{1,0},{2,3},{3,2},{4,5},{5,4},{6,7},{7,6},{8,9},{9,8},{10,11... | collective-permute-start | bytes 393224 | tf_op jit(solution)/shard_map/ppermute | solution.py:22
  39.8 1.5 %collective-permute-start.19 = (bf16[4,256,128]{2,1,0:T(8,128)(2,1)S(1)}, bf16[4,256,128]{2,1,0:T(8,128)(2,1)S(1)}, u32[]{:S(2)}, u32[]{:S(2)}) collective-permute-start(bf16[4,256,128]{2,1,0:T(8,128)(2,1)S(1)} %collective-permute-done.11.refs_8_.refs_7_), channel_id=1, source_target_pairs={{0,4},{4,0},{8,12},{12,8},{16,20},{20,16},{24,28},{28,24},{1,5},{5... | collective-permute-start | bytes 786440 | tf_op jit(solution)/shard_map/ppermute | solution.py:22
  39.8 7.2 %collective-permute-start.13 = (bf16[144,1024]{1,0:T(8,128)(2,1)S(1)}, bf16[144,1024]{1,0:T(8,128)(2,1)S(1)}, u32[]{:S(2)}, u32[]{:S(2)}) collective-permute-start(bf16[144,1024]{1,0:T(8,128)(2,1)S(1)} %get-tuple-element.33.refs_4_), channel_id=1, source_target_pairs={{0,4},{4,0},{8,12},{12,8},{16,20},{20,16},{24,28},{28,24},{1,5},{5... | collective-permute-start | bytes 884744 | tf_op jit(solution)/shard_map/ppermute | solution.py:22
  40.4 6.7 %collective-permute-start.15 = (bf16[144,1024]{1,0:T(8,128)(2,1)S(1)}, bf16[144,1024]{1,0:T(8,128)(2,1)S(1)}, u32[]{:S(2)}, u32[]{:S(2)}) collective-permute-start(bf16[144,1024]{1,0:T(8,128)(2,1)S(1)} %collective-permute-done.10.refs_6_), channel_id=1, source_target_pairs={{0,4},{4,0},{8,12},{12,8},{16,20},{20,16},{24,28},{28,24},{1,5},{5... | collective-permute-start | bytes 884744 | tf_op jit(solution)/shard_map/ppermute | solution.py:22
  40.4 9.2 %collective-permute-start.14 = (bf16[144,1024]{1,0:T(8,128)(2,1)S(1)}, bf16[144,1024]{1,0:T(8,128)(2,1)S(1)}, u32[]{:S(2)}, u32[]{:S(2)}) collective-permute-start(bf16[144,1024]{1,0:T(8,128)(2,1)S(1)} %collective-permute-done.9.refs_5_), channel_id=1, source_target_pairs={{0,4},{4,0},{8,12},{12,8},{16,20},{20,16},{24,28},{28,24},{1,5},{5... | collective-permute-start | bytes 884744 | tf_op jit(solution)/shard_map/ppermute | solution.py:22
  40.9 8.7 %collective-permute-start.16 = (bf16[144,1024]{1,0:T(8,128)(2,1)S(1)}, bf16[144,1024]{1,0:T(8,128)(2,1)S(1)}, u32[]{:S(2)}, u32[]{:S(2)}) collective-permute-start(bf16[144,1024]{1,0:T(8,128)(2,1)S(1)} %collective-permute-done.12.refs_7_), channel_id=1, source_target_pairs={{0,4},{4,0},{8,12},{12,8},{16,20},{20,16},{24,28},{28,24},{1,5},{5... | collective-permute-start | bytes 884744 | tf_op jit(solution)/shard_map/ppermute | solution.py:22
  41.4 1.0 copy-start.2
  42.3 0.9 copy-start.10
  45.1 18.4 %copy-start.14 = (f32[256,256]{1,0:T(8,128)}, f32[256,256]{1,0:T(8,128)S(1)}, u32[]{:S(2)}) copy-start(f32[256,256]{1,0:T(8,128)S(1)} %get-tuple-element.53.refs_3_) | copy-start | bytes 786436
  45.1 11.3 %copy-start.18 = (s32[4096]{0:T(1024)S(1)}, s32[4096]{0:T(1024)}, u32[]{:S(2)}) copy-start(s32[4096]{0:T(1024)} %param.15) | copy-start | bytes 49156
  45.1 11.3 %copy-start.19 = (s32[4096]{0:T(1024)S(1)}, s32[4096]{0:T(1024)}, u32[]{:S(2)}) copy-start(s32[4096]{0:T(1024)} %param.16) | copy-start | bytes 49156
  45.1 11.3 %copy-start.20 = (f32[4096]{0:T(1024)S(1)}, f32[4096]{0:T(1024)}, u32[]{:S(2)}) copy-start(f32[4096]{0:T(1024)} %param.17) | copy-start | bytes 49156
  45.1 14.4 %copy-start.3 = (bf16[4,256,128]{2,1,0:T(8,128)(2,1)S(1)}, bf16[4,256,128]{2,1,0:T(8,128)(2,1)}, u32[]{:S(2)}) copy-start(bf16[4,256,128]{2,1,0:T(8,128)(2,1)} %refs_4_.1) | copy-start | bytes 786436
  45.1 9.2 %collective-permute-start.22 = (bf16[256,256]{1,0:T(8,128)(2,1)S(1)}, bf16[256,256]{1,0:T(8,128)(2,1)S(1)}, u32[]{:S(2)}, u32[]{:S(2)}) collective-permute-start(bf16[256,256]{1,0:T(8,128)(2,1)S(1)} %get-tuple-element.41.refs_0_), channel_id=1, source_target_pairs={{0,3},{1,2},{2,1},{3,0},{4,7},{5,6},{6,5},{7,4},{8,11},{9,10},{10,... | collective-permute-start | bytes 393224 | tf_op jit(solution)/shard_map/ppermute | solution.py:22
  47.1 12.5 %collective-permute-start.21 = (bf16[256,256]{1,0:T(8,128)(2,1)S(1)}, bf16[256,256]{1,0:T(8,128)(2,1)S(1)}, u32[]{:S(2)}, u32[]{:S(2)}) collective-permute-start(bf16[256,256]{1,0:T(8,128)(2,1)S(1)} %get-tuple-element.41.refs_0_), channel_id=1, source_target_pairs={{0,2},{1,3},{2,0},{3,1},{4,6},{5,7},{6,4},{7,5},{8,10},{9,11},{10,... | collective-permute-start | bytes 393224 | tf_op jit(solution)/shard_map/ppermute | solution.py:22
  47.1 12.5 %collective-permute-start.20 = (bf16[256,256]{1,0:T(8,128)(2,1)S(1)}, bf16[256,256]{1,0:T(8,128)(2,1)S(1)}, u32[]{:S(2)}, u32[]{:S(2)}) collective-permute-start(bf16[256,256]{1,0:T(8,128)(2,1)S(1)} %get-tuple-element.41.refs_0_), channel_id=1, source_target_pairs={{0,1},{1,0},{2,3},{3,2},{4,5},{5,4},{6,7},{7,6},{8,9},{9,8},{10,11... | collective-permute-start | bytes 393224 | tf_op jit(solution)/shard_map/ppermute | solution.py:22
  51.9 15.1 %collective-permute-start.23 = (bf16[64,1024]{1,0:T(8,128)(2,1)S(1)}, bf16[64,1024]{1,0:T(8,128)(2,1)S(1)}, u32[]{:S(2)}, u32[]{:S(2)}) collective-permute-start(bf16[64,1024]{1,0:T(8,128)(2,1)S(1)} %get-tuple-element.44), channel_id=1, source_target_pairs={{0,1},{1,0},{2,3},{3,2},{4,5},{5,4},{6,7},{7,6},{8,9},{9,8},{10,11... | collective-permute-start | bytes 393224 | tf_op jit(solution)/shard_map/ppermute | solution.py:22
  52.0 15.9 %collective-permute-start.24 = (bf16[64,1024]{1,0:T(8,128)(2,1)S(1)}, bf16[64,1024]{1,0:T(8,128)(2,1)S(1)}, u32[]{:S(2)}, u32[]{:S(2)}) collective-permute-start(bf16[64,1024]{1,0:T(8,128)(2,1)S(1)} %get-tuple-element.45), channel_id=1, source_target_pairs={{0,2},{1,3},{2,0},{3,1},{4,6},{5,7},{6,4},{7,5},{8,10},{9,11},{10,... | collective-permute-start | bytes 393224 | tf_op jit(solution)/shard_map/ppermute | solution.py:22
  54.4 13.5 %collective-permute-start.25 = (bf16[64,1024]{1,0:T(8,128)(2,1)S(1)}, bf16[64,1024]{1,0:T(8,128)(2,1)S(1)}, u32[]{:S(2)}, u32[]{:S(2)}) collective-permute-start(bf16[64,1024]{1,0:T(8,128)(2,1)S(1)} %get-tuple-element.46), channel_id=1, source_target_pairs={{0,3},{1,2},{2,1},{3,0},{4,7},{5,6},{6,5},{7,4},{8,11},{9,10},{10,... | collective-permute-start | bytes 393224 | tf_op jit(solution)/shard_map/ppermute | solution.py:22
  59.0 8.9 %copy-start = (bf16[8,256,512]{2,1,0:T(8,128)(2,1)}, bf16[8,256,512]{2,1,0:T(8,128)(2,1)S(1)}, u32[]{:S(2)}) copy-start(bf16[8,256,512]{2,1,0:T(8,128)(2,1)S(1)} %get-tuple-element.37.refs_5_.refs_2_) | copy-start | bytes 6291460
  59.0 8.9 %copy-start.8 = (f32[256,256]{1,0:T(8,128)}, f32[256,256]{1,0:T(8,128)S(1)}, u32[]{:S(2)}) copy-start(f32[256,256]{1,0:T(8,128)S(1)} %get-tuple-element.38.refs_6_.refs_3_) | copy-start | bytes 786436
  59.6 1.1 %copy-start.5 = (bf16[4,256,128]{2,1,0:T(8,128)(2,1)S(1)}, bf16[4,256,128]{2,1,0:T(8,128)(2,1)}, u32[]{:S(2)}) copy-start(bf16[4,256,128]{2,1,0:T(8,128)(2,1)} %copy-done.4) | copy-start | bytes 786436
  60.7 0.9 copy-start.7
  63.5 4.4 %copy-start.12 = (f32[64,256]{1,0:T(8,128)S(1)}, f32[64,256]{1,0:T(8,128)}, u32[]{:S(2)}) copy-start(f32[64,256]{1,0:T(8,128)} %refs_0_.5) | copy-start | bytes 196612
  63.5 4.4 %copy-start.22 = (s32[64,1]{0,1:T(1,128)S(1)}, s32[64,1]{0,1:T(1,128)}, u32[]{:S(2)}) copy-start(s32[64,1]{0,1:T(1,128)} %param.13) | copy-start | bytes 772
  63.5 4.4 %copy-start.24 = (s32[256,1]{0,1:T(1,128)S(1)}, s32[256,1]{0,1:T(1,128)}, u32[]{:S(2)}) copy-start(s32[256,1]{0,1:T(1,128)} %param.14) | copy-start | bytes 3076
  66.4 0.7 copy-start.16
  67.0 5.1 %copy-start.25 = (bf16[64,1024]{1,0:T(8,128)(2,1)}, bf16[64,1024]{1,0:T(8,128)(2,1)S(1)}, u32[]{:S(2)}) copy-start(bf16[64,1024]{1,0:T(8,128)(2,1)S(1)} %get-tuple-element.50) | copy-start | bytes 393220
  67.0 5.1 %copy-start.26 = (bf16[64,1024]{1,0:T(8,128)(2,1)}, bf16[64,1024]{1,0:T(8,128)(2,1)S(1)}, u32[]{:S(2)}) copy-start(bf16[64,1024]{1,0:T(8,128)(2,1)S(1)} %get-tuple-element.49) | copy-start | bytes 393220
  72.1 28.0 %all-to-all-start = ((f32[32,8,128]{2,1,0:T(8,128)}), f32[32,8,128]{2,1,0:T(8,128)S(1)}, u32[]{:S(2)}, u32[]{:S(2)}) async-start(f32[32,8,128]{2,1,0:T(8,128)} %bitcast.14), calls=%async_computation | async-start | bytes 262144 | tf_op jit(solution)/shard_map/all_to_all | solution.py:415
  77.7 10.4 %collective-permute-start.26 = (bf16[64,1024]{1,0:T(8,128)(2,1)}, bf16[64,1024]{1,0:T(8,128)(2,1)S(1)}, u32[]{:S(2)}, u32[]{:S(2)}) collective-permute-start(bf16[64,1024]{1,0:T(8,128)(2,1)} %copy-done.26), channel_id=1, source_target_pairs={{0,1},{1,0},{2,3},{3,2},{4,5},{5,4},{6,7},{7,6},{8,9},{9,8},{10,11... | collective-permute-start | bytes 393224 | tf_op jit(solution)/shard_map/ppermute | solution.py:22
  79.4 8.7 %collective-permute-start.27 = (bf16[64,1024]{1,0:T(8,128)(2,1)}, bf16[64,1024]{1,0:T(8,128)(2,1)S(1)}, u32[]{:S(2)}, u32[]{:S(2)}) collective-permute-start(bf16[64,1024]{1,0:T(8,128)(2,1)} %copy-done.25), channel_id=1, source_target_pairs={{0,2},{1,3},{2,0},{3,1},{4,6},{5,7},{6,4},{7,5},{8,10},{9,11},{10,... | collective-permute-start | bytes 393224 | tf_op jit(solution)/shard_map/ppermute | solution.py:22
  81.8 11.1 %collective-permute-start.28 = (bf16[64,1024]{1,0:T(8,128)(2,1)S(1)}, bf16[64,1024]{1,0:T(8,128)(2,1)S(1)}, u32[]{:S(2)}, u32[]{:S(2)}) collective-permute-start(bf16[64,1024]{1,0:T(8,128)(2,1)S(1)} %get-tuple-element.51), channel_id=1, source_target_pairs={{0,3},{1,2},{2,1},{3,0},{4,7},{5,6},{6,5},{7,4},{8,11},{9,10},{10,... | collective-permute-start | bytes 393224 | tf_op jit(solution)/shard_map/ppermute | solution.py:22
  92.9 1.6 %copy-start.1 = (bf16[8,256,512]{2,1,0:T(8,128)(2,1)S(1)}, bf16[8,256,512]{2,1,0:T(8,128)(2,1)}, u32[]{:S(2)}) copy-start(bf16[8,256,512]{2,1,0:T(8,128)(2,1)} %copy-done) | copy-start | bytes 6291460
  94.5 0.9 copy-start.9
  95.5 0.9 copy-start.17
  100.1 1.0 copy-start.15

commit v3 on v2

--- a/solution.py
+++ b/solution.py
@@ -27,16 +27,16 @@
     return [x] + [got[mask] for mask in range(1, ne)]
 
 
-def cross(x, first):
-    masks = (2, 4) if first else (4, 2)
-    return lax.ppermute(x, "cells", [(i, i ^ masks[i & 1]) for i in range(8)])
+def chips(x):
+    return [x] + [swap(x, "cells", mask, 8) for mask in (6, 2, 4)]
+
+
+def siblings(own):
+    return own + [swap(v, "cells", 1, 8) for v in own]
 
 
 def gathered_places(i):
-    first = jnp.where((i & 1) == 0, 2, 4)
-    own = [i, i ^ first, i ^ (6 - first), i ^ 6]
-    sibling = [i ^ 1, i ^ 1 ^ (6 - first), i ^ 1 ^ first, i ^ 7]
-    return own + sibling
+    return [i ^ mask for mask in (0, 6, 2, 4, 1, 7, 3, 5)]
 
 
 def aligned(index, size):
@@ -109,16 +109,18 @@
 
 
 def message_kernel(ints_ref, args, outs, scratch):
-    section_ref, level_ref, partner_ref, owner_ref = args
+    spectra_ref, section_ref, level_ref, partner_ref, owner_ref = args
+    block = spectra_ref.shape[0]
     k = ints_ref[0]
     news = halves(news_of(level_ref[...], zones_of(owner_ref), partner_ref))
-    part = outs[0].shape[0] - 2 * TILE
+    part = outs[0].shape[0] - 2 * TILE - block
     width = outs[0].shape[1]
     if width > LANES:
         news = jnp.concatenate([news, jnp.zeros((2 * TILE, width - LANES), BF)], 1)
     for mask, out in enumerate(outs):
-        out[:part, :] = section_ref[aligned(k ^ mask, part), :]
-        out[part:, :] = news
+        out[:block, :] = spectra_ref[...]
+        out[block : block + part, :] = section_ref[aligned(k ^ mask, part), :]
+        out[block + part :, :] = news
 
 
 def pack_kernel(ints_ref, args, outs, scratch):
@@ -127,8 +129,9 @@
     part = packed_ref.shape[0] - 2 * TILE
     total = None
     for mask, ref in enumerate(args):
-        packed_ref[:part, aligned(k ^ mask, ref.shape[1])] = ref[:part, :]
-        news = fold(ref[part:, :LANES].astype(F32))
+        below = ref.shape[0] - 2 * TILE
+        packed_ref[:part, aligned(k ^ mask, ref.shape[1])] = ref[below - part : below, :]
+        news = fold(ref[below:, :LANES].astype(F32))
         news_ref[aligned(k ^ mask, TILE), :] = news
         total = news if total is None else total + news
     packed_ref[part:, :] = jnp.concatenate(
@@ -214,9 +217,7 @@
             (moved,) = scatter(pairs, ints_ref[0], rates, pick_ref, move_ref, 1)
             levels = levels + level_step * (moved + escape * drained(pairs, drain_ref))
         outs[0][...] = levels
-        news = news_of(levels, zones, partner_ref)
-        for n in range(outs[1].shape[0] // TILE):
-            outs[1][n * TILE : (n + 1) * TILE, :] = news
+        outs[1][...] = news_of(levels, zones, partner_ref)
 
     return kernel
 
@@ -238,11 +239,16 @@
 
 def final_kernel(block, ne, slab):
     def kernel(ints_ref, args, outs, scratch):
-        news_ref, owner_ref, term_ref, current_ref, product_ref = args
-        news = news_ref[...].reshape(news_ref.shape[0] // TILE, TILE, LANES)
-        escape = escape_of(jnp.sum(news, axis=0), zones_of(owner_ref), block)
+        owner_ref, term_ref, current_ref, product_ref, *tiles = args
+        (news_ref,) = scratch
+        for mask, ref in enumerate(tiles[:ne]):
+            news_ref[aligned(ints_ref[0] ^ mask, TILE), :] = ref[...]
+        column = tiles[ne][...]
+        for ref in tiles[ne + 1 :]:
+            column = column + ref[...]
+        escape = escape_of(column, zones_of(owner_ref), block)
         outs[1][...] = term_ref[0] + escape * (term_ref[1] + escape * term_ref[2])
-        density = density_of(news_ref, ints_ref[1] * ne, ne, slab)
+        density = density_of(news_ref, 0, ne, slab)
         summed = density[:, 0:1] * product_ref[0]
         for p in range(1, product_ref.shape[0]):
             summed = summed + density[:, p : p + 1] * product_ref[p]
@@ -253,7 +259,7 @@
 
 def place(ints_ref, parts, row_ref):
     for mask, ref in enumerate(parts):
-        row_ref[:, aligned(ints_ref[0] ^ mask, ref.shape[1])] = ref[...]
+        row_ref[:, aligned(ints_ref[0] ^ mask, ref.shape[1])] = ref[: row_ref.shape[0], :]
 
 
 def product_of(ints_ref, row_ref, parts, p):
@@ -276,7 +282,7 @@
         for p in range(parts[0].shape[0]):
             term = density[:, p : p + 1] * product_of(ints_ref, row_ref, parts, p)
             summed = term if summed is None else summed + term
-        current = spectra[0][...].astype(F32) + boltz_step * summed
+        current = spectra[0][: row_ref.shape[0], :].astype(F32) + boltz_step * summed
         outs[0][...] = current
         outs[1][...] = current.astype(BF)
 
@@ -343,24 +349,20 @@
 
     messages = call(
         message_kernel,
-        [((part + 2 * TILE, width), BF)] * ne,
-        ints,
-        [sections, populations, partner_row, owner_row],
-    )
-    shares = {m: swap(messages[m], "energy", m, ne) for m in range(ne - 1, 0, -1)}
-    spectra = others(distribution, ne)
+        [((block + part + 2 * TILE, width), BF)] * ne,
+        ints,
+        [distribution, sections, populations, partner_row, owner_row],
+    )
+    got = {m: swap(messages[m], "energy", m, ne) for m in range(ne - 1, 0, -1)}
+    spectra = [messages[0]] + [got[m] for m in range(1, ne)]
     packed_shape = [((part + 2 * TILE, ne * width), BF), ((ne * TILE, LANES), F32)]
-    packed_args = [messages[0]] + [shares[m] for m in range(1, ne)]
+    packed_args = list(spectra)
     if small:
-        a, b = cross(operators, True), cross(operators, False)
-        c = cross(b, True)
-        own = swap(operators, "cells", 1, 8)
-        packed_args[1] = after(packed_args[1], a, b, own)
+        operator_parts = chips(operators)
+        packed_args[1] = after(packed_args[1], *operator_parts[1:])
         packed, density = call(pack_kernel, packed_shape, ints, packed_args)
-        operator_parts = [operators, a, b, c, own] + [swap(v, "cells", 1, 8) for v in (a, b, c)]
-        a, b = cross(packed, True), cross(packed, False)
-        c = cross(after(b, operator_parts[3]), True)
-        section_parts = [packed, a, b, c] + [swap(v, "cells", 1, 8) for v in (packed, a, b, c)]
+        operator_parts = siblings(operator_parts)
+        section_parts = chips(packed)
     else:
         packed, density = call(pack_kernel, packed_shape, ints, packed_args)
         operator_parts = [lax.all_gather(operators, "cells", axis=2, tiled=True)]
@@ -376,6 +378,17 @@
     )
 
     row = pltpu.VMEM((block, ne * width), BF)
+
+    current, later = call(
+        first_product_kernel(ne, slab),
+        [((block, outs), F32), ((block, outs), BF)],
+        ints,
+        [density] + spectra + operator_parts,
+        [row],
+    )
+    later = others(later, ne)
+    if small:
+        section_parts = siblings(section_parts[:1] + [after(v, later[1], later[2]) for v in section_parts[1:]])
 
     def rates_of(spectra):
         *rates, column = call(
@@ -388,14 +401,6 @@
         got = {m: swap(rates[m], "energy", m, ne) for m in range(ne - 1, 0, -1)}
         return [rates[0]] + [got[m] for m in range(1, ne)], column
 
-    current, later = call(
-        first_product_kernel(ne, slab),
-        [((block, outs), F32), ((block, outs), BF)],
-        ints,
-        [density] + spectra + operator_parts,
-        [row],
-    )
-    later = others(later, ne)
     rates, column = rates_of(spectra)
     (products,) = call(
         second_product_kernel(ne),
@@ -408,11 +413,17 @@
     rates[0] = after(rates[0], later_rates[0], products)
     levels, news = call(
         first_kernel(block),
-        [(populations.shape, F32), ((nc * ne * TILE, LANES), F32)],
+        [(populations.shape, F32), ((TILE, LANES), F32)],
         ints,
         [populations, column, owner_row, partner_row, pick, move, drain] + rates,
     )
-    news = lax.all_to_all(news, ("cells", "energy"), 0, 0, tiled=True)
+    if small:
+        row_of = lax.broadcasted_iota(jnp.int32, (TILE, LANES), 0)
+        news = after(news, later_rates[1])
+        news = news + jnp.where(row_of == COLUMN_ROW, swap(news, "cells", 1, nc), 0.0)
+    news = others(news, ne)
+    column = sum(news[1:], news[0])
+    columns = chips(column) if small else [lax.psum(column, "cells")]
     (terms,) = call(
         second_kernel,
         [((3,) + populations.shape, F32)],
@@ -423,7 +434,8 @@
         final_kernel(block, ne, slab),
         [((block, outs), F32), (populations.shape, F32)],
         ints,
-        [after(news, terms), owner_row, terms, current, products],
+        [owner_row, terms, current, products] + news + columns,
+        [pltpu.VMEM((ne * TILE, LANES), F32)],
     )
 
 

time: 103 us -> 92.4 us (0.90)
  local copies, waits for them, and re-layouts: 12.3 us -> 5.1 us
  starting transfers between devices: 41 us -> 39 us
    ppermute x23 -> x33, starting transfers between devices: 27.9 us -> 39 us  [swap(): return lax.ppermute(x, axis, [(i, i ^ mask) for i in range(count)])]
    ppermute x6 -> x0, starting transfers between devices: 7.44 us -> none  [cross(): return lax.ppermute(x, 'cells', [(i, i ^ masks[i & 1]) for i in range(8)])]
    unnamed x54 -> x26, local copies, waits for them, and re-layouts: 12.2 us -> 5.01 us
    all_to_all x1 -> x0, starting transfers between devices: 5.61 us -> none  [body(): news = lax.all_to_all(news, ('cells', 'energy'), 0, 0, tiled=True)]
    ppermute x6 -> x0, waiting for transfers between devices: 3.36 us -> none  [cross(): return lax.ppermute(x, 'cells', [(i, i ^ masks[i & 1]) for i in range(8)])]
    ppermute x23 -> x33, waiting for transfers between devices: 23 us -> 25.6 us  [swap(): return lax.ppermute(x, axis, [(i, i ^ mask) for i in range(count)])]
  transfers between devices with their start and end apart: 30 -> 33, of which waited for: 12 -> 11; matrix products, arithmetic and copies ran while one was open for 0% -> 0% of each run, Pallas kernels for 15% -> 22%
where the time goes in v3:
time: 92.4 us; the launch traced here: 92.2 us
  starting transfers between devices  39 us (42%)
  waiting for transfers between devices  25.6 us (28%)
  Pallas kernels  21.5 us (23%)
  local copies, waits for them, and re-layouts  5.1 us (6%)
    ppermute x33, starting transfers between devices, swap(): return lax.ppermute(x, axis, [(i, i ^ mask) for i in range(count)])  39 us
    ppermute x33, waiting for transfers between devices, swap(): return lax.ppermute(x, axis, [(i, i ^ mask) for i in range(count)])  25.6 us
    pallas_call x10, Pallas kernels, call(): pl.pallas_call(whole, out_shape=tuple((jax.ShapeDtypeStruct(s, t) for s,...  21.5 us
    unnamed x26, local copies, waits for them, and re-layouts  5.01 us
  transfers between devices with their start and end apart: 33, of which 11 were waited for; matrix products, arithmetic and copies ran while one was open for 0% of the time, Pallas kernels for 22%

profile of v3, /device:TPU:0, one launch (start us, length us, event | category | flops | bytes accessed | tf_op | source)
XLA Modules:
  0.0 92.2 jit_solution(17178107226118159516)
XLA Ops:
  0.6 3.0 %collective-permute-start.5 = (bf16[4,256,128]{2,1,0:T(8,128)(2,1)}, bf16[4,256,128]{2,1,0:T(8,128)(2,1)S(1)}, u32[]{:S(2)}, u32[]{:S(2)}) collective-permute-start(bf16[4,256,128]{2,1,0:T(8,128)(2,1)} %refs_4_.1), channel_id=1, source_target_pairs={{0,16},{4,20},{8,24},{12,28},{16,0},{20,4},{24,8},{28,12},{1,17},{... | collective-permute-start | bytes 786440 | tf_op jit(solution)/shard_map/ppermute | solution.py:22
  3.7 0.1 stack.40.ints_ref
  3.7 0.8 copy-done.2
  4.6 0.9 %copy-done.4 = bf16[512,256]{1,0:T(8,128)(2,1)S(1)} copy-done((bf16[512,256]{1,0:T(8,128)(2,1)S(1)}, bf16[512,256]{1,0:T(8,128)(2,1)}, u32[]{:S(2)}) %copy-start.4) | copy-done | bytes 262168
  5.5 0.9 copy-done.5
  6.4 0.7 copy-done.9
  7.1 0.7 copy-done.11
  7.8 0.7 shard_map.104
  8.5 1.6 %collective-permute-start = (bf16[400,256]{1,0:T(8,128)(2,1)S(1)}, bf16[400,256]{1,0:T(8,128)(2,1)S(1)}, u32[]{:S(2)}, u32[]{:S(2)}) collective-permute-start(bf16[400,256]{1,0:T(8,128)(2,1)S(1)} %get-tuple-element.31), channel_id=1, source_target_pairs={{0,1},{1,0},{2,3},{3,2},{4,5},{5,4},{6,7},{7,6},{8,9},{9,8},{10,11... | collective-permute-start | bytes 614408 | tf_op jit(solution)/shard_map/ppermute | solution.py:22
  10.1 2.6 %collective-permute-start.1 = (bf16[400,256]{1,0:T(8,128)(2,1)S(1)}, bf16[400,256]{1,0:T(8,128)(2,1)S(1)}, u32[]{:S(2)}, u32[]{:S(2)}) collective-permute-start(bf16[400,256]{1,0:T(8,128)(2,1)S(1)} %get-tuple-element.32), channel_id=1, source_target_pairs={{0,2},{1,3},{2,0},{3,1},{4,6},{5,7},{6,4},{7,5},{8,10},{9,11},{10,... | collective-permute-start | bytes 614408 | tf_op jit(solution)/shard_map/ppermute | solution.py:22
  12.7 1.4 %collective-permute-start.3 = (bf16[4,256,128]{2,1,0:T(8,128)(2,1)}, bf16[4,256,128]{2,1,0:T(8,128)(2,1)S(1)}, u32[]{:S(2)}, u32[]{:S(2)}) collective-permute-start(bf16[4,256,128]{2,1,0:T(8,128)(2,1)} %refs_4_.1), channel_id=1, source_target_pairs={{0,24},{4,28},{8,16},{12,20},{16,8},{20,12},{24,0},{28,4},{1,25},{... | collective-permute-start | bytes 786440 | tf_op jit(solution)/shard_map/ppermute | solution.py:22
  14.2 0.5 collective-permute-start.4
  14.7 4.7 %collective-permute-done.refs_1_.refs_2_ = bf16[400,256]{1,0:T(8,128)(2,1)S(1)} collective-permute-done((bf16[400,256]{1,0:T(8,128)(2,1)S(1)}, bf16[400,256]{1,0:T(8,128)(2,1)S(1)}, u32[]{:S(2)}, u32[]{:S(2)}) %collective-permute-start) | collective-permute-done | bytes 204832 | tf_op jit(solution)/shard_map/ppermute | solution.py:22
  19.4 0.5 collective-permute-start.10
  19.9 1.8 %collective-permute-done.1.refs_2_.refs_3_ = bf16[400,256]{1,0:T(8,128)(2,1)S(1)} collective-permute-done((bf16[400,256]{1,0:T(8,128)(2,1)S(1)}, bf16[400,256]{1,0:T(8,128)(2,1)S(1)}, u32[]{:S(2)}, u32[]{:S(2)}) %collective-permute-start.1) | collective-permute-done | bytes 204832 | tf_op jit(solution)/shard_map/ppermute | solution.py:22
  21.7 2.5 %collective-permute-start.2 = (bf16[400,256]{1,0:T(8,128)(2,1)S(1)}, bf16[400,256]{1,0:T(8,128)(2,1)S(1)}, u32[]{:S(2)}, u32[]{:S(2)}) collective-permute-start(bf16[400,256]{1,0:T(8,128)(2,1)S(1)} %get-tuple-element.33), channel_id=1, source_target_pairs={{0,3},{1,2},{2,1},{3,0},{4,7},{5,6},{6,5},{7,4},{8,11},{9,10},{10,... | collective-permute-start | bytes 614408 | tf_op jit(solution)/shard_map/ppermute | solution.py:22
  24.2 0.0 collective-permute-done.3.refs_6_.refs_5_
  24.2 1.5 %collective-permute-done.4.refs_7_.refs_6_ = bf16[4,256,128]{2,1,0:T(8,128)(2,1)S(1)} collective-permute-done((bf16[4,256,128]{2,1,0:T(8,128)(2,1)}, bf16[4,256,128]{2,1,0:T(8,128)(2,1)S(1)}, u32[]{:S(2)}, u32[]{:S(2)}) %collective-permute-start.4) | collective-permute-done | bytes 262176 | tf_op jit(solution)/shard_map/ppermute | solution.py:22
  25.7 3.6 %collective-permute-done.2.refs_3_.refs_4_ = bf16[400,256]{1,0:T(8,128)(2,1)S(1)} collective-permute-done((bf16[400,256]{1,0:T(8,128)(2,1)S(1)}, bf16[400,256]{1,0:T(8,128)(2,1)S(1)}, u32[]{:S(2)}, u32[]{:S(2)}) %collective-permute-start.2) | collective-permute-done | bytes 204832 | tf_op jit(solution)/shard_map/ppermute | solution.py:22
  29.4 0.6 shard_map.105
  29.9 0.6 collective-permute-start.14
  30.6 1.4 %collective-permute-start.13 = (bf16[144,1024]{1,0:T(8,128)(2,1)S(1)}, bf16[144,1024]{1,0:T(8,128)(2,1)S(1)}, u32[]{:S(2)}, u32[]{:S(2)}) collective-permute-start(bf16[144,1024]{1,0:T(8,128)(2,1)S(1)} %get-tuple-element.35.refs_4_), channel_id=1, source_target_pairs={{0,8},{4,12},{8,0},{12,4},{16,24},{20,28},{24,16},{28,20},{1,9},{5... | collective-permute-start | bytes 884744 | tf_op jit(solution)/shard_map/ppermute | solution.py:22
  32.0 0.0 collective-permute-done.10.refs_12_.refs_11_
  32.0 1.5 %collective-permute-start.6 = (bf16[144,1024]{1,0:T(8,128)(2,1)S(1)}, bf16[144,1024]{1,0:T(8,128)(2,1)S(1)}, u32[]{:S(2)}, u32[]{:S(2)}) collective-permute-start(bf16[144,1024]{1,0:T(8,128)(2,1)S(1)} %get-tuple-element.35.refs_4_), channel_id=1, source_target_pairs={{0,24},{4,28},{8,16},{12,20},{16,8},{20,12},{24,0},{28,4},{1,25},{... | collective-permute-start | bytes 884744 | tf_op jit(solution)/shard_map/ppermute | solution.py:22
  33.5 0.0 collective-permute-done.8.refs_10_.refs_9_
  33.5 0.0 collective-permute-done.9.refs_11_.refs_10_
  33.5 0.9 %copy-done = bf16[4,256,128]{2,1,0:T(8,128)(2,1)S(1)} copy-done((bf16[4,256,128]{2,1,0:T(8,128)(2,1)S(1)}, bf16[4,256,128]{2,1,0:T(8,128)(2,1)}, u32[]{:S(2)}) %copy-start) | copy-done | bytes 262168
  34.4 1.8 %shard_map.106 = (f32[256,256]{1,0:T(8,128)S(1)}, bf16[256,256]{1,0:T(8,128)(2,1)S(1)}) custom-call(s32[10]{0:T(128)S(1)} %stack.40.ints_ref, f32[32,128]{1,0:T(8,128)S(1)} %get-tuple-element.36.refs_0_, bf16[400,256]{1,0:T(8,128)(2,1)S(1)} %get-tuple-element.30.refs_0_.refs_1_, bf16[400,256]{1,0:T(8,128)(2,1)S(1)} %collective-permute-done.refs_1_.refs_2_, ...), custom_call_target="tpu_custom_call" | custom-call | tf_op jit(solution)/shard_map/pallas_call | solution.py:74
  36.3 2.9 %collective-permute-start.11 = (bf16[256,256]{1,0:T(8,128)(2,1)S(1)}, bf16[256,256]{1,0:T(8,128)(2,1)S(1)}, u32[]{:S(2)}, u32[]{:S(2)}) collective-permute-start(bf16[256,256]{1,0:T(8,128)(2,1)S(1)} %get-tuple-element.37.refs_0_), channel_id=1, source_target_pairs={{0,1},{1,0},{2,3},{3,2},{4,5},{5,4},{6,7},{7,6},{8,9},{9,8},{10,11... | collective-permute-start | bytes 393224 | tf_op jit(solution)/shard_map/ppermute | solution.py:22
  39.2 0.2 collective-permute-start.12
  39.4 0.5 collective-permute-done.14.refs_7_
  39.9 3.6 %collective-permute-done.11.refs_1_ = bf16[256,256]{1,0:T(8,128)(2,1)S(1)} collective-permute-done((bf16[256,256]{1,0:T(8,128)(2,1)S(1)}, bf16[256,256]{1,0:T(8,128)(2,1)S(1)}, u32[]{:S(2)}, u32[]{:S(2)}) %collective-permute-start.11) | collective-permute-done | bytes 131104 | tf_op jit(solution)/shard_map/ppermute | solution.py:22
  43.4 3.0 %collective-permute-done.12.refs_2_ = bf16[256,256]{1,0:T(8,128)(2,1)S(1)} collective-permute-done((bf16[256,256]{1,0:T(8,128)(2,1)S(1)}, bf16[256,256]{1,0:T(8,128)(2,1)S(1)}, u32[]{:S(2)}, u32[]{:S(2)}) %collective-permute-start.12) | collective-permute-done | bytes 131104 | tf_op jit(solution)/shard_map/ppermute | solution.py:22
  46.4 0.5 collective-permute-start.17
  46.9 0.1 collective-permute-start.16
  47.0 1.5 %collective-permute-start.19 = (bf16[256,256]{1,0:T(8,128)(2,1)S(1)}, bf16[256,256]{1,0:T(8,128)(2,1)S(1)}, u32[]{:S(2)}, u32[]{:S(2)}) collective-permute-start(bf16[256,256]{1,0:T(8,128)(2,1)S(1)} %get-tuple-element.37.refs_0_), channel_id=1, source_target_pairs={{0,3},{1,2},{2,1},{3,0},{4,7},{5,6},{6,5},{7,4},{8,11},{9,10},{10,... | collective-permute-start | bytes 393224 | tf_op jit(solution)/shard_map/ppermute | solution.py:22
  48.6 0.3 collective-permute-done.16.refs_9_
  48.9 2.3 %shard_map.107 = (bf16[64,1024]{1,0:T(8,128)(2,1)S(1)}, bf16[64,1024]{1,0:T(8,128)(2,1)S(1)}, bf16[64,1024]{1,0:T(8,128)(2,1)S(1)}, bf16[64,1024]{1,0:T(8,128)(2,1)S(1)}, f32[8,128]{1,0:T(8,128)S(1)}) custom-call(s32[10]{0:T(128)S(1)} %stack.40.ints_ref, bf16[400,256]{1,0:T(8,128)(2,1)S(1)} %get-tuple-element.30.refs_0_.refs_1_, ...), custom_call_target="tpu_custom_call" | custom-call | tf_op jit(solution)/shard_map/pallas_call | solution.py:74
  51.1 0.0 copy-start.6
  51.1 0.0 copy-start.7
  51.1 0.0 copy-start.8
  51.2 0.0 copy-start.1
  51.2 0.4 collective-permute-start.20
  51.6 2.3 %collective-permute-start.21 = (bf16[64,1024]{1,0:T(8,128)(2,1)S(1)}, bf16[64,1024]{1,0:T(8,128)(2,1)S(1)}, u32[]{:S(2)}, u32[]{:S(2)}) collective-permute-start(bf16[64,1024]{1,0:T(8,128)(2,1)S(1)} %get-tuple-element.49), channel_id=1, source_target_pairs={{0,2},{1,3},{2,0},{3,1},{4,6},{5,7},{6,4},{7,5},{8,10},{9,11},{10,... | collective-permute-start | bytes 393224 | tf_op jit(solution)/shard_map/ppermute | solution.py:22
  53.8 1.8 %collective-permute-start.22 = (bf16[64,1024]{1,0:T(8,128)(2,1)S(1)}, bf16[64,1024]{1,0:T(8,128)(2,1)S(1)}, u32[]{:S(2)}, u32[]{:S(2)}) collective-permute-start(bf16[64,1024]{1,0:T(8,128)(2,1)S(1)} %get-tuple-element.50), channel_id=1, source_target_pairs={{0,3},{1,2},{2,1},{3,0},{4,7},{5,6},{6,5},{7,4},{8,11},{9,10},{10,... | collective-permute-start | bytes 393224 | tf_op jit(solution)/shard_map/ppermute | solution.py:22
  55.6 2.8 %shard_map.109 = (bf16[64,1024]{1,0:T(8,128)(2,1)S(1)}, bf16[64,1024]{1,0:T(8,128)(2,1)S(1)}, bf16[64,1024]{1,0:T(8,128)(2,1)S(1)}, bf16[64,1024]{1,0:T(8,128)(2,1)S(1)}, f32[8,128]{1,0:T(8,128)}) custom-call(s32[10]{0:T(128)S(1)} %stack.40.ints_ref, bf16[256,256]{1,0:T(8,128)(2,1)S(1)} %get-tuple-element.37.refs_0_, ...), custom_call_target="tpu_custom_call" | custom-call | tf_op jit(solution)/shard_map/pallas_call | solution.py:74
  58.4 1.1 %collective-permute-start.23 = (bf16[64,1024]{1,0:T(8,128)(2,1)S(1)}, bf16[64,1024]{1,0:T(8,128)(2,1)S(1)}, u32[]{:S(2)}, u32[]{:S(2)}) collective-permute-start(bf16[64,1024]{1,0:T(8,128)(2,1)S(1)} %get-tuple-element.52), channel_id=1, source_target_pairs={{0,1},{1,0},{2,3},{3,2},{4,5},{5,4},{6,7},{7,6},{8,9},{9,8},{10,11... | collective-permute-start | bytes 393224 | tf_op jit(solution)/shard_map/ppermute | solution.py:22
  59.5 2.6 %shard_map.108 = (bf16[8,256,512]{2,1,0:T(8,128)(2,1)S(1)}, bf16[8,256,512]{2,1,0:T(8,128)(2,1)S(1)}, f32[256,256]{1,0:T(8,128)S(1)}) custom-call(s32[10]{0:T(128)S(1)} %stack.40.ints_ref, s32[1,4096]{1,0:T(1,128)S(1)} %bitcast.14, s32[1,4096]{1,0:T(1,128)S(1)} %bitcast.15, f32[1,4096]{1,0:T(1,128)S(1)} %bitcast.16), custom_call_target="tpu_custom_call" | custom-call | tf_op jit(solution)/shard_map/pallas_call | solution.py:74
  62.1 1.9 %shard_map.110.refs_3_ = f32[4,256,256]{2,1,0:T(8,128)S(1)} custom-call(s32[10]{0:T(128)S(1)} %stack.40.ints_ref, bf16[256,256]{1,0:T(8,128)(2,1)S(1)} %get-tuple-element.37.refs_0_, bf16[256,256]{1,0:T(8,128)(2,1)S(1)} %collective-permute-done.11.refs_1_, bf16[256,256]{1,0:T(8,128)(2,1)S(1)} %collective-permute-done.12.refs_2_, ...), custom_call_target="tpu_custom_call" | custom-call | tf_op jit(solution)/shard_map/pallas_call | solution.py:74
  64.0 0.6 collective-permute-done.21.refs_9_
  64.6 3.5 %shard_map.111 = (f32[64,256]{1,0:T(8,128)S(1)}, f32[8,128]{1,0:T(8,128)S(1)}) custom-call(s32[10]{0:T(128)S(1)} %stack.40.ints_ref, f32[64,256]{1,0:T(8,128)S(1)} %copy-done.3, f32[8,128]{1,0:T(8,128)S(1)} %get-tuple-element.41.refs_1_, s32[1,64]{1,0:T(1,128)S(1)} %bitcast.18, s32[1,256]{1,0:T(1,128)S(1)} %bitcast.21, ...), custom_call_target="tpu_custom_call" | custom-call | tf_op jit(solution)/shard_map/pallas_call | solution.py:74
  68.1 0.1 collective-permute-start.26
  68.2 1.1 %collective-permute-done.26 = f32[8,128]{1,0:T(8,128)S(1)} collective-permute-done((f32[8,128]{1,0:T(8,128)S(1)}, f32[8,128]{1,0:T(8,128)S(1)}, u32[]{:S(2)}, u32[]{:S(2)}) %collective-permute-start.26) | collective-permute-done | bytes 4128 | tf_op jit(solution)/shard_map/ppermute | solution.py:22
  69.4 0.1 select_add_fusion.refs_4_
  69.4 3.0 %collective-permute-start.27 = (f32[8,128]{1,0:T(8,128)S(1)}, f32[8,128]{1,0:T(8,128)S(1)}, u32[]{:S(2)}, u32[]{:S(2)}) collective-permute-start(f32[8,128]{1,0:T(8,128)S(1)} %select_add_fusion.refs_4_), channel_id=1, source_target_pairs={{0,1},{1,0},{2,3},{3,2},{4,5},{5,4},{6,7},{7,6},{8,9},{9,8},{10,11... | collective-permute-start | bytes 12296 | tf_op jit(solution)/shard_map/ppermute | solution.py:22
  72.4 2.4 %collective-permute-start.29 = (f32[8,128]{1,0:T(8,128)S(1)}, f32[8,128]{1,0:T(8,128)S(1)}, u32[]{:S(2)}, u32[]{:S(2)}) collective-permute-start(f32[8,128]{1,0:T(8,128)S(1)} %select_add_fusion.refs_4_), channel_id=1, source_target_pairs={{0,3},{1,2},{2,1},{3,0},{4,7},{5,6},{6,5},{7,4},{8,11},{9,10},{10,... | collective-permute-start | bytes 12296 | tf_op jit(solution)/shard_map/ppermute | solution.py:22
  74.8 0.9 %collective-permute-start.24 = (bf16[64,1024]{1,0:T(8,128)(2,1)S(1)}, bf16[64,1024]{1,0:T(8,128)(2,1)S(1)}, u32[]{:S(2)}, u32[]{:S(2)}) collective-permute-start(bf16[64,1024]{1,0:T(8,128)(2,1)S(1)} %get-tuple-element.53), channel_id=1, source_target_pairs={{0,2},{1,3},{2,0},{3,1},{4,6},{5,7},{6,4},{7,5},{8,10},{9,11},{10,... | collective-permute-start | bytes 393224 | tf_op jit(solution)/shard_map/ppermute | solution.py:22
  75.7 2.5 %collective-permute-start.25 = (bf16[64,1024]{1,0:T(8,128)(2,1)S(1)}, bf16[64,1024]{1,0:T(8,128)(2,1)S(1)}, u32[]{:S(2)}, u32[]{:S(2)}) collective-permute-start(bf16[64,1024]{1,0:T(8,128)(2,1)S(1)} %get-tuple-element.54), channel_id=1, source_target_pairs={{0,3},{1,2},{2,1},{3,0},{4,7},{5,6},{6,5},{7,4},{8,11},{9,10},{10,... | collective-permute-start | bytes 393224 | tf_op jit(solution)/shard_map/ppermute | solution.py:22
  78.3 1.5 %collective-permute-start.30 = (f32[8,128]{1,0:T(8,128)S(1)}, f32[8,128]{1,0:T(8,128)S(1)}, u32[]{:S(2)}, u32[]{:S(2)}) collective-permute-start(f32[8,128]{1,0:T(8,128)S(1)} %add_add_fusion.refs_8_), channel_id=1, source_target_pairs={{0,24},{4,28},{8,16},{12,20},{16,8},{20,12},{24,0},{28,4},{1,25},{... | collective-permute-start | bytes 12296 | tf_op jit(solution)/shard_map/ppermute | solution.py:22
  79.8 0.7 collective-permute-start.31
  80.5 1.3 %collective-permute-start.32 = (f32[8,128]{1,0:T(8,128)S(1)}, f32[8,128]{1,0:T(8,128)S(1)}, u32[]{:S(2)}, u32[]{:S(2)}) collective-permute-start(f32[8,128]{1,0:T(8,128)S(1)} %add_add_fusion.refs_8_), channel_id=1, source_target_pairs={{0,16},{4,20},{8,24},{12,28},{16,0},{20,4},{24,8},{28,12},{1,17},{... | collective-permute-start | bytes 12296 | tf_op jit(solution)/shard_map/ppermute | solution.py:22
  81.9 4.9 %collective-permute-done.24.refs_6_ = bf16[64,1024]{1,0:T(8,128)(2,1)S(1)} collective-permute-done((bf16[64,1024]{1,0:T(8,128)(2,1)S(1)}, bf16[64,1024]{1,0:T(8,128)(2,1)S(1)}, u32[]{:S(2)}, u32[]{:S(2)}) %collective-permute-start.24) | collective-permute-done | bytes 131104 | tf_op jit(solution)/shard_map/ppermute | solution.py:22
  86.7 3.7 %shard_map.112.refs_1_ = f32[3,64,256]{2,1,0:T(8,128)S(1)} custom-call(s32[10]{0:T(128)S(1)} %stack.40.ints_ref, f32[64,256]{1,0:T(8,128)S(1)} %get-tuple-element.51.refs_0_, bf16[8,256,512]{2,1,0:T(8,128)(2,1)S(1)} %get-tuple-element.42.refs_4_.refs_1_, bf16[8,256,512]{2,1,0:T(8,128)(2,1)S(1)} %get-tuple-element.43.refs_5_.refs_2_, ...), custom_call_target="tpu_custom_call" | custom-call | tf_op jit(solution)/shard_map/pallas_call | solution.py:74
  90.5 1.7 %shard_map.113 = (f32[256,256]{1,0:T(8,128)}, f32[64,256]{1,0:T(8,128)}) custom-call(s32[10]{0:T(128)S(1)} %stack.40.ints_ref, s32[1,64]{1,0:T(1,128)S(1)} %bitcast.19, f32[3,64,256]{2,1,0:T(8,128)S(1)} %shard_map.112.refs_1_, f32[256,256]{1,0:T(8,128)S(1)} %get-tuple-element.55.refs_2_, f32[4,256,256]{2,1,0:T(8,128)S(1)} %shard_map.110.refs_3_, ...), custom_call_target="tpu_custom_call" | custom-call | tf_op jit(solution)/shard_map/pallas_call | solution.py:74
  (42 shorter events, 0.1 us)
Async XLA Ops:
  0.6 18.8 %collective-permute-start.5 = (bf16[4,256,128]{2,1,0:T(8,128)(2,1)}, bf16[4,256,128]{2,1,0:T(8,128)(2,1)S(1)}, u32[]{:S(2)}, u32[]{:S(2)}) collective-permute-start(bf16[4,256,128]{2,1,0:T(8,128)(2,1)} %refs_4_.1), channel_id=1, source_target_pairs={{0,16},{4,20},{8,24},{12,28},{16,0},{20,4},{24,8},{28,12},{1,17},{... | collective-permute-start | bytes 786440 | tf_op jit(solution)/shard_map/ppermute | solution.py:22
  3.7 0.8 copy-start.2
  4.6 0.9 %copy-start.4 = (bf16[512,256]{1,0:T(8,128)(2,1)S(1)}, bf16[512,256]{1,0:T(8,128)(2,1)}, u32[]{:S(2)}) copy-start(bf16[512,256]{1,0:T(8,128)(2,1)} %refs_1_.1) | copy-start | bytes 786436
  5.5 0.9 copy-start.5
  6.4 0.7 copy-start.9
  7.1 0.7 copy-start.11
  8.5 10.9 %collective-permute-start = (bf16[400,256]{1,0:T(8,128)(2,1)S(1)}, bf16[400,256]{1,0:T(8,128)(2,1)S(1)}, u32[]{:S(2)}, u32[]{:S(2)}) collective-permute-start(bf16[400,256]{1,0:T(8,128)(2,1)S(1)} %get-tuple-element.31), channel_id=1, source_target_pairs={{0,1},{1,0},{2,3},{3,2},{4,5},{5,4},{6,7},{7,6},{8,9},{9,8},{10,11... | collective-permute-start | bytes 614408 | tf_op jit(solution)/shard_map/ppermute | solution.py:22
  10.1 11.6 %collective-permute-start.1 = (bf16[400,256]{1,0:T(8,128)(2,1)S(1)}, bf16[400,256]{1,0:T(8,128)(2,1)S(1)}, u32[]{:S(2)}, u32[]{:S(2)}) collective-permute-start(bf16[400,256]{1,0:T(8,128)(2,1)S(1)} %get-tuple-element.32), channel_id=1, source_target_pairs={{0,2},{1,3},{2,0},{3,1},{4,6},{5,7},{6,4},{7,5},{8,10},{9,11},{10,... | collective-permute-start | bytes 614408 | tf_op jit(solution)/shard_map/ppermute | solution.py:22
  12.7 11.5 %collective-permute-start.3 = (bf16[4,256,128]{2,1,0:T(8,128)(2,1)}, bf16[4,256,128]{2,1,0:T(8,128)(2,1)S(1)}, u32[]{:S(2)}, u32[]{:S(2)}) collective-permute-start(bf16[4,256,128]{2,1,0:T(8,128)(2,1)} %refs_4_.1), channel_id=1, source_target_pairs={{0,24},{4,28},{8,16},{12,20},{16,8},{20,12},{24,0},{28,4},{1,25},{... | collective-permute-start | bytes 786440 | tf_op jit(solution)/shard_map/ppermute | solution.py:22
  14.2 11.5 %collective-permute-start.4 = (bf16[4,256,128]{2,1,0:T(8,128)(2,1)}, bf16[4,256,128]{2,1,0:T(8,128)(2,1)S(1)}, u32[]{:S(2)}, u32[]{:S(2)}) collective-permute-start(bf16[4,256,128]{2,1,0:T(8,128)(2,1)} %refs_4_.1), channel_id=1, source_target_pairs={{0,8},{4,12},{8,0},{12,4},{16,24},{20,28},{24,16},{28,20},{1,9},{5... | collective-permute-start | bytes 786440 | tf_op jit(solution)/shard_map/ppermute | solution.py:22
  19.4 11.2 %collective-permute-start.7 = (bf16[4,256,128]{2,1,0:T(8,128)(2,1)}, bf16[4,256,128]{2,1,0:T(8,128)(2,1)S(1)}, u32[]{:S(2)}, u32[]{:S(2)}) collective-permute-start(bf16[4,256,128]{2,1,0:T(8,128)(2,1)} %refs_4_.1), channel_id=1, source_target_pairs={{0,4},{4,0},{8,12},{12,8},{16,20},{20,16},{24,28},{28,24},{1,5},{5... | collective-permute-start | bytes 786440 | tf_op jit(solution)/shard_map/ppermute | solution.py:22
  19.4 12.6 %collective-permute-start.10 = (bf16[4,256,128]{2,1,0:T(8,128)(2,1)S(1)}, bf16[4,256,128]{2,1,0:T(8,128)(2,1)S(1)}, u32[]{:S(2)}, u32[]{:S(2)}) collective-permute-start(bf16[4,256,128]{2,1,0:T(8,128)(2,1)S(1)} %collective-permute-done.5.refs_8_.refs_7_), channel_id=1, source_target_pairs={{0,4},{4,0},{8,12},{12,8},{16,20},{20,16},{24,28},{28,24},{1,5},{5... | collective-permute-start | bytes 786440 | tf_op jit(solution)/shard_map/ppermute | solution.py:22
  21.7 7.6 %collective-permute-start.2 = (bf16[400,256]{1,0:T(8,128)(2,1)S(1)}, bf16[400,256]{1,0:T(8,128)(2,1)S(1)}, u32[]{:S(2)}, u32[]{:S(2)}) collective-permute-start(bf16[400,256]{1,0:T(8,128)(2,1)S(1)} %get-tuple-element.33), channel_id=1, source_target_pairs={{0,3},{1,2},{2,1},{3,0},{4,7},{5,6},{6,5},{7,4},{8,11},{9,10},{10,... | collective-permute-start | bytes 614408 | tf_op jit(solution)/shard_map/ppermute | solution.py:22
  24.2 9.3 %collective-permute-start.8 = (bf16[4,256,128]{2,1,0:T(8,128)(2,1)S(1)}, bf16[4,256,128]{2,1,0:T(8,128)(2,1)S(1)}, u32[]{:S(2)}, u32[]{:S(2)}) collective-permute-start(bf16[4,256,128]{2,1,0:T(8,128)(2,1)S(1)} %collective-permute-done.3.refs_6_.refs_5_), channel_id=1, source_target_pairs={{0,4},{4,0},{8,12},{12,8},{16,20},{20,16},{24,28},{28,24},{1,5},{5... | collective-permute-start | bytes 786440 | tf_op jit(solution)/shard_map/ppermute | solution.py:22
  25.7 7.8 %collective-permute-start.9 = (bf16[4,256,128]{2,1,0:T(8,128)(2,1)S(1)}, bf16[4,256,128]{2,1,0:T(8,128)(2,1)S(1)}, u32[]{:S(2)}, u32[]{:S(2)}) collective-permute-start(bf16[4,256,128]{2,1,0:T(8,128)(2,1)S(1)} %collective-permute-done.4.refs_7_.refs_6_), channel_id=1, source_target_pairs={{0,4},{4,0},{8,12},{12,8},{16,20},{20,16},{24,28},{28,24},{1,5},{5... | collective-permute-start | bytes 786440 | tf_op jit(solution)/shard_map/ppermute | solution.py:22
  29.9 9.9 %collective-permute-start.14 = (bf16[144,1024]{1,0:T(8,128)(2,1)S(1)}, bf16[144,1024]{1,0:T(8,128)(2,1)S(1)}, u32[]{:S(2)}, u32[]{:S(2)}) collective-permute-start(bf16[144,1024]{1,0:T(8,128)(2,1)S(1)} %get-tuple-element.35.refs_4_), channel_id=1, source_target_pairs={{0,16},{4,20},{8,24},{12,28},{16,0},{20,4},{24,8},{28,12},{1,17},{... | collective-permute-start | bytes 884744 | tf_op jit(solution)/shard_map/ppermute | solution.py:22
  30.6 15.9 %collective-permute-start.13 = (bf16[144,1024]{1,0:T(8,128)(2,1)S(1)}, bf16[144,1024]{1,0:T(8,128)(2,1)S(1)}, u32[]{:S(2)}, u32[]{:S(2)}) collective-permute-start(bf16[144,1024]{1,0:T(8,128)(2,1)S(1)} %get-tuple-element.35.refs_4_), channel_id=1, source_target_pairs={{0,8},{4,12},{8,0},{12,4},{16,24},{20,28},{24,16},{28,20},{1,9},{5... | collective-permute-start | bytes 884744 | tf_op jit(solution)/shard_map/ppermute | solution.py:22
  32.0 14.9 %collective-permute-start.6 = (bf16[144,1024]{1,0:T(8,128)(2,1)S(1)}, bf16[144,1024]{1,0:T(8,128)(2,1)S(1)}, u32[]{:S(2)}, u32[]{:S(2)}) collective-permute-start(bf16[144,1024]{1,0:T(8,128)(2,1)S(1)} %get-tuple-element.35.refs_4_), channel_id=1, source_target_pairs={{0,24},{4,28},{8,16},{12,20},{16,8},{20,12},{24,0},{28,4},{1,25},{... | collective-permute-start | bytes 884744 | tf_op jit(solution)/shard_map/ppermute | solution.py:22
  33.5 1.0 %copy-start = (bf16[4,256,128]{2,1,0:T(8,128)(2,1)S(1)}, bf16[4,256,128]{2,1,0:T(8,128)(2,1)}, u32[]{:S(2)}) copy-start(bf16[4,256,128]{2,1,0:T(8,128)(2,1)} %refs_4_.1) | copy-start | bytes 786436
  36.3 7.1 %collective-permute-start.11 = (bf16[256,256]{1,0:T(8,128)(2,1)S(1)}, bf16[256,256]{1,0:T(8,128)(2,1)S(1)}, u32[]{:S(2)}, u32[]{:S(2)}) collective-permute-start(bf16[256,256]{1,0:T(8,128)(2,1)S(1)} %get-tuple-element.37.refs_0_), channel_id=1, source_target_pairs={{0,1},{1,0},{2,3},{3,2},{4,5},{5,4},{6,7},{7,6},{8,9},{9,8},{10,11... | collective-permute-start | bytes 393224 | tf_op jit(solution)/shard_map/ppermute | solution.py:22
  39.2 7.3 %collective-permute-start.12 = (bf16[256,256]{1,0:T(8,128)(2,1)S(1)}, bf16[256,256]{1,0:T(8,128)(2,1)S(1)}, u32[]{:S(2)}, u32[]{:S(2)}) collective-permute-start(bf16[256,256]{1,0:T(8,128)(2,1)S(1)} %get-tuple-element.37.refs_0_), channel_id=1, source_target_pairs={{0,2},{1,3},{2,0},{3,1},{4,6},{5,7},{6,4},{7,5},{8,10},{9,11},{10,... | collective-permute-start | bytes 393224 | tf_op jit(solution)/shard_map/ppermute | solution.py:22
  39.9 8.7 %collective-permute-start.15 = (bf16[144,1024]{1,0:T(8,128)(2,1)S(1)}, bf16[144,1024]{1,0:T(8,128)(2,1)S(1)}, u32[]{:S(2)}, u32[]{:S(2)}) collective-permute-start(bf16[144,1024]{1,0:T(8,128)(2,1)S(1)} %get-tuple-element.35.refs_4_), channel_id=1, source_target_pairs={{0,4},{4,0},{8,12},{12,8},{16,20},{20,16},{24,28},{28,24},{1,5},{5... | collective-permute-start | bytes 884744 | tf_op jit(solution)/shard_map/ppermute | solution.py:22
  46.4 2.1 %collective-permute-start.18 = (bf16[144,1024]{1,0:T(8,128)(2,1)S(1)}, bf16[144,1024]{1,0:T(8,128)(2,1)S(1)}, u32[]{:S(2)}, u32[]{:S(2)}) collective-permute-start(bf16[144,1024]{1,0:T(8,128)(2,1)S(1)} %collective-permute-done.14.refs_7_), channel_id=1, source_target_pairs={{0,4},{4,0},{8,12},{12,8},{16,20},{20,16},{24,28},{28,24},{1,5},{5... | collective-permute-start | bytes 884744 | tf_op jit(solution)/shard_map/ppermute | solution.py:22
  46.4 2.1 %collective-permute-start.17 = (bf16[144,1024]{1,0:T(8,128)(2,1)S(1)}, bf16[144,1024]{1,0:T(8,128)(2,1)S(1)}, u32[]{:S(2)}, u32[]{:S(2)}) collective-permute-start(bf16[144,1024]{1,0:T(8,128)(2,1)S(1)} %collective-permute-done.13.refs_6_), channel_id=1, source_target_pairs={{0,4},{4,0},{8,12},{12,8},{16,20},{20,16},{24,28},{28,24},{1,5},{5... | collective-permute-start | bytes 884744 | tf_op jit(solution)/shard_map/ppermute | solution.py:22
  46.9 1.9 %collective-permute-start.16 = (bf16[144,1024]{1,0:T(8,128)(2,1)S(1)}, bf16[144,1024]{1,0:T(8,128)(2,1)S(1)}, u32[]{:S(2)}, u32[]{:S(2)}) collective-permute-start(bf16[144,1024]{1,0:T(8,128)(2,1)S(1)} %collective-permute-done.6.refs_5_), channel_id=1, source_target_pairs={{0,4},{4,0},{8,12},{12,8},{16,20},{20,16},{24,28},{28,24},{1,5},{5... | collective-permute-start | bytes 884744 | tf_op jit(solution)/shard_map/ppermute | solution.py:22
  47.0 8.6 %collective-permute-start.19 = (bf16[256,256]{1,0:T(8,128)(2,1)S(1)}, bf16[256,256]{1,0:T(8,128)(2,1)S(1)}, u32[]{:S(2)}, u32[]{:S(2)}) collective-permute-start(bf16[256,256]{1,0:T(8,128)(2,1)S(1)} %get-tuple-element.37.refs_0_), channel_id=1, source_target_pairs={{0,3},{1,2},{2,1},{3,0},{4,7},{5,6},{6,5},{7,4},{8,11},{9,10},{10,... | collective-permute-start | bytes 393224 | tf_op jit(solution)/shard_map/ppermute | solution.py:22
  51.1 8.4 %copy-start.6 = (s32[4096]{0:T(1024)S(1)}, s32[4096]{0:T(1024)}, u32[]{:S(2)}) copy-start(s32[4096]{0:T(1024)} %param.15) | copy-start | bytes 49156
  51.1 8.4 %copy-start.7 = (s32[4096]{0:T(1024)S(1)}, s32[4096]{0:T(1024)}, u32[]{:S(2)}) copy-start(s32[4096]{0:T(1024)} %param.16) | copy-start | bytes 49156
  51.1 8.4 %copy-start.8 = (f32[4096]{0:T(1024)S(1)}, f32[4096]{0:T(1024)}, u32[]{:S(2)}) copy-start(f32[4096]{0:T(1024)} %param.17) | copy-start | bytes 49156
  51.2 11.0 %copy-start.1 = (bf16[4,256,128]{2,1,0:T(8,128)(2,1)S(1)}, bf16[4,256,128]{2,1,0:T(8,128)(2,1)}, u32[]{:S(2)}) copy-start(bf16[4,256,128]{2,1,0:T(8,128)(2,1)} %refs_4_.1) | copy-start | bytes 786436
  51.2 12.8 %collective-permute-start.20 = (bf16[64,1024]{1,0:T(8,128)(2,1)S(1)}, bf16[64,1024]{1,0:T(8,128)(2,1)S(1)}, u32[]{:S(2)}, u32[]{:S(2)}) collective-permute-start(bf16[64,1024]{1,0:T(8,128)(2,1)S(1)} %get-tuple-element.48), channel_id=1, source_target_pairs={{0,1},{1,0},{2,3},{3,2},{4,5},{5,4},{6,7},{7,6},{8,9},{9,8},{10,11... | collective-permute-start | bytes 393224 | tf_op jit(solution)/shard_map/ppermute | solution.py:22
  51.6 13.0 %collective-permute-start.21 = (bf16[64,1024]{1,0:T(8,128)(2,1)S(1)}, bf16[64,1024]{1,0:T(8,128)(2,1)S(1)}, u32[]{:S(2)}, u32[]{:S(2)}) collective-permute-start(bf16[64,1024]{1,0:T(8,128)(2,1)S(1)} %get-tuple-element.49), channel_id=1, source_target_pairs={{0,2},{1,3},{2,0},{3,1},{4,6},{5,7},{6,4},{7,5},{8,10},{9,11},{10,... | collective-permute-start | bytes 393224 | tf_op jit(solution)/shard_map/ppermute | solution.py:22
  53.8 10.8 %collective-permute-start.22 = (bf16[64,1024]{1,0:T(8,128)(2,1)S(1)}, bf16[64,1024]{1,0:T(8,128)(2,1)S(1)}, u32[]{:S(2)}, u32[]{:S(2)}) collective-permute-start(bf16[64,1024]{1,0:T(8,128)(2,1)S(1)} %get-tuple-element.50), channel_id=1, source_target_pairs={{0,3},{1,2},{2,1},{3,0},{4,7},{5,6},{6,5},{7,4},{8,11},{9,10},{10,... | collective-permute-start | bytes 393224 | tf_op jit(solution)/shard_map/ppermute | solution.py:22
  58.4 6.2 %copy-start.3 = (f32[64,256]{1,0:T(8,128)S(1)}, f32[64,256]{1,0:T(8,128)}, u32[]{:S(2)}) copy-start(f32[64,256]{1,0:T(8,128)} %refs_0_.3) | copy-start | bytes 196612
  58.4 6.2 %copy-start.10 = (s32[64,1]{0,1:T(1,128)S(1)}, s32[64,1]{0,1:T(1,128)}, u32[]{:S(2)}) copy-start(s32[64,1]{0,1:T(1,128)} %param.13) | copy-start | bytes 772
  58.4 6.2 %copy-start.12 = (s32[256,1]{0,1:T(1,128)S(1)}, s32[256,1]{0,1:T(1,128)}, u32[]{:S(2)}) copy-start(s32[256,1]{0,1:T(1,128)} %param.14) | copy-start | bytes 3076
  58.4 9.7 %collective-permute-start.23 = (bf16[64,1024]{1,0:T(8,128)(2,1)S(1)}, bf16[64,1024]{1,0:T(8,128)(2,1)S(1)}, u32[]{:S(2)}, u32[]{:S(2)}) collective-permute-start(bf16[64,1024]{1,0:T(8,128)(2,1)S(1)} %get-tuple-element.52), channel_id=1, source_target_pairs={{0,1},{1,0},{2,3},{3,2},{4,5},{5,4},{6,7},{7,6},{8,9},{9,8},{10,11... | collective-permute-start | bytes 393224 | tf_op jit(solution)/shard_map/ppermute | solution.py:22
  68.1 1.2 %collective-permute-start.26 = (f32[8,128]{1,0:T(8,128)S(1)}, f32[8,128]{1,0:T(8,128)S(1)}, u32[]{:S(2)}, u32[]{:S(2)}) collective-permute-start(f32[8,128]{1,0:T(8,128)S(1)} %get-tuple-element.57), channel_id=1, source_target_pairs={{0,4},{4,0},{8,12},{12,8},{16,20},{20,16},{24,28},{28,24},{1,5},{5... | collective-permute-start | bytes 12296 | tf_op jit(solution)/shard_map/ppermute | solution.py:22
  69.4 8.8 %collective-permute-start.27 = (f32[8,128]{1,0:T(8,128)S(1)}, f32[8,128]{1,0:T(8,128)S(1)}, u32[]{:S(2)}, u32[]{:S(2)}) collective-permute-start(f32[8,128]{1,0:T(8,128)S(1)} %select_add_fusion.refs_4_), channel_id=1, source_target_pairs={{0,1},{1,0},{2,3},{3,2},{4,5},{5,4},{6,7},{7,6},{8,9},{9,8},{10,11... | collective-permute-start | bytes 12296 | tf_op jit(solution)/shard_map/ppermute | solution.py:22
  72.4 5.9 %collective-permute-start.28 = (f32[8,128]{1,0:T(8,128)S(1)}, f32[8,128]{1,0:T(8,128)S(1)}, u32[]{:S(2)}, u32[]{:S(2)}) collective-permute-start(f32[8,128]{1,0:T(8,128)S(1)} %select_add_fusion.refs_4_), channel_id=1, source_target_pairs={{0,2},{1,3},{2,0},{3,1},{4,6},{5,7},{6,4},{7,5},{8,10},{9,11},{10,... | collective-permute-start | bytes 12296 | tf_op jit(solution)/shard_map/ppermute | solution.py:22
  72.4 5.9 %collective-permute-start.29 = (f32[8,128]{1,0:T(8,128)S(1)}, f32[8,128]{1,0:T(8,128)S(1)}, u32[]{:S(2)}, u32[]{:S(2)}) collective-permute-start(f32[8,128]{1,0:T(8,128)S(1)} %select_add_fusion.refs_4_), channel_id=1, source_target_pairs={{0,3},{1,2},{2,1},{3,0},{4,7},{5,6},{6,5},{7,4},{8,11},{9,10},{10,... | collective-permute-start | bytes 12296 | tf_op jit(solution)/shard_map/ppermute | solution.py:22
  74.8 12.0 %collective-permute-start.24 = (bf16[64,1024]{1,0:T(8,128)(2,1)S(1)}, bf16[64,1024]{1,0:T(8,128)(2,1)S(1)}, u32[]{:S(2)}, u32[]{:S(2)}) collective-permute-start(bf16[64,1024]{1,0:T(8,128)(2,1)S(1)} %get-tuple-element.53), channel_id=1, source_target_pairs={{0,2},{1,3},{2,0},{3,1},{4,6},{5,7},{6,4},{7,5},{8,10},{9,11},{10,... | collective-permute-start | bytes 393224 | tf_op jit(solution)/shard_map/ppermute | solution.py:22
  75.7 11.0 %collective-permute-start.25 = (bf16[64,1024]{1,0:T(8,128)(2,1)S(1)}, bf16[64,1024]{1,0:T(8,128)(2,1)S(1)}, u32[]{:S(2)}, u32[]{:S(2)}) collective-permute-start(bf16[64,1024]{1,0:T(8,128)(2,1)S(1)} %get-tuple-element.54), channel_id=1, source_target_pairs={{0,3},{1,2},{2,1},{3,0},{4,7},{5,6},{6,5},{7,4},{8,11},{9,10},{10,... | collective-permute-start | bytes 393224 | tf_op jit(solution)/shard_map/ppermute | solution.py:22
  78.3 12.2 %collective-permute-start.30 = (f32[8,128]{1,0:T(8,128)S(1)}, f32[8,128]{1,0:T(8,128)S(1)}, u32[]{:S(2)}, u32[]{:S(2)}) collective-permute-start(f32[8,128]{1,0:T(8,128)S(1)} %add_add_fusion.refs_8_), channel_id=1, source_target_pairs={{0,24},{4,28},{8,16},{12,20},{16,8},{20,12},{24,0},{28,4},{1,25},{... | collective-permute-start | bytes 12296 | tf_op jit(solution)/shard_map/ppermute | solution.py:22
  79.8 10.7 %collective-permute-start.31 = (f32[8,128]{1,0:T(8,128)S(1)}, f32[8,128]{1,0:T(8,128)S(1)}, u32[]{:S(2)}, u32[]{:S(2)}) collective-permute-start(f32[8,128]{1,0:T(8,128)S(1)} %add_add_fusion.refs_8_), channel_id=1, source_target_pairs={{0,8},{4,12},{8,0},{12,4},{16,24},{20,28},{24,16},{28,20},{1,9},{5... | collective-permute-start | bytes 12296 | tf_op jit(solution)/shard_map/ppermute | solution.py:22
  80.5 10.0 %collective-permute-start.32 = (f32[8,128]{1,0:T(8,128)S(1)}, f32[8,128]{1,0:T(8,128)S(1)}, u32[]{:S(2)}, u32[]{:S(2)}) collective-permute-start(f32[8,128]{1,0:T(8,128)S(1)} %add_add_fusion.refs_8_), channel_id=1, source_target_pairs={{0,16},{4,20},{8,24},{12,28},{16,0},{20,4},{24,8},{28,12},{1,17},{... | collective-permute-start | bytes 12296 | tf_op jit(solution)/shard_map/ppermute | solution.py:22

commit v4 on v3

--- a/solution.py
+++ b/solution.py
@@ -419,7 +419,7 @@
     )
     if small:
         row_of = lax.broadcasted_iota(jnp.int32, (TILE, LANES), 0)
-        news = after(news, later_rates[1])
+        news = after(news, later_rates[1], later_rates[2])
         news = news + jnp.where(row_of == COLUMN_ROW, swap(news, "cells", 1, nc), 0.0)
     news = others(news, ne)
     column = sum(news[1:], news[0])

time: 92.4 us -> 90.8 us (0.983)
  starting transfers between devices: 39 us -> 37.3 us
    ppermute x33, starting transfers between devices: 39 us -> 37.3 us  [swap(): return lax.ppermute(x, axis, [(i, i ^ mask) for i in range(count)])]
  transfers between devices with their start and end apart: 33 -> 33, of which waited for: 11 -> 13; matrix products, arithmetic and copies ran while one was open for 0% -> 0% of each run, Pallas kernels for 22% -> 22%
where the time goes in v4:
time: 90.8 us; the launch traced here: 90.5 us
  starting transfers between devices  37.3 us (41%)
  waiting for transfers between devices  25.7 us (28%)
  Pallas kernels  21.5 us (24%)
  local copies, waits for them, and re-layouts  5.1 us (6%)
    ppermute x33, starting transfers between devices, swap(): return lax.ppermute(x, axis, [(i, i ^ mask) for i in range(count)])  37.3 us
    ppermute x33, waiting for transfers between devices, swap(): return lax.ppermute(x, axis, [(i, i ^ mask) for i in range(count)])  25.7 us
    pallas_call x10, Pallas kernels, call(): pl.pallas_call(whole, out_shape=tuple((jax.ShapeDtypeStruct(s, t) for s,...  21.5 us
    unnamed x26, local copies, waits for them, and re-layouts  5.01 us
  transfers between devices with their start and end apart: 33, of which 13 were waited for; matrix products, arithmetic and copies ran while one was open for 0% of the time, Pallas kernels for 22%

profile of v4, /device:TPU:0, one launch (start us, length us, event | category | flops | bytes accessed | tf_op | source)
XLA Modules:
  0.0 90.5 jit_solution(160643303910021539)
XLA Ops:
  0.6 3.0 %collective-permute-start.5 = (bf16[4,256,128]{2,1,0:T(8,128)(2,1)}, bf16[4,256,128]{2,1,0:T(8,128)(2,1)S(1)}, u32[]{:S(2)}, u32[]{:S(2)}) collective-permute-start(bf16[4,256,128]{2,1,0:T(8,128)(2,1)} %refs_4_.1), channel_id=1, source_target_pairs={{0,16},{4,20},{8,24},{12,28},{16,0},{20,4},{24,8},{28,12},{1,17},{... | collective-permute-start | bytes 786440 | tf_op jit(solution)/shard_map/ppermute | solution.py:22
  3.7 0.1 stack.40.ints_ref
  3.7 0.8 copy-done.2
  4.6 0.9 %copy-done.4 = bf16[512,256]{1,0:T(8,128)(2,1)S(1)} copy-done((bf16[512,256]{1,0:T(8,128)(2,1)S(1)}, bf16[512,256]{1,0:T(8,128)(2,1)}, u32[]{:S(2)}) %copy-start.4) | copy-done | bytes 262168
  5.5 0.9 copy-done.5
  6.4 0.7 copy-done.9
  7.1 0.7 copy-done.11
  7.8 0.7 shard_map.104
  8.5 1.6 %collective-permute-start = (bf16[400,256]{1,0:T(8,128)(2,1)S(1)}, bf16[400,256]{1,0:T(8,128)(2,1)S(1)}, u32[]{:S(2)}, u32[]{:S(2)}) collective-permute-start(bf16[400,256]{1,0:T(8,128)(2,1)S(1)} %get-tuple-element.31), channel_id=1, source_target_pairs={{0,1},{1,0},{2,3},{3,2},{4,5},{5,4},{6,7},{7,6},{8,9},{9,8},{10,11... | collective-permute-start | bytes 614408 | tf_op jit(solution)/shard_map/ppermute | solution.py:22
  10.1 2.6 %collective-permute-start.1 = (bf16[400,256]{1,0:T(8,128)(2,1)S(1)}, bf16[400,256]{1,0:T(8,128)(2,1)S(1)}, u32[]{:S(2)}, u32[]{:S(2)}) collective-permute-start(bf16[400,256]{1,0:T(8,128)(2,1)S(1)} %get-tuple-element.32), channel_id=1, source_target_pairs={{0,2},{1,3},{2,0},{3,1},{4,6},{5,7},{6,4},{7,5},{8,10},{9,11},{10,... | collective-permute-start | bytes 614408 | tf_op jit(solution)/shard_map/ppermute | solution.py:22
  12.7 1.4 %collective-permute-start.3 = (bf16[4,256,128]{2,1,0:T(8,128)(2,1)}, bf16[4,256,128]{2,1,0:T(8,128)(2,1)S(1)}, u32[]{:S(2)}, u32[]{:S(2)}) collective-permute-start(bf16[4,256,128]{2,1,0:T(8,128)(2,1)} %refs_4_.1), channel_id=1, source_target_pairs={{0,24},{4,28},{8,16},{12,20},{16,8},{20,12},{24,0},{28,4},{1,25},{... | collective-permute-start | bytes 786440 | tf_op jit(solution)/shard_map/ppermute | solution.py:22
  14.2 0.5 collective-permute-start.4
  14.7 4.7 %collective-permute-done.refs_1_.refs_2_ = bf16[400,256]{1,0:T(8,128)(2,1)S(1)} collective-permute-done((bf16[400,256]{1,0:T(8,128)(2,1)S(1)}, bf16[400,256]{1,0:T(8,128)(2,1)S(1)}, u32[]{:S(2)}, u32[]{:S(2)}) %collective-permute-start) | collective-permute-done | bytes 204832 | tf_op jit(solution)/shard_map/ppermute | solution.py:22
  19.4 0.5 collective-permute-start.10
  19.9 1.8 %collective-permute-done.1.refs_2_.refs_3_ = bf16[400,256]{1,0:T(8,128)(2,1)S(1)} collective-permute-done((bf16[400,256]{1,0:T(8,128)(2,1)S(1)}, bf16[400,256]{1,0:T(8,128)(2,1)S(1)}, u32[]{:S(2)}, u32[]{:S(2)}) %collective-permute-start.1) | collective-permute-done | bytes 204832 | tf_op jit(solution)/shard_map/ppermute | solution.py:22
  21.7 2.5 %collective-permute-start.2 = (bf16[400,256]{1,0:T(8,128)(2,1)S(1)}, bf16[400,256]{1,0:T(8,128)(2,1)S(1)}, u32[]{:S(2)}, u32[]{:S(2)}) collective-permute-start(bf16[400,256]{1,0:T(8,128)(2,1)S(1)} %get-tuple-element.33), channel_id=1, source_target_pairs={{0,3},{1,2},{2,1},{3,0},{4,7},{5,6},{6,5},{7,4},{8,11},{9,10},{10,... | collective-permute-start | bytes 614408 | tf_op jit(solution)/shard_map/ppermute | solution.py:22
  24.2 0.0 collective-permute-done.3.refs_6_.refs_5_
  24.2 0.0 collective-permute-start.8
  24.2 1.5 %collective-permute-done.4.refs_7_.refs_6_ = bf16[4,256,128]{2,1,0:T(8,128)(2,1)S(1)} collective-permute-done((bf16[4,256,128]{2,1,0:T(8,128)(2,1)}, bf16[4,256,128]{2,1,0:T(8,128)(2,1)S(1)}, u32[]{:S(2)}, u32[]{:S(2)}) %collective-permute-start.4) | collective-permute-done | bytes 262176 | tf_op jit(solution)/shard_map/ppermute | solution.py:22
  25.7 3.6 %collective-permute-done.2.refs_3_.refs_4_ = bf16[400,256]{1,0:T(8,128)(2,1)S(1)} collective-permute-done((bf16[400,256]{1,0:T(8,128)(2,1)S(1)}, bf16[400,256]{1,0:T(8,128)(2,1)S(1)}, u32[]{:S(2)}, u32[]{:S(2)}) %collective-permute-start.2) | collective-permute-done | bytes 204832 | tf_op jit(solution)/shard_map/ppermute | solution.py:22
  29.4 0.6 shard_map.105
  29.9 0.6 collective-permute-start.14
  30.6 1.4 %collective-permute-start.13 = (bf16[144,1024]{1,0:T(8,128)(2,1)S(1)}, bf16[144,1024]{1,0:T(8,128)(2,1)S(1)}, u32[]{:S(2)}, u32[]{:S(2)}) collective-permute-start(bf16[144,1024]{1,0:T(8,128)(2,1)S(1)} %get-tuple-element.35.refs_4_), channel_id=1, source_target_pairs={{0,8},{4,12},{8,0},{12,4},{16,24},{20,28},{24,16},{28,20},{1,9},{5... | collective-permute-start | bytes 884744 | tf_op jit(solution)/shard_map/ppermute | solution.py:22
  32.0 1.5 %collective-permute-start.6 = (bf16[144,1024]{1,0:T(8,128)(2,1)S(1)}, bf16[144,1024]{1,0:T(8,128)(2,1)S(1)}, u32[]{:S(2)}, u32[]{:S(2)}) collective-permute-start(bf16[144,1024]{1,0:T(8,128)(2,1)S(1)} %get-tuple-element.35.refs_4_), channel_id=1, source_target_pairs={{0,24},{4,28},{8,16},{12,20},{16,8},{20,12},{24,0},{28,4},{1,25},{... | collective-permute-start | bytes 884744 | tf_op jit(solution)/shard_map/ppermute | solution.py:22
  33.5 0.9 %copy-done = bf16[4,256,128]{2,1,0:T(8,128)(2,1)S(1)} copy-done((bf16[4,256,128]{2,1,0:T(8,128)(2,1)S(1)}, bf16[4,256,128]{2,1,0:T(8,128)(2,1)}, u32[]{:S(2)}) %copy-start) | copy-done | bytes 262168
  34.4 1.8 %shard_map.106 = (f32[256,256]{1,0:T(8,128)S(1)}, bf16[256,256]{1,0:T(8,128)(2,1)S(1)}) custom-call(s32[10]{0:T(128)S(1)} %stack.40.ints_ref, f32[32,128]{1,0:T(8,128)S(1)} %get-tuple-element.36.refs_0_, bf16[400,256]{1,0:T(8,128)(2,1)S(1)} %get-tuple-element.30.refs_0_.refs_1_, bf16[400,256]{1,0:T(8,128)(2,1)S(1)} %collective-permute-done.refs_1_.refs_2_, ...), custom_call_target="tpu_custom_call" | custom-call | tf_op jit(solution)/shard_map/pallas_call | solution.py:74
  36.3 2.9 %collective-permute-start.11 = (bf16[256,256]{1,0:T(8,128)(2,1)S(1)}, bf16[256,256]{1,0:T(8,128)(2,1)S(1)}, u32[]{:S(2)}, u32[]{:S(2)}) collective-permute-start(bf16[256,256]{1,0:T(8,128)(2,1)S(1)} %get-tuple-element.37.refs_0_), channel_id=1, source_target_pairs={{0,1},{1,0},{2,3},{3,2},{4,5},{5,4},{6,7},{7,6},{8,9},{9,8},{10,11... | collective-permute-start | bytes 393224 | tf_op jit(solution)/shard_map/ppermute | solution.py:22
  39.2 0.2 collective-permute-start.12
  39.4 0.5 collective-permute-done.14.refs_7_
  39.9 3.6 %collective-permute-done.11.refs_1_ = bf16[256,256]{1,0:T(8,128)(2,1)S(1)} collective-permute-done((bf16[256,256]{1,0:T(8,128)(2,1)S(1)}, bf16[256,256]{1,0:T(8,128)(2,1)S(1)}, u32[]{:S(2)}, u32[]{:S(2)}) %collective-permute-start.11) | collective-permute-done | bytes 131104 | tf_op jit(solution)/shard_map/ppermute | solution.py:22
  43.4 3.0 %collective-permute-done.12.refs_2_ = bf16[256,256]{1,0:T(8,128)(2,1)S(1)} collective-permute-done((bf16[256,256]{1,0:T(8,128)(2,1)S(1)}, bf16[256,256]{1,0:T(8,128)(2,1)S(1)}, u32[]{:S(2)}, u32[]{:S(2)}) %collective-permute-start.12) | collective-permute-done | bytes 131104 | tf_op jit(solution)/shard_map/ppermute | solution.py:22
  46.4 0.5 collective-permute-start.17
  46.9 0.1 collective-permute-start.16
  47.0 1.5 %collective-permute-start.19 = (bf16[256,256]{1,0:T(8,128)(2,1)S(1)}, bf16[256,256]{1,0:T(8,128)(2,1)S(1)}, u32[]{:S(2)}, u32[]{:S(2)}) collective-permute-start(bf16[256,256]{1,0:T(8,128)(2,1)S(1)} %get-tuple-element.37.refs_0_), channel_id=1, source_target_pairs={{0,3},{1,2},{2,1},{3,0},{4,7},{5,6},{6,5},{7,4},{8,11},{9,10},{10,... | collective-permute-start | bytes 393224 | tf_op jit(solution)/shard_map/ppermute | solution.py:22
  48.6 0.3 collective-permute-done.16.refs_9_
  48.9 2.3 %shard_map.107 = (bf16[64,1024]{1,0:T(8,128)(2,1)S(1)}, bf16[64,1024]{1,0:T(8,128)(2,1)S(1)}, bf16[64,1024]{1,0:T(8,128)(2,1)S(1)}, bf16[64,1024]{1,0:T(8,128)(2,1)S(1)}, f32[8,128]{1,0:T(8,128)S(1)}) custom-call(s32[10]{0:T(128)S(1)} %stack.40.ints_ref, bf16[400,256]{1,0:T(8,128)(2,1)S(1)} %get-tuple-element.30.refs_0_.refs_1_, ...), custom_call_target="tpu_custom_call" | custom-call | tf_op jit(solution)/shard_map/pallas_call | solution.py:74
  51.1 0.0 copy-start.6
  51.1 0.0 copy-start.7
  51.1 0.0 copy-start.8
  51.2 0.0 copy-start.1
  51.2 0.4 collective-permute-start.20
  51.6 2.3 %collective-permute-start.21 = (bf16[64,1024]{1,0:T(8,128)(2,1)S(1)}, bf16[64,1024]{1,0:T(8,128)(2,1)S(1)}, u32[]{:S(2)}, u32[]{:S(2)}) collective-permute-start(bf16[64,1024]{1,0:T(8,128)(2,1)S(1)} %get-tuple-element.49), channel_id=1, source_target_pairs={{0,2},{1,3},{2,0},{3,1},{4,6},{5,7},{6,4},{7,5},{8,10},{9,11},{10,... | collective-permute-start | bytes 393224 | tf_op jit(solution)/shard_map/ppermute | solution.py:22
  53.8 1.8 %collective-permute-start.22 = (bf16[64,1024]{1,0:T(8,128)(2,1)S(1)}, bf16[64,1024]{1,0:T(8,128)(2,1)S(1)}, u32[]{:S(2)}, u32[]{:S(2)}) collective-permute-start(bf16[64,1024]{1,0:T(8,128)(2,1)S(1)} %get-tuple-element.50), channel_id=1, source_target_pairs={{0,3},{1,2},{2,1},{3,0},{4,7},{5,6},{6,5},{7,4},{8,11},{9,10},{10,... | collective-permute-start | bytes 393224 | tf_op jit(solution)/shard_map/ppermute | solution.py:22
  55.6 2.8 %shard_map.109 = (bf16[64,1024]{1,0:T(8,128)(2,1)S(1)}, bf16[64,1024]{1,0:T(8,128)(2,1)S(1)}, bf16[64,1024]{1,0:T(8,128)(2,1)S(1)}, bf16[64,1024]{1,0:T(8,128)(2,1)S(1)}, f32[8,128]{1,0:T(8,128)}) custom-call(s32[10]{0:T(128)S(1)} %stack.40.ints_ref, bf16[256,256]{1,0:T(8,128)(2,1)S(1)} %get-tuple-element.37.refs_0_, ...), custom_call_target="tpu_custom_call" | custom-call | tf_op jit(solution)/shard_map/pallas_call | solution.py:74
  58.4 1.1 %collective-permute-start.23 = (bf16[64,1024]{1,0:T(8,128)(2,1)S(1)}, bf16[64,1024]{1,0:T(8,128)(2,1)S(1)}, u32[]{:S(2)}, u32[]{:S(2)}) collective-permute-start(bf16[64,1024]{1,0:T(8,128)(2,1)S(1)} %get-tuple-element.52), channel_id=1, source_target_pairs={{0,1},{1,0},{2,3},{3,2},{4,5},{5,4},{6,7},{7,6},{8,9},{9,8},{10,11... | collective-permute-start | bytes 393224 | tf_op jit(solution)/shard_map/ppermute | solution.py:22
  59.5 1.5 %collective-permute-start.24 = (bf16[64,1024]{1,0:T(8,128)(2,1)S(1)}, bf16[64,1024]{1,0:T(8,128)(2,1)S(1)}, u32[]{:S(2)}, u32[]{:S(2)}) collective-permute-start(bf16[64,1024]{1,0:T(8,128)(2,1)S(1)} %get-tuple-element.53), channel_id=1, source_target_pairs={{0,2},{1,3},{2,0},{3,1},{4,6},{5,7},{6,4},{7,5},{8,10},{9,11},{10,... | collective-permute-start | bytes 393224 | tf_op jit(solution)/shard_map/ppermute | solution.py:22
  61.0 2.6 %shard_map.108 = (bf16[8,256,512]{2,1,0:T(8,128)(2,1)S(1)}, bf16[8,256,512]{2,1,0:T(8,128)(2,1)S(1)}, f32[256,256]{1,0:T(8,128)S(1)}) custom-call(s32[10]{0:T(128)S(1)} %stack.40.ints_ref, s32[1,4096]{1,0:T(1,128)S(1)} %bitcast.14, s32[1,4096]{1,0:T(1,128)S(1)} %bitcast.15, f32[1,4096]{1,0:T(1,128)S(1)} %bitcast.16), custom_call_target="tpu_custom_call" | custom-call | tf_op jit(solution)/shard_map/pallas_call | solution.py:74
  63.7 1.9 %shard_map.110.refs_3_ = f32[4,256,256]{2,1,0:T(8,128)S(1)} custom-call(s32[10]{0:T(128)S(1)} %stack.40.ints_ref, bf16[256,256]{1,0:T(8,128)(2,1)S(1)} %get-tuple-element.37.refs_0_, bf16[256,256]{1,0:T(8,128)(2,1)S(1)} %collective-permute-done.11.refs_1_, bf16[256,256]{1,0:T(8,128)(2,1)S(1)} %collective-permute-done.12.refs_2_, ...), custom_call_target="tpu_custom_call" | custom-call | tf_op jit(solution)/shard_map/pallas_call | solution.py:74
  65.6 3.5 %shard_map.111 = (f32[64,256]{1,0:T(8,128)S(1)}, f32[8,128]{1,0:T(8,128)S(1)}) custom-call(s32[10]{0:T(128)S(1)} %stack.40.ints_ref, f32[64,256]{1,0:T(8,128)S(1)} %copy-done.3, f32[8,128]{1,0:T(8,128)S(1)} %get-tuple-element.41.refs_1_, s32[1,64]{1,0:T(1,128)S(1)} %bitcast.18, s32[1,256]{1,0:T(1,128)S(1)} %bitcast.21, ...), custom_call_target="tpu_custom_call" | custom-call | tf_op jit(solution)/shard_map/pallas_call | solution.py:74
  69.1 3.6 %collective-permute-done.24.refs_6_ = bf16[64,1024]{1,0:T(8,128)(2,1)S(1)} collective-permute-done((bf16[64,1024]{1,0:T(8,128)(2,1)S(1)}, bf16[64,1024]{1,0:T(8,128)(2,1)S(1)}, u32[]{:S(2)}, u32[]{:S(2)}) %collective-permute-start.24) | collective-permute-done | bytes 131104 | tf_op jit(solution)/shard_map/ppermute | solution.py:22
  72.7 1.2 %collective-permute-done.26 = f32[8,128]{1,0:T(8,128)S(1)} collective-permute-done((f32[8,128]{1,0:T(8,128)S(1)}, f32[8,128]{1,0:T(8,128)S(1)}, u32[]{:S(2)}, u32[]{:S(2)}) %collective-permute-start.26) | collective-permute-done | bytes 4128 | tf_op jit(solution)/shard_map/ppermute | solution.py:22
  73.8 0.1 select_add_fusion.refs_4_
  73.9 1.7 %collective-permute-start.27 = (f32[8,128]{1,0:T(8,128)S(1)}, f32[8,128]{1,0:T(8,128)S(1)}, u32[]{:S(2)}, u32[]{:S(2)}) collective-permute-start(f32[8,128]{1,0:T(8,128)S(1)} %select_add_fusion.refs_4_), channel_id=1, source_target_pairs={{0,1},{1,0},{2,3},{3,2},{4,5},{5,4},{6,7},{7,6},{8,9},{9,8},{10,11... | collective-permute-start | bytes 12296 | tf_op jit(solution)/shard_map/ppermute | solution.py:22
  75.6 0.2 collective-permute-start.28
  75.8 2.4 %collective-permute-start.29 = (f32[8,128]{1,0:T(8,128)S(1)}, f32[8,128]{1,0:T(8,128)S(1)}, u32[]{:S(2)}, u32[]{:S(2)}) collective-permute-start(f32[8,128]{1,0:T(8,128)S(1)} %select_add_fusion.refs_4_), channel_id=1, source_target_pairs={{0,3},{1,2},{2,1},{3,0},{4,7},{5,6},{6,5},{7,4},{8,11},{9,10},{10,... | collective-permute-start | bytes 12296 | tf_op jit(solution)/shard_map/ppermute | solution.py:22
  78.3 1.4 %collective-permute-start.25 = (bf16[64,1024]{1,0:T(8,128)(2,1)S(1)}, bf16[64,1024]{1,0:T(8,128)(2,1)S(1)}, u32[]{:S(2)}, u32[]{:S(2)}) collective-permute-start(bf16[64,1024]{1,0:T(8,128)(2,1)S(1)} %get-tuple-element.54), channel_id=1, source_target_pairs={{0,3},{1,2},{2,1},{3,0},{4,7},{5,6},{6,5},{7,4},{8,11},{9,10},{10,... | collective-permute-start | bytes 393224 | tf_op jit(solution)/shard_map/ppermute | solution.py:22
  79.7 0.5 collective-permute-done.28.refs_6_
  80.1 1.2 %collective-permute-done.29.refs_7_ = f32[8,128]{1,0:T(8,128)S(1)} collective-permute-done((f32[8,128]{1,0:T(8,128)S(1)}, f32[8,128]{1,0:T(8,128)S(1)}, u32[]{:S(2)}, u32[]{:S(2)}) %collective-permute-start.29) | collective-permute-done | bytes 4128 | tf_op jit(solution)/shard_map/ppermute | solution.py:22
  81.4 1.4 %collective-permute-start.30 = (f32[8,128]{1,0:T(8,128)S(1)}, f32[8,128]{1,0:T(8,128)S(1)}, u32[]{:S(2)}, u32[]{:S(2)}) collective-permute-start(f32[8,128]{1,0:T(8,128)S(1)} %add_add_fusion.refs_8_), channel_id=1, source_target_pairs={{0,24},{4,28},{8,16},{12,20},{16,8},{20,12},{24,0},{28,4},{1,25},{... | collective-permute-start | bytes 12296 | tf_op jit(solution)/shard_map/ppermute | solution.py:22
  82.8 0.5 collective-permute-start.31
  83.3 1.5 %collective-permute-start.32 = (f32[8,128]{1,0:T(8,128)S(1)}, f32[8,128]{1,0:T(8,128)S(1)}, u32[]{:S(2)}, u32[]{:S(2)}) collective-permute-start(f32[8,128]{1,0:T(8,128)S(1)} %add_add_fusion.refs_8_), channel_id=1, source_target_pairs={{0,16},{4,20},{8,24},{12,28},{16,0},{20,4},{24,8},{28,12},{1,17},{... | collective-permute-start | bytes 12296 | tf_op jit(solution)/shard_map/ppermute | solution.py:22
  84.8 0.3 collective-permute-done.25.refs_7_
  85.1 3.7 %shard_map.112.refs_1_ = f32[3,64,256]{2,1,0:T(8,128)S(1)} custom-call(s32[10]{0:T(128)S(1)} %stack.40.ints_ref, f32[64,256]{1,0:T(8,128)S(1)} %get-tuple-element.51.refs_0_, bf16[8,256,512]{2,1,0:T(8,128)(2,1)S(1)} %get-tuple-element.42.refs_4_.refs_1_, bf16[8,256,512]{2,1,0:T(8,128)(2,1)S(1)} %get-tuple-element.43.refs_5_.refs_2_, ...), custom_call_target="tpu_custom_call" | custom-call | tf_op jit(solution)/shard_map/pallas_call | solution.py:74
  88.9 1.7 %shard_map.113 = (f32[256,256]{1,0:T(8,128)}, f32[64,256]{1,0:T(8,128)}) custom-call(s32[10]{0:T(128)S(1)} %stack.40.ints_ref, s32[1,64]{1,0:T(1,128)S(1)} %bitcast.19, f32[3,64,256]{2,1,0:T(8,128)S(1)} %shard_map.112.refs_1_, f32[256,256]{1,0:T(8,128)S(1)} %get-tuple-element.55.refs_2_, f32[4,256,256]{2,1,0:T(8,128)S(1)} %shard_map.110.refs_3_, ...), custom_call_target="tpu_custom_call" | custom-call | tf_op jit(solution)/shard_map/pallas_call | solution.py:74
  (42 shorter events, 0.1 us)
Async XLA Ops:
  0.6 18.8 %collective-permute-start.5 = (bf16[4,256,128]{2,1,0:T(8,128)(2,1)}, bf16[4,256,128]{2,1,0:T(8,128)(2,1)S(1)}, u32[]{:S(2)}, u32[]{:S(2)}) collective-permute-start(bf16[4,256,128]{2,1,0:T(8,128)(2,1)} %refs_4_.1), channel_id=1, source_target_pairs={{0,16},{4,20},{8,24},{12,28},{16,0},{20,4},{24,8},{28,12},{1,17},{... | collective-permute-start | bytes 786440 | tf_op jit(solution)/shard_map/ppermute | solution.py:22
  3.7 0.8 copy-start.2
  4.6 0.9 %copy-start.4 = (bf16[512,256]{1,0:T(8,128)(2,1)S(1)}, bf16[512,256]{1,0:T(8,128)(2,1)}, u32[]{:S(2)}) copy-start(bf16[512,256]{1,0:T(8,128)(2,1)} %refs_1_.1) | copy-start | bytes 786436
  5.5 0.9 copy-start.5
  6.4 0.7 copy-start.9
  7.1 0.7 copy-start.11
  8.5 10.9 %collective-permute-start = (bf16[400,256]{1,0:T(8,128)(2,1)S(1)}, bf16[400,256]{1,0:T(8,128)(2,1)S(1)}, u32[]{:S(2)}, u32[]{:S(2)}) collective-permute-start(bf16[400,256]{1,0:T(8,128)(2,1)S(1)} %get-tuple-element.31), channel_id=1, source_target_pairs={{0,1},{1,0},{2,3},{3,2},{4,5},{5,4},{6,7},{7,6},{8,9},{9,8},{10,11... | collective-permute-start | bytes 614408 | tf_op jit(solution)/shard_map/ppermute | solution.py:22
  10.1 11.6 %collective-permute-start.1 = (bf16[400,256]{1,0:T(8,128)(2,1)S(1)}, bf16[400,256]{1,0:T(8,128)(2,1)S(1)}, u32[]{:S(2)}, u32[]{:S(2)}) collective-permute-start(bf16[400,256]{1,0:T(8,128)(2,1)S(1)} %get-tuple-element.32), channel_id=1, source_target_pairs={{0,2},{1,3},{2,0},{3,1},{4,6},{5,7},{6,4},{7,5},{8,10},{9,11},{10,... | collective-permute-start | bytes 614408 | tf_op jit(solution)/shard_map/ppermute | solution.py:22
  12.7 11.5 %collective-permute-start.3 = (bf16[4,256,128]{2,1,0:T(8,128)(2,1)}, bf16[4,256,128]{2,1,0:T(8,128)(2,1)S(1)}, u32[]{:S(2)}, u32[]{:S(2)}) collective-permute-start(bf16[4,256,128]{2,1,0:T(8,128)(2,1)} %refs_4_.1), channel_id=1, source_target_pairs={{0,24},{4,28},{8,16},{12,20},{16,8},{20,12},{24,0},{28,4},{1,25},{... | collective-permute-start | bytes 786440 | tf_op jit(solution)/shard_map/ppermute | solution.py:22
  14.2 11.5 %collective-permute-start.4 = (bf16[4,256,128]{2,1,0:T(8,128)(2,1)}, bf16[4,256,128]{2,1,0:T(8,128)(2,1)S(1)}, u32[]{:S(2)}, u32[]{:S(2)}) collective-permute-start(bf16[4,256,128]{2,1,0:T(8,128)(2,1)} %refs_4_.1), channel_id=1, source_target_pairs={{0,8},{4,12},{8,0},{12,4},{16,24},{20,28},{24,16},{28,20},{1,9},{5... | collective-permute-start | bytes 786440 | tf_op jit(solution)/shard_map/ppermute | solution.py:22
  19.4 11.2 %collective-permute-start.7 = (bf16[4,256,128]{2,1,0:T(8,128)(2,1)}, bf16[4,256,128]{2,1,0:T(8,128)(2,1)S(1)}, u32[]{:S(2)}, u32[]{:S(2)}) collective-permute-start(bf16[4,256,128]{2,1,0:T(8,128)(2,1)} %refs_4_.1), channel_id=1, source_target_pairs={{0,4},{4,0},{8,12},{12,8},{16,20},{20,16},{24,28},{28,24},{1,5},{5... | collective-permute-start | bytes 786440 | tf_op jit(solution)/shard_map/ppermute | solution.py:22
  19.4 12.6 %collective-permute-start.10 = (bf16[4,256,128]{2,1,0:T(8,128)(2,1)S(1)}, bf16[4,256,128]{2,1,0:T(8,128)(2,1)S(1)}, u32[]{:S(2)}, u32[]{:S(2)}) collective-permute-start(bf16[4,256,128]{2,1,0:T(8,128)(2,1)S(1)} %collective-permute-done.5.refs_8_.refs_7_), channel_id=1, source_target_pairs={{0,4},{4,0},{8,12},{12,8},{16,20},{20,16},{24,28},{28,24},{1,5},{5... | collective-permute-start | bytes 786440 | tf_op jit(solution)/shard_map/ppermute | solution.py:22
  21.7 7.6 %collective-permute-start.2 = (bf16[400,256]{1,0:T(8,128)(2,1)S(1)}, bf16[400,256]{1,0:T(8,128)(2,1)S(1)}, u32[]{:S(2)}, u32[]{:S(2)}) collective-permute-start(bf16[400,256]{1,0:T(8,128)(2,1)S(1)} %get-tuple-element.33), channel_id=1, source_target_pairs={{0,3},{1,2},{2,1},{3,0},{4,7},{5,6},{6,5},{7,4},{8,11},{9,10},{10,... | collective-permute-start | bytes 614408 | tf_op jit(solution)/shard_map/ppermute | solution.py:22
  24.2 9.3 %collective-permute-start.8 = (bf16[4,256,128]{2,1,0:T(8,128)(2,1)S(1)}, bf16[4,256,128]{2,1,0:T(8,128)(2,1)S(1)}, u32[]{:S(2)}, u32[]{:S(2)}) collective-permute-start(bf16[4,256,128]{2,1,0:T(8,128)(2,1)S(1)} %collective-permute-done.3.refs_6_.refs_5_), channel_id=1, source_target_pairs={{0,4},{4,0},{8,12},{12,8},{16,20},{20,16},{24,28},{28,24},{1,5},{5... | collective-permute-start | bytes 786440 | tf_op jit(solution)/shard_map/ppermute | solution.py:22
  25.7 7.8 %collective-permute-start.9 = (bf16[4,256,128]{2,1,0:T(8,128)(2,1)S(1)}, bf16[4,256,128]{2,1,0:T(8,128)(2,1)S(1)}, u32[]{:S(2)}, u32[]{:S(2)}) collective-permute-start(bf16[4,256,128]{2,1,0:T(8,128)(2,1)S(1)} %collective-permute-done.4.refs_7_.refs_6_), channel_id=1, source_target_pairs={{0,4},{4,0},{8,12},{12,8},{16,20},{20,16},{24,28},{28,24},{1,5},{5... | collective-permute-start | bytes 786440 | tf_op jit(solution)/shard_map/ppermute | solution.py:22
  29.9 9.9 %collective-permute-start.14 = (bf16[144,1024]{1,0:T(8,128)(2,1)S(1)}, bf16[144,1024]{1,0:T(8,128)(2,1)S(1)}, u32[]{:S(2)}, u32[]{:S(2)}) collective-permute-start(bf16[144,1024]{1,0:T(8,128)(2,1)S(1)} %get-tuple-element.35.refs_4_), channel_id=1, source_target_pairs={{0,16},{4,20},{8,24},{12,28},{16,0},{20,4},{24,8},{28,12},{1,17},{... | collective-permute-start | bytes 884744 | tf_op jit(solution)/shard_map/ppermute | solution.py:22
  30.6 15.9 %collective-permute-start.13 = (bf16[144,1024]{1,0:T(8,128)(2,1)S(1)}, bf16[144,1024]{1,0:T(8,128)(2,1)S(1)}, u32[]{:S(2)}, u32[]{:S(2)}) collective-permute-start(bf16[144,1024]{1,0:T(8,128)(2,1)S(1)} %get-tuple-element.35.refs_4_), channel_id=1, source_target_pairs={{0,8},{4,12},{8,0},{12,4},{16,24},{20,28},{24,16},{28,20},{1,9},{5... | collective-permute-start | bytes 884744 | tf_op jit(solution)/shard_map/ppermute | solution.py:22
  32.0 14.9 %collective-permute-start.6 = (bf16[144,1024]{1,0:T(8,128)(2,1)S(1)}, bf16[144,1024]{1,0:T(8,128)(2,1)S(1)}, u32[]{:S(2)}, u32[]{:S(2)}) collective-permute-start(bf16[144,1024]{1,0:T(8,128)(2,1)S(1)} %get-tuple-element.35.refs_4_), channel_id=1, source_target_pairs={{0,24},{4,28},{8,16},{12,20},{16,8},{20,12},{24,0},{28,4},{1,25},{... | collective-permute-start | bytes 884744 | tf_op jit(solution)/shard_map/ppermute | solution.py:22
  33.5 1.0 %copy-start = (bf16[4,256,128]{2,1,0:T(8,128)(2,1)S(1)}, bf16[4,256,128]{2,1,0:T(8,128)(2,1)}, u32[]{:S(2)}) copy-start(bf16[4,256,128]{2,1,0:T(8,128)(2,1)} %refs_4_.1) | copy-start | bytes 786436
  36.3 7.1 %collective-permute-start.11 = (bf16[256,256]{1,0:T(8,128)(2,1)S(1)}, bf16[256,256]{1,0:T(8,128)(2,1)S(1)}, u32[]{:S(2)}, u32[]{:S(2)}) collective-permute-start(bf16[256,256]{1,0:T(8,128)(2,1)S(1)} %get-tuple-element.37.refs_0_), channel_id=1, source_target_pairs={{0,1},{1,0},{2,3},{3,2},{4,5},{5,4},{6,7},{7,6},{8,9},{9,8},{10,11... | collective-permute-start | bytes 393224 | tf_op jit(solution)/shard_map/ppermute | solution.py:22
  39.2 7.3 %collective-permute-start.12 = (bf16[256,256]{1,0:T(8,128)(2,1)S(1)}, bf16[256,256]{1,0:T(8,128)(2,1)S(1)}, u32[]{:S(2)}, u32[]{:S(2)}) collective-permute-start(bf16[256,256]{1,0:T(8,128)(2,1)S(1)} %get-tuple-element.37.refs_0_), channel_id=1, source_target_pairs={{0,2},{1,3},{2,0},{3,1},{4,6},{5,7},{6,4},{7,5},{8,10},{9,11},{10,... | collective-permute-start | bytes 393224 | tf_op jit(solution)/shard_map/ppermute | solution.py:22
  39.9 8.7 %collective-permute-start.15 = (bf16[144,1024]{1,0:T(8,128)(2,1)S(1)}, bf16[144,1024]{1,0:T(8,128)(2,1)S(1)}, u32[]{:S(2)}, u32[]{:S(2)}) collective-permute-start(bf16[144,1024]{1,0:T(8,128)(2,1)S(1)} %get-tuple-element.35.refs_4_), channel_id=1, source_target_pairs={{0,4},{4,0},{8,12},{12,8},{16,20},{20,16},{24,28},{28,24},{1,5},{5... | collective-permute-start | bytes 884744 | tf_op jit(solution)/shard_map/ppermute | solution.py:22
  46.4 2.1 %collective-permute-start.18 = (bf16[144,1024]{1,0:T(8,128)(2,1)S(1)}, bf16[144,1024]{1,0:T(8,128)(2,1)S(1)}, u32[]{:S(2)}, u32[]{:S(2)}) collective-permute-start(bf16[144,1024]{1,0:T(8,128)(2,1)S(1)} %collective-permute-done.14.refs_7_), channel_id=1, source_target_pairs={{0,4},{4,0},{8,12},{12,8},{16,20},{20,16},{24,28},{28,24},{1,5},{5... | collective-permute-start | bytes 884744 | tf_op jit(solution)/shard_map/ppermute | solution.py:22
  46.4 2.1 %collective-permute-start.17 = (bf16[144,1024]{1,0:T(8,128)(2,1)S(1)}, bf16[144,1024]{1,0:T(8,128)(2,1)S(1)}, u32[]{:S(2)}, u32[]{:S(2)}) collective-permute-start(bf16[144,1024]{1,0:T(8,128)(2,1)S(1)} %collective-permute-done.13.refs_6_), channel_id=1, source_target_pairs={{0,4},{4,0},{8,12},{12,8},{16,20},{20,16},{24,28},{28,24},{1,5},{5... | collective-permute-start | bytes 884744 | tf_op jit(solution)/shard_map/ppermute | solution.py:22
  46.9 1.9 %collective-permute-start.16 = (bf16[144,1024]{1,0:T(8,128)(2,1)S(1)}, bf16[144,1024]{1,0:T(8,128)(2,1)S(1)}, u32[]{:S(2)}, u32[]{:S(2)}) collective-permute-start(bf16[144,1024]{1,0:T(8,128)(2,1)S(1)} %collective-permute-done.6.refs_5_), channel_id=1, source_target_pairs={{0,4},{4,0},{8,12},{12,8},{16,20},{20,16},{24,28},{28,24},{1,5},{5... | collective-permute-start | bytes 884744 | tf_op jit(solution)/shard_map/ppermute | solution.py:22
  47.0 8.6 %collective-permute-start.19 = (bf16[256,256]{1,0:T(8,128)(2,1)S(1)}, bf16[256,256]{1,0:T(8,128)(2,1)S(1)}, u32[]{:S(2)}, u32[]{:S(2)}) collective-permute-start(bf16[256,256]{1,0:T(8,128)(2,1)S(1)} %get-tuple-element.37.refs_0_), channel_id=1, source_target_pairs={{0,3},{1,2},{2,1},{3,0},{4,7},{5,6},{6,5},{7,4},{8,11},{9,10},{10,... | collective-permute-start | bytes 393224 | tf_op jit(solution)/shard_map/ppermute | solution.py:22
  51.1 9.9 %copy-start.6 = (s32[4096]{0:T(1024)S(1)}, s32[4096]{0:T(1024)}, u32[]{:S(2)}) copy-start(s32[4096]{0:T(1024)} %param.15) | copy-start | bytes 49156
  51.1 9.9 %copy-start.7 = (s32[4096]{0:T(1024)S(1)}, s32[4096]{0:T(1024)}, u32[]{:S(2)}) copy-start(s32[4096]{0:T(1024)} %param.16) | copy-start | bytes 49156
  51.1 9.9 %copy-start.8 = (f32[4096]{0:T(1024)S(1)}, f32[4096]{0:T(1024)}, u32[]{:S(2)}) copy-start(f32[4096]{0:T(1024)} %param.17) | copy-start | bytes 49156
  51.2 12.5 %copy-start.1 = (bf16[4,256,128]{2,1,0:T(8,128)(2,1)S(1)}, bf16[4,256,128]{2,1,0:T(8,128)(2,1)}, u32[]{:S(2)}) copy-start(bf16[4,256,128]{2,1,0:T(8,128)(2,1)} %refs_4_.1) | copy-start | bytes 786436
  51.2 14.3 %collective-permute-start.20 = (bf16[64,1024]{1,0:T(8,128)(2,1)S(1)}, bf16[64,1024]{1,0:T(8,128)(2,1)S(1)}, u32[]{:S(2)}, u32[]{:S(2)}) collective-permute-start(bf16[64,1024]{1,0:T(8,128)(2,1)S(1)} %get-tuple-element.48), channel_id=1, source_target_pairs={{0,1},{1,0},{2,3},{3,2},{4,5},{5,4},{6,7},{7,6},{8,9},{9,8},{10,11... | collective-permute-start | bytes 393224 | tf_op jit(solution)/shard_map/ppermute | solution.py:22
  51.6 14.0 %collective-permute-start.21 = (bf16[64,1024]{1,0:T(8,128)(2,1)S(1)}, bf16[64,1024]{1,0:T(8,128)(2,1)S(1)}, u32[]{:S(2)}, u32[]{:S(2)}) collective-permute-start(bf16[64,1024]{1,0:T(8,128)(2,1)S(1)} %get-tuple-element.49), channel_id=1, source_target_pairs={{0,2},{1,3},{2,0},{3,1},{4,6},{5,7},{6,4},{7,5},{8,10},{9,11},{10,... | collective-permute-start | bytes 393224 | tf_op jit(solution)/shard_map/ppermute | solution.py:22
  53.8 11.7 %collective-permute-start.22 = (bf16[64,1024]{1,0:T(8,128)(2,1)S(1)}, bf16[64,1024]{1,0:T(8,128)(2,1)S(1)}, u32[]{:S(2)}, u32[]{:S(2)}) collective-permute-start(bf16[64,1024]{1,0:T(8,128)(2,1)S(1)} %get-tuple-element.50), channel_id=1, source_target_pairs={{0,3},{1,2},{2,1},{3,0},{4,7},{5,6},{6,5},{7,4},{8,11},{9,10},{10,... | collective-permute-start | bytes 393224 | tf_op jit(solution)/shard_map/ppermute | solution.py:22
  58.4 7.1 %copy-start.3 = (f32[64,256]{1,0:T(8,128)S(1)}, f32[64,256]{1,0:T(8,128)}, u32[]{:S(2)}) copy-start(f32[64,256]{1,0:T(8,128)} %refs_0_.3) | copy-start | bytes 196612
  58.4 7.1 %copy-start.10 = (s32[64,1]{0,1:T(1,128)S(1)}, s32[64,1]{0,1:T(1,128)}, u32[]{:S(2)}) copy-start(s32[64,1]{0,1:T(1,128)} %param.13) | copy-start | bytes 772
  58.4 7.1 %copy-start.12 = (s32[256,1]{0,1:T(1,128)S(1)}, s32[256,1]{0,1:T(1,128)}, u32[]{:S(2)}) copy-start(s32[256,1]{0,1:T(1,128)} %param.14) | copy-start | bytes 3076
  58.4 10.6 %collective-permute-start.23 = (bf16[64,1024]{1,0:T(8,128)(2,1)S(1)}, bf16[64,1024]{1,0:T(8,128)(2,1)S(1)}, u32[]{:S(2)}, u32[]{:S(2)}) collective-permute-start(bf16[64,1024]{1,0:T(8,128)(2,1)S(1)} %get-tuple-element.52), channel_id=1, source_target_pairs={{0,1},{1,0},{2,3},{3,2},{4,5},{5,4},{6,7},{7,6},{8,9},{9,8},{10,11... | collective-permute-start | bytes 393224 | tf_op jit(solution)/shard_map/ppermute | solution.py:22
  59.5 13.1 %collective-permute-start.24 = (bf16[64,1024]{1,0:T(8,128)(2,1)S(1)}, bf16[64,1024]{1,0:T(8,128)(2,1)S(1)}, u32[]{:S(2)}, u32[]{:S(2)}) collective-permute-start(bf16[64,1024]{1,0:T(8,128)(2,1)S(1)} %get-tuple-element.53), channel_id=1, source_target_pairs={{0,2},{1,3},{2,0},{3,1},{4,6},{5,7},{6,4},{7,5},{8,10},{9,11},{10,... | collective-permute-start | bytes 393224 | tf_op jit(solution)/shard_map/ppermute | solution.py:22
  72.7 1.2 %collective-permute-start.26 = (f32[8,128]{1,0:T(8,128)S(1)}, f32[8,128]{1,0:T(8,128)S(1)}, u32[]{:S(2)}, u32[]{:S(2)}) collective-permute-start(f32[8,128]{1,0:T(8,128)S(1)} %get-tuple-element.57), channel_id=1, source_target_pairs={{0,4},{4,0},{8,12},{12,8},{16,20},{20,16},{24,28},{28,24},{1,5},{5... | collective-permute-start | bytes 12296 | tf_op jit(solution)/shard_map/ppermute | solution.py:22
  73.9 5.8 %collective-permute-start.27 = (f32[8,128]{1,0:T(8,128)S(1)}, f32[8,128]{1,0:T(8,128)S(1)}, u32[]{:S(2)}, u32[]{:S(2)}) collective-permute-start(f32[8,128]{1,0:T(8,128)S(1)} %select_add_fusion.refs_4_), channel_id=1, source_target_pairs={{0,1},{1,0},{2,3},{3,2},{4,5},{5,4},{6,7},{7,6},{8,9},{9,8},{10,11... | collective-permute-start | bytes 12296 | tf_op jit(solution)/shard_map/ppermute | solution.py:22
  75.6 4.5 %collective-permute-start.28 = (f32[8,128]{1,0:T(8,128)S(1)}, f32[8,128]{1,0:T(8,128)S(1)}, u32[]{:S(2)}, u32[]{:S(2)}) collective-permute-start(f32[8,128]{1,0:T(8,128)S(1)} %select_add_fusion.refs_4_), channel_id=1, source_target_pairs={{0,2},{1,3},{2,0},{3,1},{4,6},{5,7},{6,4},{7,5},{8,10},{9,11},{10,... | collective-permute-start | bytes 12296 | tf_op jit(solution)/shard_map/ppermute | solution.py:22
  75.8 5.5 %collective-permute-start.29 = (f32[8,128]{1,0:T(8,128)S(1)}, f32[8,128]{1,0:T(8,128)S(1)}, u32[]{:S(2)}, u32[]{:S(2)}) collective-permute-start(f32[8,128]{1,0:T(8,128)S(1)} %select_add_fusion.refs_4_), channel_id=1, source_target_pairs={{0,3},{1,2},{2,1},{3,0},{4,7},{5,6},{6,5},{7,4},{8,11},{9,10},{10,... | collective-permute-start | bytes 12296 | tf_op jit(solution)/shard_map/ppermute | solution.py:22
  78.3 6.8 %collective-permute-start.25 = (bf16[64,1024]{1,0:T(8,128)(2,1)S(1)}, bf16[64,1024]{1,0:T(8,128)(2,1)S(1)}, u32[]{:S(2)}, u32[]{:S(2)}) collective-permute-start(bf16[64,1024]{1,0:T(8,128)(2,1)S(1)} %get-tuple-element.54), channel_id=1, source_target_pairs={{0,3},{1,2},{2,1},{3,0},{4,7},{5,6},{6,5},{7,4},{8,11},{9,10},{10,... | collective-permute-start | bytes 393224 | tf_op jit(solution)/shard_map/ppermute | solution.py:22
  81.4 7.5 %collective-permute-start.30 = (f32[8,128]{1,0:T(8,128)S(1)}, f32[8,128]{1,0:T(8,128)S(1)}, u32[]{:S(2)}, u32[]{:S(2)}) collective-permute-start(f32[8,128]{1,0:T(8,128)S(1)} %add_add_fusion.refs_8_), channel_id=1, source_target_pairs={{0,24},{4,28},{8,16},{12,20},{16,8},{20,12},{24,0},{28,4},{1,25},{... | collective-permute-start | bytes 12296 | tf_op jit(solution)/shard_map/ppermute | solution.py:22
  82.8 6.1 %collective-permute-start.31 = (f32[8,128]{1,0:T(8,128)S(1)}, f32[8,128]{1,0:T(8,128)S(1)}, u32[]{:S(2)}, u32[]{:S(2)}) collective-permute-start(f32[8,128]{1,0:T(8,128)S(1)} %add_add_fusion.refs_8_), channel_id=1, source_target_pairs={{0,8},{4,12},{8,0},{12,4},{16,24},{20,28},{24,16},{28,20},{1,9},{5... | collective-permute-start | bytes 12296 | tf_op jit(solution)/shard_map/ppermute | solution.py:22
  83.3 5.5 %collective-permute-start.32 = (f32[8,128]{1,0:T(8,128)S(1)}, f32[8,128]{1,0:T(8,128)S(1)}, u32[]{:S(2)}, u32[]{:S(2)}) collective-permute-start(f32[8,128]{1,0:T(8,128)S(1)} %add_add_fusion.refs_8_), channel_id=1, source_target_pairs={{0,16},{4,20},{8,24},{12,28},{16,0},{20,4},{24,8},{28,12},{1,17},{... | collective-permute-start | bytes 12296 | tf_op jit(solution)/shard_map/ppermute | solution.py:22

commit v5 on v4

--- a/solution.py
+++ b/solution.py
@@ -418,11 +418,11 @@
         [populations, column, owner_row, partner_row, pick, move, drain] + rates,
     )
     if small:
-        row_of = lax.broadcasted_iota(jnp.int32, (TILE, LANES), 0)
-        news = after(news, later_rates[1], later_rates[2])
-        news = news + jnp.where(row_of == COLUMN_ROW, swap(news, "cells", 1, nc), 0.0)
+        news = after(news, later_rates[1], later_rates[3])
     news = others(news, ne)
     column = sum(news[1:], news[0])
+    if small:
+        column = column + swap(column, "cells", 1, nc)
     columns = chips(column) if small else [lax.psum(column, "cells")]
     (terms,) = call(
         second_kernel,

time: 90.8 us -> 90.3 us (level)
  waiting for transfers between devices: 25.7 us -> 19.6 us
  starting transfers between devices: 37.3 us -> 42.9 us
    ppermute x33, waiting for transfers between devices: 25.7 us -> 19.6 us  [swap(): return lax.ppermute(x, axis, [(i, i ^ mask) for i in range(count)])]
    ppermute x33, starting transfers between devices: 37.3 us -> 42.9 us  [swap(): return lax.ppermute(x, axis, [(i, i ^ mask) for i in range(count)])]
  transfers between devices with their start and end apart: 33 -> 33, of which waited for: 13 -> 10; matrix products, arithmetic and copies ran while one was open for 0% -> 0% of each run, Pallas kernels for 22% -> 22%
where the time goes in v5:
time: 90.3 us; the launch traced here: 90 us
  starting transfers between devices  42.9 us (48%)
  Pallas kernels  21.5 us (24%)
  waiting for transfers between devices  19.6 us (22%)
  local copies, waits for them, and re-layouts  5.1 us (6%)
    ppermute x33, starting transfers between devices, swap(): return lax.ppermute(x, axis, [(i, i ^ mask) for i in range(count)])  42.9 us
    pallas_call x10, Pallas kernels, call(): pl.pallas_call(whole, out_shape=tuple((jax.ShapeDtypeStruct(s, t) for s,...  21.5 us
    ppermute x33, waiting for transfers between devices, swap(): return lax.ppermute(x, axis, [(i, i ^ mask) for i in range(count)])  19.6 us
    unnamed x26, local copies, waits for them, and re-layouts  5.01 us
  transfers between devices with their start and end apart: 33, of which 10 were waited for; matrix products, arithmetic and copies ran while one was open for 0% of the time, Pallas kernels for 22%

profile of v5, /device:TPU:0, one launch (start us, length us, event | category | flops | bytes accessed | tf_op | source)
XLA Modules:
  0.0 90.0 jit_solution(7520213809095870288)
XLA Ops:
  0.6 3.0 %collective-permute-start.5 = (bf16[4,256,128]{2,1,0:T(8,128)(2,1)}, bf16[4,256,128]{2,1,0:T(8,128)(2,1)S(1)}, u32[]{:S(2)}, u32[]{:S(2)}) collective-permute-start(bf16[4,256,128]{2,1,0:T(8,128)(2,1)} %refs_4_.1), channel_id=1, source_target_pairs={{0,16},{4,20},{8,24},{12,28},{16,0},{20,4},{24,8},{28,12},{1,17},{... | collective-permute-start | bytes 786440 | tf_op jit(solution)/shard_map/ppermute | solution.py:22
  3.7 0.1 stack.40.ints_ref
  3.7 0.8 copy-done.2
  4.6 0.9 %copy-done.4 = bf16[512,256]{1,0:T(8,128)(2,1)S(1)} copy-done((bf16[512,256]{1,0:T(8,128)(2,1)S(1)}, bf16[512,256]{1,0:T(8,128)(2,1)}, u32[]{:S(2)}) %copy-start.4) | copy-done | bytes 262168
  5.5 0.9 %copy-done.5 = bf16[256,256]{1,0:T(8,128)(2,1)S(1)} copy-done((bf16[256,256]{1,0:T(8,128)(2,1)S(1)}, bf16[256,256]{1,0:T(8,128)(2,1)}, u32[]{:S(2)}) %copy-start.5) | copy-done | bytes 131096
  6.4 0.7 copy-done.9
  7.1 0.7 copy-done.11
  7.8 0.7 shard_map.104
  8.5 1.6 %collective-permute-start = (bf16[400,256]{1,0:T(8,128)(2,1)S(1)}, bf16[400,256]{1,0:T(8,128)(2,1)S(1)}, u32[]{:S(2)}, u32[]{:S(2)}) collective-permute-start(bf16[400,256]{1,0:T(8,128)(2,1)S(1)} %get-tuple-element.31), channel_id=1, source_target_pairs={{0,1},{1,0},{2,3},{3,2},{4,5},{5,4},{6,7},{7,6},{8,9},{9,8},{10,11... | collective-permute-start | bytes 614408 | tf_op jit(solution)/shard_map/ppermute | solution.py:22
  10.1 2.6 %collective-permute-start.1 = (bf16[400,256]{1,0:T(8,128)(2,1)S(1)}, bf16[400,256]{1,0:T(8,128)(2,1)S(1)}, u32[]{:S(2)}, u32[]{:S(2)}) collective-permute-start(bf16[400,256]{1,0:T(8,128)(2,1)S(1)} %get-tuple-element.32), channel_id=1, source_target_pairs={{0,2},{1,3},{2,0},{3,1},{4,6},{5,7},{6,4},{7,5},{8,10},{9,11},{10,... | collective-permute-start | bytes 614408 | tf_op jit(solution)/shard_map/ppermute | solution.py:22
  12.7 1.5 %collective-permute-start.4 = (bf16[4,256,128]{2,1,0:T(8,128)(2,1)}, bf16[4,256,128]{2,1,0:T(8,128)(2,1)S(1)}, u32[]{:S(2)}, u32[]{:S(2)}) collective-permute-start(bf16[4,256,128]{2,1,0:T(8,128)(2,1)} %refs_4_.1), channel_id=1, source_target_pairs={{0,8},{4,12},{8,0},{12,4},{16,24},{20,28},{24,16},{28,20},{1,9},{5... | collective-permute-start | bytes 786440 | tf_op jit(solution)/shard_map/ppermute | solution.py:22
  14.2 0.5 collective-permute-start.3
  14.7 4.7 %collective-permute-done.refs_1_.refs_2_ = bf16[400,256]{1,0:T(8,128)(2,1)S(1)} collective-permute-done((bf16[400,256]{1,0:T(8,128)(2,1)S(1)}, bf16[400,256]{1,0:T(8,128)(2,1)S(1)}, u32[]{:S(2)}, u32[]{:S(2)}) %collective-permute-start) | collective-permute-done | bytes 204832 | tf_op jit(solution)/shard_map/ppermute | solution.py:22
  19.4 0.5 collective-permute-start.10
  19.9 1.8 %collective-permute-done.1.refs_2_.refs_3_ = bf16[400,256]{1,0:T(8,128)(2,1)S(1)} collective-permute-done((bf16[400,256]{1,0:T(8,128)(2,1)S(1)}, bf16[400,256]{1,0:T(8,128)(2,1)S(1)}, u32[]{:S(2)}, u32[]{:S(2)}) %collective-permute-start.1) | collective-permute-done | bytes 204832 | tf_op jit(solution)/shard_map/ppermute | solution.py:22
  21.7 2.5 %collective-permute-start.2 = (bf16[400,256]{1,0:T(8,128)(2,1)S(1)}, bf16[400,256]{1,0:T(8,128)(2,1)S(1)}, u32[]{:S(2)}, u32[]{:S(2)}) collective-permute-start(bf16[400,256]{1,0:T(8,128)(2,1)S(1)} %get-tuple-element.33), channel_id=1, source_target_pairs={{0,3},{1,2},{2,1},{3,0},{4,7},{5,6},{6,5},{7,4},{8,11},{9,10},{10,... | collective-permute-start | bytes 614408 | tf_op jit(solution)/shard_map/ppermute | solution.py:22
  24.2 0.0 collective-permute-done.4.refs_7_.refs_6_
  24.2 0.0 collective-permute-start.9
  24.2 1.5 %collective-permute-done.3.refs_6_.refs_5_ = bf16[4,256,128]{2,1,0:T(8,128)(2,1)S(1)} collective-permute-done((bf16[4,256,128]{2,1,0:T(8,128)(2,1)}, bf16[4,256,128]{2,1,0:T(8,128)(2,1)S(1)}, u32[]{:S(2)}, u32[]{:S(2)}) %collective-permute-start.3) | collective-permute-done | bytes 262176 | tf_op jit(solution)/shard_map/ppermute | solution.py:22
  25.7 0.0 collective-permute-start.8
  25.7 3.6 %collective-permute-done.2.refs_3_.refs_4_ = bf16[400,256]{1,0:T(8,128)(2,1)S(1)} collective-permute-done((bf16[400,256]{1,0:T(8,128)(2,1)S(1)}, bf16[400,256]{1,0:T(8,128)(2,1)S(1)}, u32[]{:S(2)}, u32[]{:S(2)}) %collective-permute-start.2) | collective-permute-done | bytes 204832 | tf_op jit(solution)/shard_map/ppermute | solution.py:22
  29.4 0.6 shard_map.105
  29.9 0.6 collective-permute-start.14
  30.6 1.4 %collective-permute-start.13 = (bf16[144,1024]{1,0:T(8,128)(2,1)S(1)}, bf16[144,1024]{1,0:T(8,128)(2,1)S(1)}, u32[]{:S(2)}, u32[]{:S(2)}) collective-permute-start(bf16[144,1024]{1,0:T(8,128)(2,1)S(1)} %get-tuple-element.35.refs_4_), channel_id=1, source_target_pairs={{0,8},{4,12},{8,0},{12,4},{16,24},{20,28},{24,16},{28,20},{1,9},{5... | collective-permute-start | bytes 884744 | tf_op jit(solution)/shard_map/ppermute | solution.py:22
  32.0 0.0 collective-permute-done.10.refs_12_.refs_11_
  32.0 1.5 %collective-permute-start.6 = (bf16[144,1024]{1,0:T(8,128)(2,1)S(1)}, bf16[144,1024]{1,0:T(8,128)(2,1)S(1)}, u32[]{:S(2)}, u32[]{:S(2)}) collective-permute-start(bf16[144,1024]{1,0:T(8,128)(2,1)S(1)} %get-tuple-element.35.refs_4_), channel_id=1, source_target_pairs={{0,24},{4,28},{8,16},{12,20},{16,8},{20,12},{24,0},{28,4},{1,25},{... | collective-permute-start | bytes 884744 | tf_op jit(solution)/shard_map/ppermute | solution.py:22
  33.5 0.0 collective-permute-done.9.refs_11_.refs_10_
  33.5 0.0 collective-permute-done.8.refs_10_.refs_9_
  33.5 0.9 %copy-done = bf16[4,256,128]{2,1,0:T(8,128)(2,1)S(1)} copy-done((bf16[4,256,128]{2,1,0:T(8,128)(2,1)S(1)}, bf16[4,256,128]{2,1,0:T(8,128)(2,1)}, u32[]{:S(2)}) %copy-start) | copy-done | bytes 262168
  34.4 1.8 %shard_map.106 = (f32[256,256]{1,0:T(8,128)S(1)}, bf16[256,256]{1,0:T(8,128)(2,1)S(1)}) custom-call(s32[10]{0:T(128)S(1)} %stack.40.ints_ref, f32[32,128]{1,0:T(8,128)S(1)} %get-tuple-element.36.refs_0_, bf16[400,256]{1,0:T(8,128)(2,1)S(1)} %get-tuple-element.30.refs_0_.refs_1_, bf16[400,256]{1,0:T(8,128)(2,1)S(1)} %collective-permute-done.refs_1_.refs_2_, ...), custom_call_target="tpu_custom_call" | custom-call | tf_op jit(solution)/shard_map/pallas_call | solution.py:74
  36.3 2.9 %collective-permute-start.12 = (bf16[256,256]{1,0:T(8,128)(2,1)S(1)}, bf16[256,256]{1,0:T(8,128)(2,1)S(1)}, u32[]{:S(2)}, u32[]{:S(2)}) collective-permute-start(bf16[256,256]{1,0:T(8,128)(2,1)S(1)} %get-tuple-element.37.refs_0_), channel_id=1, source_target_pairs={{0,2},{1,3},{2,0},{3,1},{4,6},{5,7},{6,4},{7,5},{8,10},{9,11},{10,... | collective-permute-start | bytes 393224 | tf_op jit(solution)/shard_map/ppermute | solution.py:22
  39.2 0.2 collective-permute-start.11
  39.4 0.5 collective-permute-done.14.refs_7_
  39.9 0.0 collective-permute-start.15
  39.9 2.6 %collective-permute-done.12.refs_2_ = bf16[256,256]{1,0:T(8,128)(2,1)S(1)} collective-permute-done((bf16[256,256]{1,0:T(8,128)(2,1)S(1)}, bf16[256,256]{1,0:T(8,128)(2,1)S(1)}, u32[]{:S(2)}, u32[]{:S(2)}) %collective-permute-start.12) | collective-permute-done | bytes 131104 | tf_op jit(solution)/shard_map/ppermute | solution.py:22
  42.4 1.7 %collective-permute-done.11.refs_1_ = bf16[256,256]{1,0:T(8,128)(2,1)S(1)} collective-permute-done((bf16[256,256]{1,0:T(8,128)(2,1)S(1)}, bf16[256,256]{1,0:T(8,128)(2,1)S(1)}, u32[]{:S(2)}, u32[]{:S(2)}) %collective-permute-start.11) | collective-permute-done | bytes 131104 | tf_op jit(solution)/shard_map/ppermute | solution.py:22
  44.2 0.0 collective-permute-done.13.refs_6_
  44.2 0.5 collective-permute-start.17
  44.7 0.1 collective-permute-start.18
  44.8 2.7 %collective-permute-start.19 = (bf16[256,256]{1,0:T(8,128)(2,1)S(1)}, bf16[256,256]{1,0:T(8,128)(2,1)S(1)}, u32[]{:S(2)}, u32[]{:S(2)}) collective-permute-start(bf16[256,256]{1,0:T(8,128)(2,1)S(1)} %get-tuple-element.37.refs_0_), channel_id=1, source_target_pairs={{0,3},{1,2},{2,1},{3,0},{4,7},{5,6},{6,5},{7,4},{8,11},{9,10},{10,... | collective-permute-start | bytes 393224 | tf_op jit(solution)/shard_map/ppermute | solution.py:22
  47.5 2.3 %shard_map.107 = (bf16[64,1024]{1,0:T(8,128)(2,1)S(1)}, bf16[64,1024]{1,0:T(8,128)(2,1)S(1)}, bf16[64,1024]{1,0:T(8,128)(2,1)S(1)}, bf16[64,1024]{1,0:T(8,128)(2,1)S(1)}, f32[8,128]{1,0:T(8,128)S(1)}) custom-call(s32[10]{0:T(128)S(1)} %stack.40.ints_ref, bf16[400,256]{1,0:T(8,128)(2,1)S(1)} %get-tuple-element.30.refs_0_.refs_1_, ...), custom_call_target="tpu_custom_call" | custom-call | tf_op jit(solution)/shard_map/pallas_call | solution.py:74
  49.8 0.0 copy-start.6
  49.8 0.0 copy-start.7
  49.8 0.0 copy-start.8
  49.8 0.0 copy-start.1
  49.8 2.6 %collective-permute-start.20 = (bf16[64,1024]{1,0:T(8,128)(2,1)S(1)}, bf16[64,1024]{1,0:T(8,128)(2,1)S(1)}, u32[]{:S(2)}, u32[]{:S(2)}) collective-permute-start(bf16[64,1024]{1,0:T(8,128)(2,1)S(1)} %get-tuple-element.48), channel_id=1, source_target_pairs={{0,1},{1,0},{2,3},{3,2},{4,5},{5,4},{6,7},{7,6},{8,9},{9,8},{10,11... | collective-permute-start | bytes 393224 | tf_op jit(solution)/shard_map/ppermute | solution.py:22
  52.4 2.4 %collective-permute-start.22 = (bf16[64,1024]{1,0:T(8,128)(2,1)S(1)}, bf16[64,1024]{1,0:T(8,128)(2,1)S(1)}, u32[]{:S(2)}, u32[]{:S(2)}) collective-permute-start(bf16[64,1024]{1,0:T(8,128)(2,1)S(1)} %get-tuple-element.50), channel_id=1, source_target_pairs={{0,3},{1,2},{2,1},{3,0},{4,7},{5,6},{6,5},{7,4},{8,11},{9,10},{10,... | collective-permute-start | bytes 393224 | tf_op jit(solution)/shard_map/ppermute | solution.py:22
  54.9 2.8 %shard_map.109 = (bf16[64,1024]{1,0:T(8,128)(2,1)S(1)}, bf16[64,1024]{1,0:T(8,128)(2,1)S(1)}, bf16[64,1024]{1,0:T(8,128)(2,1)S(1)}, bf16[64,1024]{1,0:T(8,128)(2,1)S(1)}, f32[8,128]{1,0:T(8,128)}) custom-call(s32[10]{0:T(128)S(1)} %stack.40.ints_ref, bf16[256,256]{1,0:T(8,128)(2,1)S(1)} %get-tuple-element.37.refs_0_, ...), custom_call_target="tpu_custom_call" | custom-call | tf_op jit(solution)/shard_map/pallas_call | solution.py:74
  57.7 1.0 %collective-permute-start.23 = (bf16[64,1024]{1,0:T(8,128)(2,1)S(1)}, bf16[64,1024]{1,0:T(8,128)(2,1)S(1)}, u32[]{:S(2)}, u32[]{:S(2)}) collective-permute-start(bf16[64,1024]{1,0:T(8,128)(2,1)S(1)} %get-tuple-element.52), channel_id=1, source_target_pairs={{0,1},{1,0},{2,3},{3,2},{4,5},{5,4},{6,7},{7,6},{8,9},{9,8},{10,11... | collective-permute-start | bytes 393224 | tf_op jit(solution)/shard_map/ppermute | solution.py:22
  58.7 2.3 %collective-permute-start.25 = (bf16[64,1024]{1,0:T(8,128)(2,1)S(1)}, bf16[64,1024]{1,0:T(8,128)(2,1)S(1)}, u32[]{:S(2)}, u32[]{:S(2)}) collective-permute-start(bf16[64,1024]{1,0:T(8,128)(2,1)S(1)} %get-tuple-element.54), channel_id=1, source_target_pairs={{0,3},{1,2},{2,1},{3,0},{4,7},{5,6},{6,5},{7,4},{8,11},{9,10},{10,... | collective-permute-start | bytes 393224 | tf_op jit(solution)/shard_map/ppermute | solution.py:22
  61.0 2.6 %shard_map.108 = (bf16[8,256,512]{2,1,0:T(8,128)(2,1)S(1)}, bf16[8,256,512]{2,1,0:T(8,128)(2,1)S(1)}, f32[256,256]{1,0:T(8,128)S(1)}) custom-call(s32[10]{0:T(128)S(1)} %stack.40.ints_ref, s32[1,4096]{1,0:T(1,128)S(1)} %bitcast.14, s32[1,4096]{1,0:T(1,128)S(1)} %bitcast.15, f32[1,4096]{1,0:T(1,128)S(1)} %bitcast.16), custom_call_target="tpu_custom_call" | custom-call | tf_op jit(solution)/shard_map/pallas_call | solution.py:74
  63.6 1.9 %shard_map.110.refs_3_ = f32[4,256,256]{2,1,0:T(8,128)S(1)} custom-call(s32[10]{0:T(128)S(1)} %stack.40.ints_ref, bf16[256,256]{1,0:T(8,128)(2,1)S(1)} %get-tuple-element.37.refs_0_, bf16[256,256]{1,0:T(8,128)(2,1)S(1)} %collective-permute-done.11.refs_1_, bf16[256,256]{1,0:T(8,128)(2,1)S(1)} %collective-permute-done.12.refs_2_, ...), custom_call_target="tpu_custom_call" | custom-call | tf_op jit(solution)/shard_map/pallas_call | solution.py:74
  65.6 3.5 %shard_map.111 = (f32[64,256]{1,0:T(8,128)S(1)}, f32[8,128]{1,0:T(8,128)S(1)}) custom-call(s32[10]{0:T(128)S(1)} %stack.40.ints_ref, f32[64,256]{1,0:T(8,128)S(1)} %copy-done.3, f32[8,128]{1,0:T(8,128)S(1)} %get-tuple-element.41.refs_1_, s32[1,64]{1,0:T(1,128)S(1)} %bitcast.18, s32[1,256]{1,0:T(1,128)S(1)} %bitcast.21, ...), custom_call_target="tpu_custom_call" | custom-call | tf_op jit(solution)/shard_map/pallas_call | solution.py:74
  69.1 0.3 collective-permute-done.23.refs_5_
  69.4 1.8 %collective-permute-start.28 = (f32[8,128]{1,0:T(8,128)S(1)}, f32[8,128]{1,0:T(8,128)S(1)}, u32[]{:S(2)}, u32[]{:S(2)}) collective-permute-start(f32[8,128]{1,0:T(8,128)S(1)} %get-tuple-element.57.refs_4_), channel_id=1, source_target_pairs={{0,3},{1,2},{2,1},{3,0},{4,7},{5,6},{6,5},{7,4},{8,11},{9,10},{10,... | collective-permute-start | bytes 12296 | tf_op jit(solution)/shard_map/ppermute | solution.py:22
  71.1 5.2 %collective-permute-start.27 = (f32[8,128]{1,0:T(8,128)S(1)}, f32[8,128]{1,0:T(8,128)S(1)}, u32[]{:S(2)}, u32[]{:S(2)}) collective-permute-start(f32[8,128]{1,0:T(8,128)S(1)} %get-tuple-element.57.refs_4_), channel_id=1, source_target_pairs={{0,2},{1,3},{2,0},{3,1},{4,6},{5,7},{6,4},{7,5},{8,10},{9,11},{10,... | collective-permute-start | bytes 12296 | tf_op jit(solution)/shard_map/ppermute | solution.py:22
  76.3 2.0 %collective-permute-start.24 = (bf16[64,1024]{1,0:T(8,128)(2,1)S(1)}, bf16[64,1024]{1,0:T(8,128)(2,1)S(1)}, u32[]{:S(2)}, u32[]{:S(2)}) collective-permute-start(bf16[64,1024]{1,0:T(8,128)(2,1)S(1)} %get-tuple-element.53), channel_id=1, source_target_pairs={{0,2},{1,3},{2,0},{3,1},{4,6},{5,7},{6,4},{7,5},{8,10},{9,11},{10,... | collective-permute-start | bytes 393224 | tf_op jit(solution)/shard_map/ppermute | solution.py:22
  78.3 1.6 %collective-permute-done.26.refs_5_ = f32[8,128]{1,0:T(8,128)S(1)} collective-permute-done((f32[8,128]{1,0:T(8,128)S(1)}, f32[8,128]{1,0:T(8,128)S(1)}, u32[]{:S(2)}, u32[]{:S(2)}) %collective-permute-start.26) | collective-permute-done | bytes 4128 | tf_op jit(solution)/shard_map/ppermute | solution.py:22
  79.9 1.2 %collective-permute-done.29 = f32[8,128]{1,0:T(8,128)S(1)} collective-permute-done((f32[8,128]{1,0:T(8,128)S(1)}, f32[8,128]{1,0:T(8,128)S(1)}, u32[]{:S(2)}, u32[]{:S(2)}) %collective-permute-start.29) | collective-permute-done | bytes 4128 | tf_op jit(solution)/shard_map/ppermute | solution.py:22
  81.1 0.7 collective-permute-start.32
  81.8 1.3 %collective-permute-start.31 = (f32[8,128]{1,0:T(8,128)S(1)}, f32[8,128]{1,0:T(8,128)S(1)}, u32[]{:S(2)}, u32[]{:S(2)}) collective-permute-start(f32[8,128]{1,0:T(8,128)S(1)} %add.15.refs_8_), channel_id=1, source_target_pairs={{0,8},{4,12},{8,0},{12,4},{16,24},{20,28},{24,16},{28,20},{1,9},{5... | collective-permute-start | bytes 12296 | tf_op jit(solution)/shard_map/ppermute | solution.py:22
  83.1 1.5 %collective-permute-start.30 = (f32[8,128]{1,0:T(8,128)S(1)}, f32[8,128]{1,0:T(8,128)S(1)}, u32[]{:S(2)}, u32[]{:S(2)}) collective-permute-start(f32[8,128]{1,0:T(8,128)S(1)} %add.15.refs_8_), channel_id=1, source_target_pairs={{0,24},{4,28},{8,16},{12,20},{16,8},{20,12},{24,0},{28,4},{1,25},{... | collective-permute-start | bytes 12296 | tf_op jit(solution)/shard_map/ppermute | solution.py:22
  84.6 3.7 %shard_map.112.refs_1_ = f32[3,64,256]{2,1,0:T(8,128)S(1)} custom-call(s32[10]{0:T(128)S(1)} %stack.40.ints_ref, f32[64,256]{1,0:T(8,128)S(1)} %get-tuple-element.51.refs_0_, bf16[8,256,512]{2,1,0:T(8,128)(2,1)S(1)} %get-tuple-element.42.refs_4_.refs_1_, bf16[8,256,512]{2,1,0:T(8,128)(2,1)S(1)} %get-tuple-element.43.refs_5_.refs_2_, ...), custom_call_target="tpu_custom_call" | custom-call | tf_op jit(solution)/shard_map/pallas_call | solution.py:74
  88.4 1.7 %shard_map.113 = (f32[256,256]{1,0:T(8,128)}, f32[64,256]{1,0:T(8,128)}) custom-call(s32[10]{0:T(128)S(1)} %stack.40.ints_ref, s32[1,64]{1,0:T(1,128)S(1)} %bitcast.19, f32[3,64,256]{2,1,0:T(8,128)S(1)} %shard_map.112.refs_1_, f32[256,256]{1,0:T(8,128)S(1)} %get-tuple-element.55.refs_2_, f32[4,256,256]{2,1,0:T(8,128)S(1)} %shard_map.110.refs_3_, ...), custom_call_target="tpu_custom_call" | custom-call | tf_op jit(solution)/shard_map/pallas_call | solution.py:74
  (41 shorter events, 0.1 us)
Async XLA Ops:
  0.6 18.8 %collective-permute-start.5 = (bf16[4,256,128]{2,1,0:T(8,128)(2,1)}, bf16[4,256,128]{2,1,0:T(8,128)(2,1)S(1)}, u32[]{:S(2)}, u32[]{:S(2)}) collective-permute-start(bf16[4,256,128]{2,1,0:T(8,128)(2,1)} %refs_4_.1), channel_id=1, source_target_pairs={{0,16},{4,20},{8,24},{12,28},{16,0},{20,4},{24,8},{28,12},{1,17},{... | collective-permute-start | bytes 786440 | tf_op jit(solution)/shard_map/ppermute | solution.py:22
  3.7 0.8 copy-start.2
  4.6 0.9 %copy-start.4 = (bf16[512,256]{1,0:T(8,128)(2,1)S(1)}, bf16[512,256]{1,0:T(8,128)(2,1)}, u32[]{:S(2)}) copy-start(bf16[512,256]{1,0:T(8,128)(2,1)} %refs_1_.1) | copy-start | bytes 786436
  5.5 0.9 %copy-start.5 = (bf16[256,256]{1,0:T(8,128)(2,1)S(1)}, bf16[256,256]{1,0:T(8,128)(2,1)}, u32[]{:S(2)}) copy-start(bf16[256,256]{1,0:T(8,128)(2,1)} %refs_0_.2) | copy-start | bytes 393220
  6.4 0.7 copy-start.9
  7.1 0.7 copy-start.11
  8.5 10.9 %collective-permute-start = (bf16[400,256]{1,0:T(8,128)(2,1)S(1)}, bf16[400,256]{1,0:T(8,128)(2,1)S(1)}, u32[]{:S(2)}, u32[]{:S(2)}) collective-permute-start(bf16[400,256]{1,0:T(8,128)(2,1)S(1)} %get-tuple-element.31), channel_id=1, source_target_pairs={{0,1},{1,0},{2,3},{3,2},{4,5},{5,4},{6,7},{7,6},{8,9},{9,8},{10,11... | collective-permute-start | bytes 614408 | tf_op jit(solution)/shard_map/ppermute | solution.py:22
  10.1 11.6 %collective-permute-start.1 = (bf16[400,256]{1,0:T(8,128)(2,1)S(1)}, bf16[400,256]{1,0:T(8,128)(2,1)S(1)}, u32[]{:S(2)}, u32[]{:S(2)}) collective-permute-start(bf16[400,256]{1,0:T(8,128)(2,1)S(1)} %get-tuple-element.32), channel_id=1, source_target_pairs={{0,2},{1,3},{2,0},{3,1},{4,6},{5,7},{6,4},{7,5},{8,10},{9,11},{10,... | collective-permute-start | bytes 614408 | tf_op jit(solution)/shard_map/ppermute | solution.py:22
  12.7 11.5 %collective-permute-start.4 = (bf16[4,256,128]{2,1,0:T(8,128)(2,1)}, bf16[4,256,128]{2,1,0:T(8,128)(2,1)S(1)}, u32[]{:S(2)}, u32[]{:S(2)}) collective-permute-start(bf16[4,256,128]{2,1,0:T(8,128)(2,1)} %refs_4_.1), channel_id=1, source_target_pairs={{0,8},{4,12},{8,0},{12,4},{16,24},{20,28},{24,16},{28,20},{1,9},{5... | collective-permute-start | bytes 786440 | tf_op jit(solution)/shard_map/ppermute | solution.py:22
  14.2 11.5 %collective-permute-start.3 = (bf16[4,256,128]{2,1,0:T(8,128)(2,1)}, bf16[4,256,128]{2,1,0:T(8,128)(2,1)S(1)}, u32[]{:S(2)}, u32[]{:S(2)}) collective-permute-start(bf16[4,256,128]{2,1,0:T(8,128)(2,1)} %refs_4_.1), channel_id=1, source_target_pairs={{0,24},{4,28},{8,16},{12,20},{16,8},{20,12},{24,0},{28,4},{1,25},{... | collective-permute-start | bytes 786440 | tf_op jit(solution)/shard_map/ppermute | solution.py:22
  19.4 11.2 %collective-permute-start.7 = (bf16[4,256,128]{2,1,0:T(8,128)(2,1)}, bf16[4,256,128]{2,1,0:T(8,128)(2,1)S(1)}, u32[]{:S(2)}, u32[]{:S(2)}) collective-permute-start(bf16[4,256,128]{2,1,0:T(8,128)(2,1)} %refs_4_.1), channel_id=1, source_target_pairs={{0,4},{4,0},{8,12},{12,8},{16,20},{20,16},{24,28},{28,24},{1,5},{5... | collective-permute-start | bytes 786440 | tf_op jit(solution)/shard_map/ppermute | solution.py:22
  19.4 12.6 %collective-permute-start.10 = (bf16[4,256,128]{2,1,0:T(8,128)(2,1)S(1)}, bf16[4,256,128]{2,1,0:T(8,128)(2,1)S(1)}, u32[]{:S(2)}, u32[]{:S(2)}) collective-permute-start(bf16[4,256,128]{2,1,0:T(8,128)(2,1)S(1)} %collective-permute-done.5.refs_8_.refs_7_), channel_id=1, source_target_pairs={{0,4},{4,0},{8,12},{12,8},{16,20},{20,16},{24,28},{28,24},{1,5},{5... | collective-permute-start | bytes 786440 | tf_op jit(solution)/shard_map/ppermute | solution.py:22
  21.7 7.6 %collective-permute-start.2 = (bf16[400,256]{1,0:T(8,128)(2,1)S(1)}, bf16[400,256]{1,0:T(8,128)(2,1)S(1)}, u32[]{:S(2)}, u32[]{:S(2)}) collective-permute-start(bf16[400,256]{1,0:T(8,128)(2,1)S(1)} %get-tuple-element.33), channel_id=1, source_target_pairs={{0,3},{1,2},{2,1},{3,0},{4,7},{5,6},{6,5},{7,4},{8,11},{9,10},{10,... | collective-permute-start | bytes 614408 | tf_op jit(solution)/shard_map/ppermute | solution.py:22
  24.2 9.3 %collective-permute-start.9 = (bf16[4,256,128]{2,1,0:T(8,128)(2,1)S(1)}, bf16[4,256,128]{2,1,0:T(8,128)(2,1)S(1)}, u32[]{:S(2)}, u32[]{:S(2)}) collective-permute-start(bf16[4,256,128]{2,1,0:T(8,128)(2,1)S(1)} %collective-permute-done.4.refs_7_.refs_6_), channel_id=1, source_target_pairs={{0,4},{4,0},{8,12},{12,8},{16,20},{20,16},{24,28},{28,24},{1,5},{5... | collective-permute-start | bytes 786440 | tf_op jit(solution)/shard_map/ppermute | solution.py:22
  25.7 7.8 %collective-permute-start.8 = (bf16[4,256,128]{2,1,0:T(8,128)(2,1)S(1)}, bf16[4,256,128]{2,1,0:T(8,128)(2,1)S(1)}, u32[]{:S(2)}, u32[]{:S(2)}) collective-permute-start(bf16[4,256,128]{2,1,0:T(8,128)(2,1)S(1)} %collective-permute-done.3.refs_6_.refs_5_), channel_id=1, source_target_pairs={{0,4},{4,0},{8,12},{12,8},{16,20},{20,16},{24,28},{28,24},{1,5},{5... | collective-permute-start | bytes 786440 | tf_op jit(solution)/shard_map/ppermute | solution.py:22
  29.9 9.9 %collective-permute-start.14 = (bf16[144,1024]{1,0:T(8,128)(2,1)S(1)}, bf16[144,1024]{1,0:T(8,128)(2,1)S(1)}, u32[]{:S(2)}, u32[]{:S(2)}) collective-permute-start(bf16[144,1024]{1,0:T(8,128)(2,1)S(1)} %get-tuple-element.35.refs_4_), channel_id=1, source_target_pairs={{0,16},{4,20},{8,24},{12,28},{16,0},{20,4},{24,8},{28,12},{1,17},{... | collective-permute-start | bytes 884744 | tf_op jit(solution)/shard_map/ppermute | solution.py:22
  30.6 13.6 %collective-permute-start.13 = (bf16[144,1024]{1,0:T(8,128)(2,1)S(1)}, bf16[144,1024]{1,0:T(8,128)(2,1)S(1)}, u32[]{:S(2)}, u32[]{:S(2)}) collective-permute-start(bf16[144,1024]{1,0:T(8,128)(2,1)S(1)} %get-tuple-element.35.refs_4_), channel_id=1, source_target_pairs={{0,8},{4,12},{8,0},{12,4},{16,24},{20,28},{24,16},{28,20},{1,9},{5... | collective-permute-start | bytes 884744 | tf_op jit(solution)/shard_map/ppermute | solution.py:22
  32.0 12.2 %collective-permute-start.6 = (bf16[144,1024]{1,0:T(8,128)(2,1)S(1)}, bf16[144,1024]{1,0:T(8,128)(2,1)S(1)}, u32[]{:S(2)}, u32[]{:S(2)}) collective-permute-start(bf16[144,1024]{1,0:T(8,128)(2,1)S(1)} %get-tuple-element.35.refs_4_), channel_id=1, source_target_pairs={{0,24},{4,28},{8,16},{12,20},{16,8},{20,12},{24,0},{28,4},{1,25},{... | collective-permute-start | bytes 884744 | tf_op jit(solution)/shard_map/ppermute | solution.py:22
  33.5 1.0 %copy-start = (bf16[4,256,128]{2,1,0:T(8,128)(2,1)S(1)}, bf16[4,256,128]{2,1,0:T(8,128)(2,1)}, u32[]{:S(2)}) copy-start(bf16[4,256,128]{2,1,0:T(8,128)(2,1)} %refs_4_.1) | copy-start | bytes 786436
  36.3 6.2 %collective-permute-start.12 = (bf16[256,256]{1,0:T(8,128)(2,1)S(1)}, bf16[256,256]{1,0:T(8,128)(2,1)S(1)}, u32[]{:S(2)}, u32[]{:S(2)}) collective-permute-start(bf16[256,256]{1,0:T(8,128)(2,1)S(1)} %get-tuple-element.37.refs_0_), channel_id=1, source_target_pairs={{0,2},{1,3},{2,0},{3,1},{4,6},{5,7},{6,4},{7,5},{8,10},{9,11},{10,... | collective-permute-start | bytes 393224 | tf_op jit(solution)/shard_map/ppermute | solution.py:22
  39.2 5.0 %collective-permute-start.11 = (bf16[256,256]{1,0:T(8,128)(2,1)S(1)}, bf16[256,256]{1,0:T(8,128)(2,1)S(1)}, u32[]{:S(2)}, u32[]{:S(2)}) collective-permute-start(bf16[256,256]{1,0:T(8,128)(2,1)S(1)} %get-tuple-element.37.refs_0_), channel_id=1, source_target_pairs={{0,1},{1,0},{2,3},{3,2},{4,5},{5,4},{6,7},{7,6},{8,9},{9,8},{10,11... | collective-permute-start | bytes 393224 | tf_op jit(solution)/shard_map/ppermute | solution.py:22
  39.9 7.6 %collective-permute-start.15 = (bf16[144,1024]{1,0:T(8,128)(2,1)S(1)}, bf16[144,1024]{1,0:T(8,128)(2,1)S(1)}, u32[]{:S(2)}, u32[]{:S(2)}) collective-permute-start(bf16[144,1024]{1,0:T(8,128)(2,1)S(1)} %get-tuple-element.35.refs_4_), channel_id=1, source_target_pairs={{0,4},{4,0},{8,12},{12,8},{16,20},{20,16},{24,28},{28,24},{1,5},{5... | collective-permute-start | bytes 884744 | tf_op jit(solution)/shard_map/ppermute | solution.py:22
  44.2 3.3 %collective-permute-start.16 = (bf16[144,1024]{1,0:T(8,128)(2,1)S(1)}, bf16[144,1024]{1,0:T(8,128)(2,1)S(1)}, u32[]{:S(2)}, u32[]{:S(2)}) collective-permute-start(bf16[144,1024]{1,0:T(8,128)(2,1)S(1)} %collective-permute-done.6.refs_5_), channel_id=1, source_target_pairs={{0,4},{4,0},{8,12},{12,8},{16,20},{20,16},{24,28},{28,24},{1,5},{5... | collective-permute-start | bytes 884744 | tf_op jit(solution)/shard_map/ppermute | solution.py:22
  44.2 3.3 %collective-permute-start.17 = (bf16[144,1024]{1,0:T(8,128)(2,1)S(1)}, bf16[144,1024]{1,0:T(8,128)(2,1)S(1)}, u32[]{:S(2)}, u32[]{:S(2)}) collective-permute-start(bf16[144,1024]{1,0:T(8,128)(2,1)S(1)} %collective-permute-done.13.refs_6_), channel_id=1, source_target_pairs={{0,4},{4,0},{8,12},{12,8},{16,20},{20,16},{24,28},{28,24},{1,5},{5... | collective-permute-start | bytes 884744 | tf_op jit(solution)/shard_map/ppermute | solution.py:22
  44.7 2.8 %collective-permute-start.18 = (bf16[144,1024]{1,0:T(8,128)(2,1)S(1)}, bf16[144,1024]{1,0:T(8,128)(2,1)S(1)}, u32[]{:S(2)}, u32[]{:S(2)}) collective-permute-start(bf16[144,1024]{1,0:T(8,128)(2,1)S(1)} %collective-permute-done.14.refs_7_), channel_id=1, source_target_pairs={{0,4},{4,0},{8,12},{12,8},{16,20},{20,16},{24,28},{28,24},{1,5},{5... | collective-permute-start | bytes 884744 | tf_op jit(solution)/shard_map/ppermute | solution.py:22
  44.8 10.1 %collective-permute-start.19 = (bf16[256,256]{1,0:T(8,128)(2,1)S(1)}, bf16[256,256]{1,0:T(8,128)(2,1)S(1)}, u32[]{:S(2)}, u32[]{:S(2)}) collective-permute-start(bf16[256,256]{1,0:T(8,128)(2,1)S(1)} %get-tuple-element.37.refs_0_), channel_id=1, source_target_pairs={{0,3},{1,2},{2,1},{3,0},{4,7},{5,6},{6,5},{7,4},{8,11},{9,10},{10,... | collective-permute-start | bytes 393224 | tf_op jit(solution)/shard_map/ppermute | solution.py:22
  49.8 11.2 %copy-start.6 = (s32[4096]{0:T(1024)S(1)}, s32[4096]{0:T(1024)}, u32[]{:S(2)}) copy-start(s32[4096]{0:T(1024)} %param.15) | copy-start | bytes 49156
  49.8 11.2 %copy-start.7 = (s32[4096]{0:T(1024)S(1)}, s32[4096]{0:T(1024)}, u32[]{:S(2)}) copy-start(s32[4096]{0:T(1024)} %param.16) | copy-start | bytes 49156
  49.8 11.2 %copy-start.8 = (f32[4096]{0:T(1024)S(1)}, f32[4096]{0:T(1024)}, u32[]{:S(2)}) copy-start(f32[4096]{0:T(1024)} %param.17) | copy-start | bytes 49156
  49.8 13.8 %copy-start.1 = (bf16[4,256,128]{2,1,0:T(8,128)(2,1)S(1)}, bf16[4,256,128]{2,1,0:T(8,128)(2,1)}, u32[]{:S(2)}) copy-start(bf16[4,256,128]{2,1,0:T(8,128)(2,1)} %refs_4_.1) | copy-start | bytes 786436
  49.8 15.7 %collective-permute-start.20 = (bf16[64,1024]{1,0:T(8,128)(2,1)S(1)}, bf16[64,1024]{1,0:T(8,128)(2,1)S(1)}, u32[]{:S(2)}, u32[]{:S(2)}) collective-permute-start(bf16[64,1024]{1,0:T(8,128)(2,1)S(1)} %get-tuple-element.48), channel_id=1, source_target_pairs={{0,1},{1,0},{2,3},{3,2},{4,5},{5,4},{6,7},{7,6},{8,9},{9,8},{10,11... | collective-permute-start | bytes 393224 | tf_op jit(solution)/shard_map/ppermute | solution.py:22
  52.4 13.1 %collective-permute-start.21 = (bf16[64,1024]{1,0:T(8,128)(2,1)S(1)}, bf16[64,1024]{1,0:T(8,128)(2,1)S(1)}, u32[]{:S(2)}, u32[]{:S(2)}) collective-permute-start(bf16[64,1024]{1,0:T(8,128)(2,1)S(1)} %get-tuple-element.49), channel_id=1, source_target_pairs={{0,2},{1,3},{2,0},{3,1},{4,6},{5,7},{6,4},{7,5},{8,10},{9,11},{10,... | collective-permute-start | bytes 393224 | tf_op jit(solution)/shard_map/ppermute | solution.py:22
  52.4 13.1 %collective-permute-start.22 = (bf16[64,1024]{1,0:T(8,128)(2,1)S(1)}, bf16[64,1024]{1,0:T(8,128)(2,1)S(1)}, u32[]{:S(2)}, u32[]{:S(2)}) collective-permute-start(bf16[64,1024]{1,0:T(8,128)(2,1)S(1)} %get-tuple-element.50), channel_id=1, source_target_pairs={{0,3},{1,2},{2,1},{3,0},{4,7},{5,6},{6,5},{7,4},{8,11},{9,10},{10,... | collective-permute-start | bytes 393224 | tf_op jit(solution)/shard_map/ppermute | solution.py:22
  57.7 7.9 %copy-start.3 = (f32[64,256]{1,0:T(8,128)S(1)}, f32[64,256]{1,0:T(8,128)}, u32[]{:S(2)}) copy-start(f32[64,256]{1,0:T(8,128)} %refs_0_.3) | copy-start | bytes 196612
  57.7 7.9 %copy-start.10 = (s32[64,1]{0,1:T(1,128)S(1)}, s32[64,1]{0,1:T(1,128)}, u32[]{:S(2)}) copy-start(s32[64,1]{0,1:T(1,128)} %param.13) | copy-start | bytes 772
  57.7 7.9 %copy-start.12 = (s32[256,1]{0,1:T(1,128)S(1)}, s32[256,1]{0,1:T(1,128)}, u32[]{:S(2)}) copy-start(s32[256,1]{0,1:T(1,128)} %param.14) | copy-start | bytes 3076
  57.7 11.7 %collective-permute-start.23 = (bf16[64,1024]{1,0:T(8,128)(2,1)S(1)}, bf16[64,1024]{1,0:T(8,128)(2,1)S(1)}, u32[]{:S(2)}, u32[]{:S(2)}) collective-permute-start(bf16[64,1024]{1,0:T(8,128)(2,1)S(1)} %get-tuple-element.52), channel_id=1, source_target_pairs={{0,1},{1,0},{2,3},{3,2},{4,5},{5,4},{6,7},{7,6},{8,9},{9,8},{10,11... | collective-permute-start | bytes 393224 | tf_op jit(solution)/shard_map/ppermute | solution.py:22
  58.7 10.7 %collective-permute-start.25 = (bf16[64,1024]{1,0:T(8,128)(2,1)S(1)}, bf16[64,1024]{1,0:T(8,128)(2,1)S(1)}, u32[]{:S(2)}, u32[]{:S(2)}) collective-permute-start(bf16[64,1024]{1,0:T(8,128)(2,1)S(1)} %get-tuple-element.54), channel_id=1, source_target_pairs={{0,3},{1,2},{2,1},{3,0},{4,7},{5,6},{6,5},{7,4},{8,11},{9,10},{10,... | collective-permute-start | bytes 393224 | tf_op jit(solution)/shard_map/ppermute | solution.py:22
  69.4 8.9 %collective-permute-start.28 = (f32[8,128]{1,0:T(8,128)S(1)}, f32[8,128]{1,0:T(8,128)S(1)}, u32[]{:S(2)}, u32[]{:S(2)}) collective-permute-start(f32[8,128]{1,0:T(8,128)S(1)} %get-tuple-element.57.refs_4_), channel_id=1, source_target_pairs={{0,3},{1,2},{2,1},{3,0},{4,7},{5,6},{6,5},{7,4},{8,11},{9,10},{10,... | collective-permute-start | bytes 12296 | tf_op jit(solution)/shard_map/ppermute | solution.py:22
  71.1 7.2 %collective-permute-start.27 = (f32[8,128]{1,0:T(8,128)S(1)}, f32[8,128]{1,0:T(8,128)S(1)}, u32[]{:S(2)}, u32[]{:S(2)}) collective-permute-start(f32[8,128]{1,0:T(8,128)S(1)} %get-tuple-element.57.refs_4_), channel_id=1, source_target_pairs={{0,2},{1,3},{2,0},{3,1},{4,6},{5,7},{6,4},{7,5},{8,10},{9,11},{10,... | collective-permute-start | bytes 12296 | tf_op jit(solution)/shard_map/ppermute | solution.py:22
  76.3 3.6 %collective-permute-start.26 = (f32[8,128]{1,0:T(8,128)S(1)}, f32[8,128]{1,0:T(8,128)S(1)}, u32[]{:S(2)}, u32[]{:S(2)}) collective-permute-start(f32[8,128]{1,0:T(8,128)S(1)} %get-tuple-element.57.refs_4_), channel_id=1, source_target_pairs={{0,1},{1,0},{2,3},{3,2},{4,5},{5,4},{6,7},{7,6},{8,9},{9,8},{10,11... | collective-permute-start | bytes 12296 | tf_op jit(solution)/shard_map/ppermute | solution.py:22
  76.3 8.3 %collective-permute-start.24 = (bf16[64,1024]{1,0:T(8,128)(2,1)S(1)}, bf16[64,1024]{1,0:T(8,128)(2,1)S(1)}, u32[]{:S(2)}, u32[]{:S(2)}) collective-permute-start(bf16[64,1024]{1,0:T(8,128)(2,1)S(1)} %get-tuple-element.53), channel_id=1, source_target_pairs={{0,2},{1,3},{2,0},{3,1},{4,6},{5,7},{6,4},{7,5},{8,10},{9,11},{10,... | collective-permute-start | bytes 393224 | tf_op jit(solution)/shard_map/ppermute | solution.py:22
  79.9 1.2 %collective-permute-start.29 = (f32[8,128]{1,0:T(8,128)S(1)}, f32[8,128]{1,0:T(8,128)S(1)}, u32[]{:S(2)}, u32[]{:S(2)}) collective-permute-start(f32[8,128]{1,0:T(8,128)S(1)} %add_add_fusion), channel_id=1, source_target_pairs={{0,4},{4,0},{8,12},{12,8},{16,20},{20,16},{24,28},{28,24},{1,5},{5... | collective-permute-start | bytes 12296 | tf_op jit(solution)/shard_map/ppermute | solution.py:22
  81.1 7.2 %collective-permute-start.32 = (f32[8,128]{1,0:T(8,128)S(1)}, f32[8,128]{1,0:T(8,128)S(1)}, u32[]{:S(2)}, u32[]{:S(2)}) collective-permute-start(f32[8,128]{1,0:T(8,128)S(1)} %add.15.refs_8_), channel_id=1, source_target_pairs={{0,16},{4,20},{8,24},{12,28},{16,0},{20,4},{24,8},{28,12},{1,17},{... | collective-permute-start | bytes 12296 | tf_op jit(solution)/shard_map/ppermute | solution.py:22
  81.8 6.5 %collective-permute-start.31 = (f32[8,128]{1,0:T(8,128)S(1)}, f32[8,128]{1,0:T(8,128)S(1)}, u32[]{:S(2)}, u32[]{:S(2)}) collective-permute-start(f32[8,128]{1,0:T(8,128)S(1)} %add.15.refs_8_), channel_id=1, source_target_pairs={{0,8},{4,12},{8,0},{12,4},{16,24},{20,28},{24,16},{28,20},{1,9},{5... | collective-permute-start | bytes 12296 | tf_op jit(solution)/shard_map/ppermute | solution.py:22
  83.1 5.2 %collective-permute-start.30 = (f32[8,128]{1,0:T(8,128)S(1)}, f32[8,128]{1,0:T(8,128)S(1)}, u32[]{:S(2)}, u32[]{:S(2)}) collective-permute-start(f32[8,128]{1,0:T(8,128)S(1)} %add.15.refs_8_), channel_id=1, source_target_pairs={{0,24},{4,28},{8,16},{12,20},{16,8},{20,12},{24,0},{28,4},{1,25},{... | collective-permute-start | bytes 12296 | tf_op jit(solution)/shard_map/ppermute | solution.py:22
